TPU v7x, 512 devices: a whole 4x4x16 slice. The times are simulated.
512 devices in a mesh: replica: 32 (over z, core), tensor: 16 (over y, x).
Axes of the slice: x: 4, y: 4, z: 16, core: 2. Of those that a mesh axis runs over, the one named last changes fastest.
Arguments:
- tokens: bfloat16 [24576, 4096], P('replica', 'tensor'), may hold values from -6 to 6
- query_weight: bfloat16 [4096, 4096], P(None, 'tensor'), may hold values from -0.09375 to 0.09375
- input_factor_pool: bfloat16 [1024, 64, 4096], P('replica', None, 'tensor'), may hold values from -0.09375 to 0.09375
- output_factor_pool: bfloat16 [1024, 64, 4096], P('replica', None, 'tensor'), may hold values from -0.375 to 0.375
- row_adapter_index: int32 [24576], P('replica'), may hold values from 0 to 1023, as said below
- adapter_pool_slot: int32 [1024], replicated, may hold values from 0 to 1023, as said below
Outputs:
- queries: bfloat16 [24576, 4096], P('replica', 'tensor')
Inputs may be any that keep to these rules, and one draw needn't show every extreme that they name: Each of 0 to 1023 appears once; adapter a uses entry adapter_pool_slot[a] of the first dimension of input_factor_pool and output_factor_pool, and its holder is adapter_pool_slot[a] // 32. `row_adapter_index`: among the 768 rows of one group (one index of replica), at most 16 rows name any one adapter, and at most 4 different named adapters share one holder. In every group some adapter is named by exactly 16 rows and some holder has exactly 4 named adapters.
All inputs are finite; a program needn't handle non-finite values.
Results may differ from a plain program's by a relative error of at most 0.0049.
Values may be sent and summed in bfloat16 or wider, within the bound.
No kernel may reach another device: no remote copies, remote signals or barrier semaphores. Data moves between devices by JAX's collectives and lax.ppermute only.
A program may use at most 64 MiB of HBM per device.

v0:
```python
import jax
import jax.numpy as jnp
from jax import lax
from jax.sharding import PartitionSpec as P

ADAPTER_RANK = 64
DISTINCT = 128
RPA = 16


adapter_scale = 2.0


def body(
    tokens,
    query_weight,
    input_factor_pool,
    output_factor_pool,
    row_adapter_index,
    adapter_pool_slot,
):
    group_count = lax.axis_size("replica")
    slot_capacity = DISTINCT // group_count
    row_count = tokens.shape[0]
    shard_width = tokens.shape[1]
    query_features = query_weight.shape[1]
    holding_count = input_factor_pool.shape[0]
    table_ids = jnp.arange(adapter_pool_slot.shape[0], dtype=jnp.int32)
    pool_row = jnp.sum(
        jnp.where(row_adapter_index[:, None] == table_ids[None, :], adapter_pool_slot[None, :], 0),
        axis=1,
    )
    holder = pool_row // holding_count
    local_slot = pool_row % holding_count
    order = jnp.arange(row_count, dtype=jnp.int32)
    same_slot = pool_row[:, None] == pool_row[None, :]
    before = order[None, :] < order[:, None]
    place_in = jnp.sum(same_slot & before, axis=1)
    first_row = place_in == 0
    same_holder = holder[:, None] == holder[None, :]
    slot_rank = jnp.sum(
        first_row[None, :] & same_holder & (pool_row[None, :] < pool_row[:, None]), axis=1
    )
    slot_bucket = (holder * slot_capacity + slot_rank) * RPA + place_in
    bucket_total = group_count * slot_capacity * RPA
    buckets = jnp.zeros((bucket_total, shard_width), jnp.bfloat16).at[slot_bucket].set(tokens)
    request_at = jnp.where(
        first_row, holder * slot_capacity + slot_rank, group_count * slot_capacity
    )
    wanted = (
        jnp.zeros((group_count * slot_capacity,), jnp.int32)
        .at[request_at]
        .set(local_slot, mode="drop")
    )
    base_output = jnp.dot(
        lax.all_gather(tokens, "tensor", axis=1, tiled=True),
        query_weight,
        preferred_element_type=jnp.float32,
    )
    asked_for = lax.all_to_all(
        wanted.reshape(group_count, slot_capacity),
        "replica",
        split_axis=0,
        concat_axis=0,
        tiled=True,
    )
    flat_requested = asked_for.reshape(-1)
    selected_input_factor = input_factor_pool[flat_requested].reshape(
        group_count, slot_capacity, ADAPTER_RANK, shard_width
    )
    selected_output_factor = output_factor_pool[flat_requested].reshape(
        group_count, slot_capacity, ADAPTER_RANK, query_features
    )
    fetched_a, fetched_b = (
        lax.all_to_all(selected_input_factor, "replica", split_axis=0, concat_axis=0, tiled=True),
        lax.all_to_all(selected_output_factor, "replica", split_axis=0, concat_axis=0, tiled=True),
    )
    bucket_x = buckets.reshape(group_count * slot_capacity, RPA, shard_width)
    partial_value = jnp.einsum(
        "srf,skf->srk",
        bucket_x,
        fetched_a.reshape(group_count * slot_capacity, ADAPTER_RANK, shard_width),
        preferred_element_type=jnp.float32,
    )
    shrunk = lax.psum(partial_value, "tensor").astype(jnp.bfloat16)
    expanded_rows = jnp.einsum(
        "srk,skc->src",
        shrunk,
        fetched_b.reshape(group_count * slot_capacity, ADAPTER_RANK, query_features),
        preferred_element_type=jnp.float32,
    ).astype(jnp.bfloat16)
    adapter_rows = expanded_rows.reshape(bucket_total, query_features)
    adapter_output = lax.optimization_barrier(adapter_rows[slot_bucket])
    return (base_output + adapter_scale * adapter_output.astype(jnp.float32)).astype(jnp.bfloat16)


def solution(mesh):
    in_specs = (
        P("replica", "tensor"),
        P(None, "tensor"),
        P("replica", None, "tensor"),
        P("replica", None, "tensor"),
        P("replica"),
        P(),
    )
    out_specs = P("replica", "tensor")
    return jax.shard_map(body, mesh=mesh, in_specs=in_specs, out_specs=out_specs, check_vma=False)
```

profile of v0, /device:TPU:30, one launch (start us, length us, event | category | flops | bytes accessed | tf_op | source)
XLA Modules:
  0.0 456.3 jit_solution(2213073135340189471)
XLA Ops:
  6.5 0.0 copy-start
  6.5 1.5 select_reduce_fusion
  8.0 0.4 convert_reduce_fusion.1
  8.4 0.8 convert_reduce_fusion
  9.2 3.4 scatter_custom_fusion.1
  12.6 0.1 all_to_all.12
  12.7 27.7 %all_to_all.19 = s32[32,1,4]{2,1,0:T(1,128)S(1)} all-to-all(s32[32,1,4]{2,1,0:T(1,128)S(1)} %bitcast.19), channel_id=1, replica_groups=mesh['replica'=32,'tensor'=16] {'replica'}, dimensions={0} | all-to-all | bytes 1024 | tf_op jit(solution)/shard_map/all_to_all | solution.py:60
  40.5 0.5 broadcast.258
  41.0 0.7 reduce.7
  41.7 0.1 reshape.186
  41.8 4.1 gather_fusion
  45.9 0.0 copy-start.1
  45.9 5.0 %all-to-all-start.1 = ((bf16[32,4,64,256]{3,2,1,0:T(8,128)(2,1)}), bf16[32,4,64,256]{3,2,1,0:T(8,128)(2,1)}, u32[]{:S(2)}, u32[]{:S(2)}) async-start(bf16[32,4,64,256]{3,2,1,0:T(8,128)(2,1)} %bitcast.16), calls=%async_computation.1 | async-start | bytes 8388608 | tf_op jit(solution)/shard_map/all_to_all | solution.py:75
  50.9 0.0 copy-done.1
  50.9 2.9 gather_fusion.1
  53.8 188.4 %all-to-all-done.1 = bf16[32,4,64,256]{3,2,1,0:T(8,128)(2,1)} async-done(((bf16[32,4,64,256]{3,2,1,0:T(8,128)(2,1)}), bf16[32,4,64,256]{3,2,1,0:T(8,128)(2,1)}, u32[]{:S(2)}, u32[]{:S(2)}) %all-to-all-start.1) | async-done | bytes 4194336 | tf_op jit(solution)/shard_map/all_to_all | solution.py:75
  242.2 4.9 %all-to-all-start.2 = ((bf16[32,4,64,256]{3,2,1,0:T(8,128)(2,1)}), bf16[32,4,64,256]{3,2,1,0:T(8,128)(2,1)}, u32[]{:S(2)}, u32[]{:S(2)}) async-start(bf16[32,4,64,256]{3,2,1,0:T(8,128)(2,1)} %bitcast.15), calls=%async_computation.2 | async-start | bytes 8388608 | tf_op jit(solution)/shard_map/all_to_all | solution.py:76
  247.1 0.0 all-gather.2.cloned.1.call-start
  247.1 0.7 all-gather.2.cloned.1.call-update
  247.8 6.2 %scatter_custom_fusion = bf16[2048,256]{1,0:T(8,128)(2,1)S(1)} fusion(s32[768]{0:T(1024)S(1)} %get-tuple-element.5, bf16[768,256]{1,0:T(8,128)(2,1)} %param.6, bf16[]{:T(256)} %constant.18.clone.1), kind=kCustom, calls=%fused_computation.15 | custom fusion | bytes 1049088 | tf_op jit(solution)/shard_map/scatter | solution.py:46
  254.1 4.4 fusion.12
  258.4 93.4 %all-reduce.1 = bf16[128,16,64]{2,1,0:T(8,128)(2,1)} all-reduce(f32[128,16,64]{2,1,0:T(8,128)} %fusion.12), channel_id=1, replica_groups=mesh['replica'=32,'tensor'=16] {'tensor'}, use_global_device_ids=true, to_apply=%region_5.6 | all-reduce | flops 131072 | bytes 786432 | tf_op jit(solution)/shard_map/psum | solution.py:85
  351.8 86.6 %all-to-all-done.2 = bf16[32,4,64,256]{3,2,1,0:T(8,128)(2,1)} async-done(((bf16[32,4,64,256]{3,2,1,0:T(8,128)(2,1)}), bf16[32,4,64,256]{3,2,1,0:T(8,128)(2,1)}, u32[]{:S(2)}, u32[]{:S(2)}) %all-to-all-start.2) | async-done | bytes 4194336 | tf_op jit(solution)/shard_map/all_to_all | solution.py:76
  438.4 3.0 convolution_convert_fusion
  441.4 2.7 gather_fusion.2
  444.1 0.0 all-gather.2.cloned.1.call-done
  444.1 0.0 copy-done
  444.1 5.3 %fusion.1 = bf16[768,256]{1,0:T(8,128)(2,1)} fusion(bf16[768,4096]{1,0:T(8,128)(2,1)} %all-gather.2.cloned.1.call-done, bf16[4096,256]{1,0:T(8,128)(2,1)S(1)} %copy-done, bf16[768,256]{1,0:T(8,128)(2,1)S(1)} %gather_fusion.2), kind=kOutput, calls=%fused_computation.13 | convolution fusion | flops 1611399168 | bytes 9175040 | tf_op jit(solution)/shard_map/dot_general | solution.py:55
  (6 shorter events, 0.1 us)
Async XLA Ops:
  6.5 437.6 %copy-start = (bf16[4096,256]{1,0:T(8,128)(2,1)S(1)}, bf16[4096,256]{1,0:T(8,128)(2,1)}, u32[]{:S(2)}) copy-start(bf16[4096,256]{1,0:T(8,128)(2,1)} %param.7) | copy-start | bytes 6291460
  45.9 5.0 %copy-start.1 = (bf16[32,64,256]{2,1,0:T(8,128)(2,1)S(1)}, bf16[32,64,256]{2,1,0:T(8,128)(2,1)}, u32[]{:S(2)}) copy-start(bf16[32,64,256]{2,1,0:T(8,128)(2,1)} %param.9) | copy-start | bytes 3145732
  45.9 196.3 %all-to-all-start.1 = ((bf16[32,4,64,256]{3,2,1,0:T(8,128)(2,1)}), bf16[32,4,64,256]{3,2,1,0:T(8,128)(2,1)}, u32[]{:S(2)}, u32[]{:S(2)}) async-start(bf16[32,4,64,256]{3,2,1,0:T(8,128)(2,1)} %bitcast.16), calls=%async_computation.1 | async-start | bytes 8388608 | tf_op jit(solution)/shard_map/all_to_all | solution.py:75
  242.2 196.2 %all-to-all-start.2 = ((bf16[32,4,64,256]{3,2,1,0:T(8,128)(2,1)}), bf16[32,4,64,256]{3,2,1,0:T(8,128)(2,1)}, u32[]{:S(2)}, u32[]{:S(2)}) async-start(bf16[32,4,64,256]{3,2,1,0:T(8,128)(2,1)} %bitcast.15), calls=%async_computation.2 | async-start | bytes 8388608 | tf_op jit(solution)/shard_map/all_to_all | solution.py:76
  247.1 197.0 %all-gather.2.cloned.1.call-start = ((), (), s32[]{:S(2)}) async-start(), calls=%async_computation.3 | async-start | bytes 6684672 | tf_op jit(solution)/shard_map/all_gather | solution.py:56
Sparse Core Ops, SparseCore 0:
  250.9 92.4 all-gather.1
where the time goes:
time: 457 us; the launch traced here: 456 us
  waiting for transfers between devices  276 us (60%)
  blocking collectives  121 us (26%)
  local copies, waits for them, and re-layouts  19.9 us (4%)
  between operations  13.5 us (3%)
  matrix products  12.7 us (3%)
  starting transfers between devices  9.88 us (2%)
    all_to_all x1, waiting for transfers between devices, body(): lax.all_to_all(selected_input_factor, 'replica', split_axis=0, concat_axi...  188 us
    psum x1, blocking collectives, body(): shrunk = lax.psum(partial_value, 'tensor').astype(jnp.bfloat16)  93.4 us
    all_to_all x1, waiting for transfers between devices, body(): lax.all_to_all(selected_output_factor, 'replica', split_axis=0, concat_ax...  86.6 us
    all_to_all x1, blocking collectives, body(): lax.all_to_all(wanted.reshape(group_count, slot_capacity), 'replica', spl...  27.7 us
  transfers between devices with their start and end apart: 3, of which 2 were waited for; matrix products, arithmetic and copies ran while one was open for 4% of the time, Pallas kernels for 0%

commit v1 on v0

v1 whole, which is shorter than its diff:
```python
import jax
import jax.numpy as jnp
from jax import lax
from jax.experimental import pallas as pl
from jax.experimental.pallas import tpu as pltpu
from jax.sharding import PartitionSpec as P

RANK = 64
SLOTS = 4
RPA = 16
PAIR = SLOTS * RPA
GROUPS = 32
HELD = 32
TENSOR = 16
ROWS = 768
WIDTH = 256
BUCKETS = GROUPS * PAIR
PAY = 136
SCALE = 2.0

BF = jnp.bfloat16
F32 = jnp.float32
I32 = jnp.int32
NT = (((1,), (1,)), ((), ()))


def params():
    return pltpu.CompilerParams(vmem_limit_bytes=40 * 1024 * 1024)


def vmem(n):
    return [pl.BlockSpec(memory_space=pltpu.VMEM)] * n


def pack_kernel(dest_ref, local_ref, tokens_ref, out_ref):
    dest = dest_ref[...]
    local = local_ref[...]
    for b in range(8):
        at = lax.broadcasted_iota(I32, (256, ROWS), 0) + b * 256
        pick = (at == dest).astype(F32).astype(BF)
        rows = jnp.dot(pick, tokens_ref[...], preferred_element_type=F32).astype(BF)
        for j in range(4):
            out_ref[4 * b + j, 0:64, :] = rows[64 * j : 64 * j + 64, 0:128]
            out_ref[4 * b + j, 64:128, :] = rows[64 * j : 64 * j + 64, 128:256]
    group = lax.broadcasted_iota(I32, (GROUPS, ROWS), 0)
    to = (group == dest // PAIR).astype(F32).astype(BF)
    lane_slot = (lax.broadcasted_iota(I32, (128, ROWS), 0) % PAIR) // RPA
    slot = (dest % PAIR) // RPA
    first = dest % RPA == 0
    value = jnp.where((lane_slot == slot) & first, local.astype(F32), 0.0).astype(BF)
    ids = lax.dot_general(to, value, NT, preferred_element_type=F32).astype(BF)
    for h in range(GROUPS):
        out_ref[h, 128:136, :] = jnp.broadcast_to(ids[h : h + 1, :], (8, 128))


def shrink_kernel(pay_ref, a_ref, out_ref, ids_ref):
    low = lax.broadcasted_iota(I32, (8, 128), 1) < PAIR
    for b in range(8):
        parts = []
        marks = []
        for j in range(4):
            g = 4 * b + j
            parts.append(jnp.concatenate([pay_ref[g, 0:64, :], pay_ref[g, 64:128, :]], axis=1))
        for j in range(2):
            g = 4 * b + 2 * j
            mark = jnp.where(
                low, pay_ref[g, 128:136, :].astype(F32), pay_ref[g + 1, 128:136, :].astype(F32)
            ).astype(I32)
            ids_ref[2 * b + j] = mark
            marks.append(mark[0:1, :])
        rows = jnp.concatenate(parts, axis=0)
        mark = jnp.concatenate(marks, axis=1)
        total = jnp.zeros((RANK, 256), F32)
        for q in range(8):
            prod = lax.dot_general(
                a_ref[256 * q : 256 * q + 256, :], rows, NT, preferred_element_type=F32
            )
            for a in range(4):
                total = total + jnp.where(mark == 4 * q + a, prod[64 * a : 64 * a + 64], 0.0)
        out_ref[2 * b] = total[:, 0:128].astype(BF)
        out_ref[2 * b + 1] = total[:, 128:256].astype(BF)


def sum_kernel(p_ref, out_ref):
    total = p_ref[0].astype(F32)
    for t in range(1, TENSOR):
        total = total + p_ref[t].astype(F32)
    mine = total.astype(BF)
    for t in range(TENSOR):
        out_ref[t] = mine


def expand_kernel(s_ref, ids_ref, bt_ref, out_ref, m_ref):
    for b in range(8):
        s = jnp.concatenate([s_ref[2 * b], s_ref[2 * b + 1]], axis=1).astype(F32)
        mark = jnp.concatenate([ids_ref[2 * b][0:1], ids_ref[2 * b + 1][0:1]], axis=1)
        for a in range(HELD):
            m_ref[64 * a : 64 * a + 64, :] = jnp.where(mark == a, s, 0.0).astype(BF)
        et = jnp.dot(bt_ref[...], m_ref[...], preferred_element_type=F32)
        rows = et.T.astype(BF)
        for j in range(4):
            out_ref[4 * b + j] = rows[64 * j : 64 * j + 64]


def final_kernel(dest_ref, base_ref, back_ref, out_ref):
    for b in range(3):
        at = lax.broadcasted_iota(I32, (256, BUCKETS), 1)
        pick = (at == dest_ref[256 * b : 256 * b + 256, :]).astype(F32).astype(BF)
        rows = jnp.dot(pick, back_ref[...], preferred_element_type=F32)
        out_ref[256 * b : 256 * b + 256, :] = (
            base_ref[256 * b : 256 * b + 256, :] + SCALE * rows
        ).astype(BF)


def route(row_adapter_index, adapter_pool_slot):
    table_ids = jnp.arange(adapter_pool_slot.shape[0], dtype=I32)
    pool_row = jnp.sum(
        jnp.where(row_adapter_index[:, None] == table_ids[None, :], adapter_pool_slot[None, :], 0),
        axis=1,
    )
    holder = pool_row // HELD
    order = jnp.arange(ROWS, dtype=I32)
    same = pool_row[:, None] == pool_row[None, :]
    place = jnp.sum(same & (order[None, :] < order[:, None]), axis=1)
    first = place == 0
    same_holder = holder[:, None] == holder[None, :]
    rank = jnp.sum(
        first[None, :] & same_holder & (pool_row[None, :] < pool_row[:, None]), axis=1
    )
    return (holder * SLOTS + rank) * RPA + place, pool_row % HELD


def exchange(x, axis):
    return lax.all_to_all(x, axis, split_axis=0, concat_axis=0, tiled=True)


def body(tokens, weight, a_pool, b_pool, row_adapter_index, adapter_pool_slot):
    everything = lax.all_gather(tokens, "tensor", axis=1, tiled=True)
    dest, local = route(row_adapter_index, adapter_pool_slot)
    payload = pl.pallas_call(
        pack_kernel,
        out_shape=jax.ShapeDtypeStruct((GROUPS, PAY, 128), BF),
        in_specs=vmem(3),
        out_specs=pl.BlockSpec(memory_space=pltpu.VMEM),
        compiler_params=params(),
        name="pack",
    )(dest.reshape(1, ROWS), local.reshape(1, ROWS), tokens)
    arrived = exchange(payload, "replica")
    partial, ids = pl.pallas_call(
        shrink_kernel,
        out_shape=(
            jax.ShapeDtypeStruct((TENSOR, RANK, 128), BF),
            jax.ShapeDtypeStruct((TENSOR, 8, 128), I32),
        ),
        in_specs=vmem(2),
        out_specs=tuple(vmem(2)),
        compiler_params=params(),
        name="shrink",
    )(arrived, a_pool.reshape(HELD * RANK, WIDTH))
    summed = pl.pallas_call(
        sum_kernel,
        out_shape=jax.ShapeDtypeStruct((TENSOR, RANK, 128), BF),
        in_specs=vmem(1),
        out_specs=pl.BlockSpec(memory_space=pltpu.VMEM),
        compiler_params=params(),
        name="total",
    )(exchange(partial, "tensor"))
    shrunk = exchange(summed, "tensor")
    expanded = pl.pallas_call(
        expand_kernel,
        out_shape=jax.ShapeDtypeStruct((GROUPS, PAIR, WIDTH), BF),
        in_specs=vmem(3),
        out_specs=pl.BlockSpec(memory_space=pltpu.VMEM),
        scratch_shapes=[pltpu.VMEM((HELD * RANK, 256), BF)],
        compiler_params=params(),
        name="expand",
    )(shrunk, ids, b_pool.reshape(HELD * RANK, WIDTH).T)
    back = exchange(expanded, "replica").reshape(BUCKETS, WIDTH)
    base = jnp.dot(everything, weight, preferred_element_type=F32)
    return pl.pallas_call(
        final_kernel,
        out_shape=jax.ShapeDtypeStruct((ROWS, WIDTH), BF),
        in_specs=vmem(3),
        out_specs=pl.BlockSpec(memory_space=pltpu.VMEM),
        compiler_params=params(),
        name="final",
    )(dest.reshape(ROWS, 1), base, back)


def solution(mesh):
    in_specs = (
        P("replica", "tensor"),
        P(None, "tensor"),
        P("replica", None, "tensor"),
        P("replica", None, "tensor"),
        P("replica"),
        P(),
    )
    return jax.shard_map(
        body, mesh=mesh, in_specs=in_specs, out_specs=P("replica", "tensor"), check_vma=False
    )
```

time: 457 us -> 194 us (0.42)
  the two profiles are of different devices: /device:TPU:30 before, /device:TPU:1 now
where the time goes in v1:
time: 194 us
  blocking collectives  89.4 us (46%)
  waiting for transfers between devices  56.6 us (29%)
  between operations  13.5 us (7%)
  starting transfers between devices  12.7 us (7%)
  Pallas kernels  9.6 us (5%)
  matrix products  5.47 us (3%)
  local copies, waits for them, and re-layouts  3.62 us (2%)
  other arithmetic  2.88 us (1%)
    all_to_all x2, blocking collectives, exchange(): return lax.all_to_all(x, axis, split_axis=0, concat_axis=0, tiled=True)  89.4 us
    all_to_all x2, waiting for transfers between devices, exchange(): return lax.all_to_all(x, axis, split_axis=0, concat_axis=0, tiled=True)  55.8 us
    all_to_all x2, starting transfers between devices, exchange(): return lax.all_to_all(x, axis, split_axis=0, concat_axis=0, tiled=True)  12.7 us
    dot_general x1, matrix products, body(): base = jnp.dot(everything, weight, preferred_element_type=F32)  5.47 us
  transfers between devices with their start and end apart: 3, of which 2 were waited for; matrix products, arithmetic and copies ran while one was open for 5% of the time, Pallas kernels for 4%

profile of v1, /device:TPU:1, one launch (start us, length us, event | category | flops | bytes accessed | tf_op | source)
XLA Modules:
  0.0 193.8 jit_solution(9140252446068082342)
XLA Ops:
  6.5 0.0 copy-start
  6.5 0.0 all-gather.2.cloned.1.call-start
  6.5 0.7 all-gather.2.cloned.1.call-update
  7.3 1.3 select_reduce_fusion
  8.6 0.4 convert_reduce_fusion.1
  9.0 0.8 convert_reduce_fusion
  9.8 0.0 copy-start.1
  9.8 1.0 copy-done.1
  10.8 0.0 copy-start.2
  10.8 1.0 pack.1
  11.8 75.2 %all_to_all.20.pay_ref = bf16[32,136,128]{2,1,0:T(8,128)(2,1)S(1)} all-to-all(bf16[32,136,128]{2,1,0:T(8,128)(2,1)S(1)} %pack.1), channel_id=1, replica_groups=mesh['replica'=32,'tensor'=16] {'replica'}, dimensions={0} | all-to-all | bytes 2228224 | tf_op jit(solution)/shard_map/all_to_all | solution.py:134
  87.1 0.0 copy-done.2
  87.1 2.6 %shrink.1 = (bf16[16,64,128]{2,1,0:T(8,128)(2,1)S(1)}, s32[16,8,128]{2,1,0:T(8,128)S(1)}) custom-call(bf16[32,136,128]{2,1,0:T(8,128)(2,1)S(1)} %all_to_all.20.pay_ref, bf16[2048,256]{1,0:T(8,128)(2,1)S(1)} %bitcast.8), custom_call_target="tpu_custom_call" | custom-call | tf_op jit(solution)/shard_map/shrink/pallas_call | solution.py:149
  89.7 14.1 %all_to_all.21.p_ref = bf16[16,64,128]{2,1,0:T(8,128)(2,1)S(1)} all-to-all(bf16[16,64,128]{2,1,0:T(8,128)(2,1)S(1)} %get-tuple-element.7), channel_id=1, replica_groups=mesh['replica'=32,'tensor'=16] {'tensor'}, dimensions={0} | all-to-all | bytes 524288 | tf_op jit(solution)/shard_map/all_to_all | solution.py:134
  103.8 0.8 total.1
  104.6 3.5 %all-to-all-start.2 = ((bf16[16,64,128]{2,1,0:T(8,128)(2,1)}), bf16[16,64,128]{2,1,0:T(8,128)(2,1)S(1)}, u32[]{:S(2)}, u32[]{:S(2)}) async-start(bf16[16,64,128]{2,1,0:T(8,128)(2,1)} %total.1), calls=%async_computation.2 | async-start | bytes 524288 | tf_op jit(solution)/shard_map/all_to_all | solution.py:134
  108.1 1.5 copy.29
  109.6 6.0 %all-to-all-done.2.s_ref = bf16[16,64,128]{2,1,0:T(8,128)(2,1)S(1)} async-done(((bf16[16,64,128]{2,1,0:T(8,128)(2,1)}), bf16[16,64,128]{2,1,0:T(8,128)(2,1)S(1)}, u32[]{:S(2)}, u32[]{:S(2)}) %all-to-all-start.2) | async-done | bytes 262176 | tf_op jit(solution)/shard_map/all_to_all | solution.py:134
  115.6 3.4 %expand.1 = bf16[32,64,256]{2,1,0:T(8,128)(2,1)} custom-call(bf16[16,64,128]{2,1,0:T(8,128)(2,1)S(1)} %all-to-all-done.2.s_ref, s32[16,8,128]{2,1,0:T(8,128)S(1)} %get-tuple-element.8.ids_ref, bf16[256,2048]{1,0:T(8,128)(2,1)S(1)} %bitcast.6), custom_call_target="tpu_custom_call" | custom-call | tf_op jit(solution)/shard_map/expand/pallas_call | solution.py:169
  119.1 9.2 %all-to-all-start.3 = ((bf16[32,64,256]{2,1,0:T(8,128)(2,1)}), bf16[32,64,256]{2,1,0:T(8,128)(2,1)S(1)}, u32[]{:S(2)}, u32[]{:S(2)}) async-start(bf16[32,64,256]{2,1,0:T(8,128)(2,1)} %expand.1), calls=%async_computation.3 | async-start | bytes 2097152 | tf_op jit(solution)/shard_map/all_to_all | solution.py:134
  128.3 0.4 fusion.8.dest_ref
  128.7 0.0 all-gather.2.cloned.1.call-done
  128.7 0.0 copy-done
  128.7 5.5 %fusion.14.base_ref = f32[768,256]{1,0:T(8,128)} fusion(bf16[768,4096]{1,0:T(8,128)(2,1)} %all-gather.2.cloned.1.call-done, bf16[4096,256]{1,0:T(8,128)(2,1)S(1)} %copy-done), kind=kOutput, calls=%fused_computation.36 | convolution fusion | flops 1610612736 | bytes 9175040 | tf_op jit(solution)/shard_map/dot_general | solution.py:179
  134.2 49.8 %all-to-all-done.3 = bf16[32,64,256]{2,1,0:T(8,128)(2,1)S(1)} async-done(((bf16[32,64,256]{2,1,0:T(8,128)(2,1)}), bf16[32,64,256]{2,1,0:T(8,128)(2,1)S(1)}, u32[]{:S(2)}, u32[]{:S(2)}) %all-to-all-start.3) | async-done | bytes 1048608 | tf_op jit(solution)/shard_map/all_to_all | solution.py:134
  184.0 0.0 copy-start.3
  184.0 1.1 copy-done.3
  185.1 1.8 final.1
  (3 shorter events, 0.0 us)
Async XLA Ops:
  6.5 122.2 %copy-start = (bf16[4096,256]{1,0:T(8,128)(2,1)S(1)}, bf16[4096,256]{1,0:T(8,128)(2,1)}, u32[]{:S(2)}) copy-start(bf16[4096,256]{1,0:T(8,128)(2,1)} %param.7) | copy-start | bytes 6291460
  6.5 122.1 %all-gather.2.cloned.1.call-start = ((), (), s32[]{:S(2)}) async-start(), calls=%async_computation.4 | async-start | bytes 6684672 | tf_op jit(solution)/shard_map/all_gather | solution.py:138
  9.8 1.0 copy-start.1
  10.8 76.3 %copy-start.2 = (bf16[32,64,256]{2,1,0:T(8,128)(2,1)S(1)}, bf16[32,64,256]{2,1,0:T(8,128)(2,1)}, u32[]{:S(2)}) copy-start(bf16[32,64,256]{2,1,0:T(8,128)(2,1)} %param.8) | copy-start | bytes 3145732
  104.6 11.0 %all-to-all-start.2 = ((bf16[16,64,128]{2,1,0:T(8,128)(2,1)}), bf16[16,64,128]{2,1,0:T(8,128)(2,1)S(1)}, u32[]{:S(2)}, u32[]{:S(2)}) async-start(bf16[16,64,128]{2,1,0:T(8,128)(2,1)} %total.1), calls=%async_computation.2 | async-start | bytes 524288 | tf_op jit(solution)/shard_map/all_to_all | solution.py:134
  119.1 64.9 %all-to-all-start.3 = ((bf16[32,64,256]{2,1,0:T(8,128)(2,1)}), bf16[32,64,256]{2,1,0:T(8,128)(2,1)S(1)}, u32[]{:S(2)}, u32[]{:S(2)}) async-start(bf16[32,64,256]{2,1,0:T(8,128)(2,1)} %expand.1), calls=%async_computation.3 | async-start | bytes 2097152 | tf_op jit(solution)/shard_map/all_to_all | solution.py:134
  184.0 1.1 copy-start.3
Sparse Core Ops, SparseCore 0:
  10.3 87.5 all-gather.1

commit v2 on v1

v2 whole, which is shorter than its diff:
```python
import jax
import jax.numpy as jnp
from jax import lax
from jax.experimental import pallas as pl
from jax.experimental.pallas import tpu as pltpu
from jax.sharding import Mesh, PartitionSpec as P

RANK = 64
SLOTS = 4
RPA = 16
PAIR = SLOTS * RPA
GROUPS = 32
HELD = 32
TENSOR = 16
ROWS = 768
WIDTH = 256
BUCKETS = GROUPS * PAIR
CHIPS = 16
PAY = 264
SCALE = 2.0

BF = jnp.bfloat16
F32 = jnp.float32
I32 = jnp.int32
NT = (((1,), (1,)), ((), ()))


def params():
    return pltpu.CompilerParams(vmem_limit_bytes=40 * 1024 * 1024)


def vmem(n):
    return [pl.BlockSpec(memory_space=pltpu.VMEM)] * n


def pack_kernel(dest_ref, local_ref, tokens_ref, out_ref):
    dest = dest_ref[...]
    local = local_ref[...]
    for b in range(8):
        at = lax.broadcasted_iota(I32, (256, ROWS), 0) + b * 256
        pick = (at == dest).astype(F32).astype(BF)
        rows = jnp.dot(pick, tokens_ref[...], preferred_element_type=F32).astype(BF)
        for j in range(2):
            for c in range(2):
                at = 128 * j + 64 * c
                out_ref[2 * b + j, 128 * c : 128 * c + 64, :] = rows[at : at + 64, 0:128]
                out_ref[2 * b + j, 128 * c + 64 : 128 * c + 128, :] = rows[at : at + 64, 128:256]
    group = lax.broadcasted_iota(I32, (GROUPS, ROWS), 0)
    to = (group == dest // PAIR).astype(F32).astype(BF)
    lane_slot = (lax.broadcasted_iota(I32, (128, ROWS), 0) % PAIR) // RPA
    slot = (dest % PAIR) // RPA
    first = dest % RPA == 0
    value = jnp.where((lane_slot == slot) & first, local.astype(F32), 0.0).astype(BF)
    ids = lax.dot_general(to, value, NT, preferred_element_type=F32)
    for z in range(CHIPS):
        two = [jnp.broadcast_to(ids[2 * z + c : 2 * z + c + 1, :], (4, 128)) for c in range(2)]
        out_ref[z, 256:264, :] = jnp.concatenate(two, axis=0).astype(BF)


def shrink_kernel(core_ref, pay_ref, own_ref, other_ref, out_ref, ids_ref):
    core = core_ref[0]
    low = lax.broadcasted_iota(I32, (8, 128), 1) < PAIR
    for pool_ref, c in ((own_ref, core), (other_ref, 1 - core)):
        at = pl.multiple_of(128 * c, 128)
        for b in range(4):
            parts = []
            marks = []
            for j in range(4):
                z = 4 * b + j
                parts.append(
                    jnp.concatenate(
                        [pay_ref[z, pl.ds(at, 64), :], pay_ref[z, pl.ds(at + 64, 64), :]], axis=1
                    )
                )
            for j in range(2):
                z = 4 * b + 2 * j
                both = jnp.where(
                    low, pay_ref[z, 256:264, :].astype(F32), pay_ref[z + 1, 256:264, :].astype(F32)
                )
                mark = jnp.where(c == 0, both[0:1, :], both[4:5, :]).astype(I32)
                ids_ref[8 * c + 2 * b + j] = jnp.broadcast_to(mark, (8, 128))
                marks.append(mark)
            rows = jnp.concatenate(parts, axis=0)
            mark = jnp.concatenate(marks, axis=1)
            total = jnp.zeros((RANK, 256), F32)
            for q in range(8):
                prod = lax.dot_general(
                    pool_ref[256 * q : 256 * q + 256, :], rows, NT, preferred_element_type=F32
                )
                for a in range(4):
                    total = total + jnp.where(mark == 4 * q + a, prod[64 * a : 64 * a + 64], 0.0)
            out_ref[8 * c + 2 * b] = total[:, 0:128].astype(BF)
            out_ref[8 * c + 2 * b + 1] = total[:, 128:256].astype(BF)


def sum_kernel(p_ref, out_ref):
    total = p_ref[0].astype(F32)
    for t in range(1, TENSOR):
        total = total + p_ref[t].astype(F32)
    mine = total.astype(BF)
    for t in range(TENSOR):
        out_ref[t] = mine


def expand_kernel(core_ref, s_ref, ids_ref, own_ref, other_ref, out_ref, m_ref):
    core = core_ref[0]
    for pool_ref, c in ((own_ref, core), (other_ref, 1 - core)):
        for b in range(4):
            at = 8 * c + 2 * b
            s = jnp.concatenate([s_ref[at], s_ref[at + 1]], axis=1).astype(F32)
            mark = jnp.concatenate([ids_ref[at][0:1], ids_ref[at + 1][0:1]], axis=1)
            for a in range(HELD):
                m_ref[64 * a : 64 * a + 64, :] = jnp.where(mark == a, s, 0.0).astype(BF)
            et = jnp.dot(pool_ref[...], m_ref[...], preferred_element_type=F32)
            rows = et.T.astype(BF)
            for j in range(4):
                out_ref[4 * b + j, c] = rows[64 * j : 64 * j + 64]


def final_kernel(dest_ref, base_ref, back_ref, out_ref):
    for b in range(3):
        at = lax.broadcasted_iota(I32, (256, BUCKETS), 1)
        pick = (at == dest_ref[256 * b : 256 * b + 256, :]).astype(F32).astype(BF)
        rows = jnp.dot(pick, back_ref[...], preferred_element_type=F32)
        out_ref[256 * b : 256 * b + 256, :] = (
            base_ref[256 * b : 256 * b + 256, :] + SCALE * rows
        ).astype(BF)


def route(row_adapter_index, adapter_pool_slot):
    table_ids = jnp.arange(adapter_pool_slot.shape[0], dtype=I32)
    pool_row = jnp.sum(
        jnp.where(row_adapter_index[:, None] == table_ids[None, :], adapter_pool_slot[None, :], 0),
        axis=1,
    )
    holder = pool_row // HELD
    order = jnp.arange(ROWS, dtype=I32)
    same = pool_row[:, None] == pool_row[None, :]
    place = jnp.sum(same & (order[None, :] < order[:, None]), axis=1)
    first = place == 0
    same_holder = holder[:, None] == holder[None, :]
    rank = jnp.sum(
        first[None, :] & same_holder & (pool_row[None, :] < pool_row[:, None]), axis=1
    )
    return (holder * SLOTS + rank) * RPA + place, pool_row % HELD


def exchange(x, axis):
    return lax.all_to_all(x, axis, split_axis=0, concat_axis=0, tiled=True)


def sibling(x):
    return lax.ppermute(x, "core", [(0, 1), (1, 0)])


def scalar():
    return pl.BlockSpec(memory_space=pltpu.SMEM)


def body(tokens, weight, a_pool, b_pool, row_adapter_index, adapter_pool_slot):
    everything = lax.all_gather(tokens, "tensor", axis=1, tiled=True)
    dest, local = route(row_adapter_index, adapter_pool_slot)
    payload = pl.pallas_call(
        pack_kernel,
        out_shape=jax.ShapeDtypeStruct((CHIPS, PAY, 128), BF),
        in_specs=vmem(3),
        out_specs=pl.BlockSpec(memory_space=pltpu.VMEM),
        compiler_params=params(),
        name="pack",
    )(dest.reshape(1, ROWS), local.reshape(1, ROWS), tokens)
    a_own = a_pool.reshape(HELD * RANK, WIDTH)
    b_own = b_pool.reshape(HELD * RANK, WIDTH).T
    a_other, b_other = sibling(a_own), sibling(b_own)
    core = lax.axis_index("core").astype(I32).reshape(1)
    arrived = exchange(payload, "z")
    partial, ids = pl.pallas_call(
        shrink_kernel,
        out_shape=(
            jax.ShapeDtypeStruct((TENSOR, RANK, 128), BF),
            jax.ShapeDtypeStruct((TENSOR, 8, 128), I32),
        ),
        in_specs=[scalar()] + vmem(3),
        out_specs=tuple(vmem(2)),
        compiler_params=params(),
        name="shrink",
    )(core, arrived, a_own, a_other)
    summed = pl.pallas_call(
        sum_kernel,
        out_shape=jax.ShapeDtypeStruct((TENSOR, RANK, 128), BF),
        in_specs=vmem(1),
        out_specs=pl.BlockSpec(memory_space=pltpu.VMEM),
        compiler_params=params(),
        name="total",
    )(exchange(partial, "tensor"))
    shrunk = exchange(summed, "tensor")
    expanded = pl.pallas_call(
        expand_kernel,
        out_shape=jax.ShapeDtypeStruct((CHIPS, 2, PAIR, WIDTH), BF),
        in_specs=[scalar()] + vmem(4),
        out_specs=pl.BlockSpec(memory_space=pltpu.VMEM),
        scratch_shapes=[pltpu.VMEM((HELD * RANK, 256), BF)],
        compiler_params=params(),
        name="expand",
    )(core, shrunk, ids, b_own, b_other)
    back = exchange(expanded, "z").reshape(BUCKETS, WIDTH)
    base = jnp.dot(everything, weight, preferred_element_type=F32)
    return pl.pallas_call(
        final_kernel,
        out_shape=jax.ShapeDtypeStruct((ROWS, WIDTH), BF),
        in_specs=vmem(3),
        out_specs=pl.BlockSpec(memory_space=pltpu.VMEM),
        compiler_params=params(),
        name="final",
    )(dest.reshape(ROWS, 1), base, back)


def solution(mesh):
    fine = Mesh(mesh.devices.reshape(CHIPS, 2, TENSOR), ("z", "core", "tensor"))
    group = ("z", "core")
    in_specs = (
        P(group, "tensor"),
        P(None, "tensor"),
        P(group, None, "tensor"),
        P(group, None, "tensor"),
        P(group),
        P(),
    )
    return jax.shard_map(
        body, mesh=fine, in_specs=in_specs, out_specs=P(group, "tensor"), check_vma=False
    )
```

time: 194 us -> 188 us (0.969)
  the two profiles are of different devices: /device:TPU:1 before, /device:TPU:32 now
where the time goes in v2:
time: 188 us; the launch traced here: 187 us
  waiting for transfers between devices  94.3 us (50%)
  starting transfers between devices  32.9 us (18%)
  blocking collectives  17.9 us (10%)
  between operations  13.5 us (7%)
  Pallas kernels  13 us (7%)
  local copies, waits for them, and re-layouts  6.89 us (4%)
  matrix products  5.46 us (3%)
  other arithmetic  2.88 us (2%)
    all_to_all x3, waiting for transfers between devices, exchange(): return lax.all_to_all(x, axis, split_axis=0, concat_axis=0, tiled=True)  93.6 us
    all_to_all x3, starting transfers between devices, exchange(): return lax.all_to_all(x, axis, split_axis=0, concat_axis=0, tiled=True)  28.6 us
    all_to_all x1, blocking collectives, exchange(): return lax.all_to_all(x, axis, split_axis=0, concat_axis=0, tiled=True)  17.9 us
    dot_general x1, matrix products, body(): base = jnp.dot(everything, weight, preferred_element_type=F32)  5.46 us
    pallas_call x1, Pallas kernels, body(): pl.pallas_call(expand_kernel, out_shape=jax.ShapeDtypeStruct((CHIPS, 2, P...  4.65 us
    unnamed x10, local copies, waits for them, and re-layouts  4.62 us
    ppermute x2, starting transfers between devices, sibling(): return lax.ppermute(x, 'core', [(0, 1), (1, 0)])  4.31 us
    pallas_call x1, Pallas kernels, body(): pl.pallas_call(shrink_kernel, out_shape=(jax.ShapeDtypeStruct((TENSOR, RA...  3.76 us
  transfers between devices with their start and end apart: 6, of which 3 were waited for; matrix products, arithmetic and copies ran while one was open for 6% of the time, Pallas kernels for 6%

profile of v2, /device:TPU:32, one launch (start us, length us, event | category | flops | bytes accessed | tf_op | source)
XLA Modules:
  0.0 186.9 jit_solution(12832234695876893409)
XLA Ops:
  6.5 0.0 copy-start
  6.5 0.0 all-gather.2.cloned.1.call-start
  6.5 0.7 all-gather.2.cloned.1.call-update
  7.3 1.3 select_reduce_fusion
  8.6 0.4 convert_reduce_fusion.1
  9.0 0.8 convert_reduce_fusion
  9.8 0.0 copy-start.2
  9.8 1.0 copy-done.2
  10.8 2.1 %pack.1 = bf16[16,264,128]{2,1,0:T(8,128)(2,1)} custom-call(s32[1,768]{1,0:T(1,128)S(1)} %get-tuple-element.10.dest_ref, s32[1,768]{1,0:T(1,128)S(1)} %get-tuple-element.9.local_ref, bf16[768,256]{1,0:T(8,128)(2,1)S(1)} %copy-done.2), custom_call_target="tpu_custom_call" | custom-call | tf_op jit(solution)/shard_map/pack/pallas_call | solution.py:163
  12.8 15.2 %all-to-all-start = ((bf16[16,264,128]{2,1,0:T(8,128)(2,1)}), bf16[16,264,128]{2,1,0:T(8,128)(2,1)S(1)}, u32[]{:S(2)}, u32[]{:S(2)}) async-start(bf16[16,264,128]{2,1,0:T(8,128)(2,1)} %pack.1), calls=%async_computation | async-start | bytes 2162688 | tf_op jit(solution)/shard_map/all_to_all | solution.py:149
  28.1 1.9 %collective-permute-start = (bf16[2048,256]{1,0:T(8,128)(2,1)}, bf16[2048,256]{1,0:T(8,128)(2,1)}, u32[]{:S(2)}, u32[]{:S(2)}) collective-permute-start(bf16[2048,256]{1,0:T(8,128)(2,1)} %bitcast.10), channel_id=1, source_target_pairs={{0,16},{16,0},{1,17},{17,1},{2,18},{18,2},{3,19},{19,3},{4,20},{20... | collective-permute-start | bytes 3145736 | tf_op jit(solution)/shard_map/ppermute | solution.py:153
  30.0 2.3 %copy.29 = bf16[2048,256]{0,1:T(8,128)(2,1)} copy(bf16[2048,256]{1,0:T(8,128)(2,1)} %bitcast.12) | data formatting | bytes 2097152 | tf_op jit(solution)/shard_map/reshape | solution.py:172
  32.3 2.4 %collective-permute-start.1 = (bf16[256,2048]{1,0:T(8,128)(2,1)}, bf16[256,2048]{1,0:T(8,128)(2,1)}, u32[]{:S(2)}, u32[]{:S(2)}) collective-permute-start(bf16[256,2048]{1,0:T(8,128)(2,1)} %bitcast.7), channel_id=1, source_target_pairs={{0,16},{16,0},{1,17},{17,1},{2,18},{18,2},{3,19},{19,3},{4,20},{20... | collective-permute-start | bytes 3145736 | tf_op jit(solution)/shard_map/ppermute | solution.py:153
  34.7 0.0 collective-permute-done.other_ref
  34.7 44.1 %all-to-all-done.pay_ref = bf16[16,264,128]{2,1,0:T(8,128)(2,1)S(1)} async-done(((bf16[16,264,128]{2,1,0:T(8,128)(2,1)}), bf16[16,264,128]{2,1,0:T(8,128)(2,1)S(1)}, u32[]{:S(2)}, u32[]{:S(2)}) %all-to-all-start) | async-done | bytes 1081376 | tf_op jit(solution)/shard_map/all_to_all | solution.py:149
  78.8 0.0 copy-start.3
  78.8 1.3 copy-done.3
  80.1 3.8 %shrink.1 = (bf16[16,64,128]{2,1,0:T(8,128)(2,1)S(1)}, s32[16,8,128]{2,1,0:T(8,128)S(1)}) custom-call(s32[1]{0:T(128)} %bitcast.core_ref, bf16[16,264,128]{2,1,0:T(8,128)(2,1)S(1)} %all-to-all-done.pay_ref, bf16[2048,256]{1,0:T(8,128)(2,1)S(1)} %bitcast.11, bf16[2048,256]{1,0:T(8,128)(2,1)} %collective-permute-done.other_ref), custom_call_target="tpu_custom_call" | custom-call | tf_op jit(solution)/shard_map/shrink/pallas_call | solution.py:176
  83.8 17.9 %all_to_all.20.p_ref = bf16[16,64,128]{2,1,0:T(8,128)(2,1)S(1)} all-to-all(bf16[16,64,128]{2,1,0:T(8,128)(2,1)S(1)} %get-tuple-element.7), channel_id=1, replica_groups=mesh['z'=16,'core'=2,'tensor'=16] {'tensor'}, dimensions={0} | all-to-all | bytes 524288 | tf_op jit(solution)/shard_map/all_to_all | solution.py:149
  101.8 0.8 total.1
  102.5 3.5 %all-to-all-start.2 = ((bf16[16,64,128]{2,1,0:T(8,128)(2,1)}), bf16[16,64,128]{2,1,0:T(8,128)(2,1)S(1)}, u32[]{:S(2)}, u32[]{:S(2)}) async-start(bf16[16,64,128]{2,1,0:T(8,128)(2,1)} %total.1), calls=%async_computation.2 | async-start | bytes 524288 | tf_op jit(solution)/shard_map/all_to_all | solution.py:149
  106.0 0.0 collective-permute-done.1.other_ref
  106.1 8.6 %all-to-all-done.2.s_ref = bf16[16,64,128]{2,1,0:T(8,128)(2,1)S(1)} async-done(((bf16[16,64,128]{2,1,0:T(8,128)(2,1)}), bf16[16,64,128]{2,1,0:T(8,128)(2,1)S(1)}, u32[]{:S(2)}, u32[]{:S(2)}) %all-to-all-start.2) | async-done | bytes 262176 | tf_op jit(solution)/shard_map/all_to_all | solution.py:149
  114.7 0.0 copy-start.1
  114.7 1.2 copy-done.1
  115.9 4.7 %expand.1 = bf16[16,2,64,256]{3,2,1,0:T(8,128)(2,1)} custom-call(s32[1]{0:T(128)} %bitcast.core_ref, bf16[16,64,128]{2,1,0:T(8,128)(2,1)S(1)} %all-to-all-done.2.s_ref, s32[16,8,128]{2,1,0:T(8,128)S(1)} %get-tuple-element.8.ids_ref, bf16[256,2048]{1,0:T(8,128)(2,1)S(1)} %bitcast.8, bf16[256,2048]{1,0:T(8,128)(2,1)} %collective-permute-done.1.other_ref), custom_call_target="tpu_custom_call" | custom-call | tf_op jit(solution)/shard_map/expand/pallas_call | solution.py:196
  120.6 9.9 %all-to-all-start.3 = ((bf16[16,2,64,256]{3,2,1,0:T(8,128)(2,1)}), bf16[16,2,64,256]{3,2,1,0:T(8,128)(2,1)S(1)}, u32[]{:S(2)}, u32[]{:S(2)}) async-start(bf16[16,2,64,256]{3,2,1,0:T(8,128)(2,1)} %expand.1), calls=%async_computation.3 | async-start | bytes 2097152 | tf_op jit(solution)/shard_map/all_to_all | solution.py:149
  130.5 0.4 fusion.8.dest_ref
  130.8 0.0 all-gather.2.cloned.1.call-done
  130.9 0.0 copy-done
  130.9 5.5 %fusion.14.base_ref = f32[768,256]{1,0:T(8,128)} fusion(bf16[768,4096]{1,0:T(8,128)(2,1)} %all-gather.2.cloned.1.call-done, bf16[4096,256]{1,0:T(8,128)(2,1)S(1)} %copy-done), kind=kOutput, calls=%fused_computation.36 | convolution fusion | flops 1610612736 | bytes 9175040 | tf_op jit(solution)/shard_map/dot_general | solution.py:206
  136.3 40.9 %all-to-all-done.3 = bf16[16,2,64,256]{3,2,1,0:T(8,128)(2,1)S(1)} async-done(((bf16[16,2,64,256]{3,2,1,0:T(8,128)(2,1)}), bf16[16,2,64,256]{3,2,1,0:T(8,128)(2,1)S(1)}, u32[]{:S(2)}, u32[]{:S(2)}) %all-to-all-start.3) | async-done | bytes 1048608 | tf_op jit(solution)/shard_map/all_to_all | solution.py:149
  177.2 0.0 copy-start.4
  177.2 1.1 copy-done.4
  178.3 1.8 final.1
  (3 shorter events, 0.0 us)
Async XLA Ops:
  6.5 124.3 %copy-start = (bf16[4096,256]{1,0:T(8,128)(2,1)S(1)}, bf16[4096,256]{1,0:T(8,128)(2,1)}, u32[]{:S(2)}) copy-start(bf16[4096,256]{1,0:T(8,128)(2,1)} %param.7) | copy-start | bytes 6291460
  6.5 124.3 %all-gather.2.cloned.1.call-start = ((), (), s32[]{:S(2)}) async-start(), calls=%async_computation.4 | async-start | bytes 6684672 | tf_op jit(solution)/shard_map/all_gather | solution.py:161
  9.8 1.0 copy-start.2
  12.8 65.9 %all-to-all-start = ((bf16[16,264,128]{2,1,0:T(8,128)(2,1)}), bf16[16,264,128]{2,1,0:T(8,128)(2,1)S(1)}, u32[]{:S(2)}, u32[]{:S(2)}) async-start(bf16[16,264,128]{2,1,0:T(8,128)(2,1)} %pack.1), calls=%async_computation | async-start | bytes 2162688 | tf_op jit(solution)/shard_map/all_to_all | solution.py:149
  28.1 6.6 %collective-permute-start = (bf16[2048,256]{1,0:T(8,128)(2,1)}, bf16[2048,256]{1,0:T(8,128)(2,1)}, u32[]{:S(2)}, u32[]{:S(2)}) collective-permute-start(bf16[2048,256]{1,0:T(8,128)(2,1)} %bitcast.10), channel_id=1, source_target_pairs={{0,16},{16,0},{1,17},{17,1},{2,18},{18,2},{3,19},{19,3},{4,20},{20... | collective-permute-start | bytes 3145736 | tf_op jit(solution)/shard_map/ppermute | solution.py:153
  32.3 73.8 %collective-permute-start.1 = (bf16[256,2048]{1,0:T(8,128)(2,1)}, bf16[256,2048]{1,0:T(8,128)(2,1)}, u32[]{:S(2)}, u32[]{:S(2)}) collective-permute-start(bf16[256,2048]{1,0:T(8,128)(2,1)} %bitcast.7), channel_id=1, source_target_pairs={{0,16},{16,0},{1,17},{17,1},{2,18},{18,2},{3,19},{19,3},{4,20},{20... | collective-permute-start | bytes 3145736 | tf_op jit(solution)/shard_map/ppermute | solution.py:153
  78.8 1.3 copy-start.3
  102.5 12.2 %all-to-all-start.2 = ((bf16[16,64,128]{2,1,0:T(8,128)(2,1)}), bf16[16,64,128]{2,1,0:T(8,128)(2,1)S(1)}, u32[]{:S(2)}, u32[]{:S(2)}) async-start(bf16[16,64,128]{2,1,0:T(8,128)(2,1)} %total.1), calls=%async_computation.2 | async-start | bytes 524288 | tf_op jit(solution)/shard_map/all_to_all | solution.py:149
  114.7 1.2 copy-start.1
  120.6 56.6 %all-to-all-start.3 = ((bf16[16,2,64,256]{3,2,1,0:T(8,128)(2,1)}), bf16[16,2,64,256]{3,2,1,0:T(8,128)(2,1)S(1)}, u32[]{:S(2)}, u32[]{:S(2)}) async-start(bf16[16,2,64,256]{3,2,1,0:T(8,128)(2,1)} %expand.1), calls=%async_computation.3 | async-start | bytes 2097152 | tf_op jit(solution)/shard_map/all_to_all | solution.py:149
  177.2 1.1 copy-start.4
Sparse Core Ops, SparseCore 0:
  10.3 90.0 all-gather.1

commit v3 on v2

v3 whole, which is shorter than its diff:
```python
import jax
import jax.numpy as jnp
from jax import lax
from jax.experimental import pallas as pl
from jax.experimental.pallas import tpu as pltpu
from jax.sharding import Mesh, PartitionSpec as P

RANK = 64
SLOTS = 4
RPA = 16
PAIR = SLOTS * RPA
GROUPS = 32
HELD = 32
TENSOR = 16
ROWS = 768
WIDTH = 256
BUCKETS = GROUPS * PAIR
CHIPS = 16
PAY = 264
SCALE = 2.0

BF = jnp.bfloat16
F32 = jnp.float32
I32 = jnp.int32
NT = (((1,), (1,)), ((), ()))


def params():
    return pltpu.CompilerParams(vmem_limit_bytes=40 * 1024 * 1024)


def vmem(n):
    return [pl.BlockSpec(memory_space=pltpu.VMEM)] * n


def pack_kernel(dest_ref, local_ref, tokens_hbm, out_ref, tokens_ref, sem):
    bring = pltpu.make_async_copy(tokens_hbm, tokens_ref, sem.at[0])
    bring.start()
    dest = dest_ref[...]
    local = local_ref[...]
    line = lax.broadcasted_iota(I32, (8 * CHIPS, ROWS), 0)
    to = (line // 4 == dest // PAIR).astype(F32).astype(BF)
    lane_slot = (lax.broadcasted_iota(I32, (128, ROWS), 0) % PAIR) // RPA
    slot = (dest % PAIR) // RPA
    first = dest % RPA == 0
    value = jnp.where((lane_slot == slot) & first, local.astype(F32), 0.0).astype(BF)
    ids = lax.dot_general(to, value, NT, preferred_element_type=F32)
    for z in range(CHIPS):
        out_ref[z, 256:264, :] = ids[8 * z : 8 * z + 8, :].astype(BF)
    bring.wait()
    for b in range(8):
        at = lax.broadcasted_iota(I32, (256, ROWS), 0) + b * 256
        pick = (at == dest).astype(F32).astype(BF)
        rows = jnp.dot(pick, tokens_ref[...], preferred_element_type=F32).astype(BF)
        for j in range(2):
            for c in range(2):
                at = 128 * j + 64 * c
                out_ref[2 * b + j, 128 * c : 128 * c + 64, :] = rows[at : at + 64, 0:128]
                out_ref[2 * b + j, 128 * c + 64 : 128 * c + 128, :] = rows[at : at + 64, 128:256]


def shrink_kernel(core_ref, pay_ref, own_hbm, other_hbm, out_ref, ids_ref, pools, sem):
    core = core_ref[0]
    brings = [
        pltpu.make_async_copy(pool, pools.at[i], sem.at[i])
        for i, pool in enumerate((own_hbm, other_hbm))
    ]
    for bring in brings:
        bring.start()
    low = lax.broadcasted_iota(I32, (8, 128), 1) < PAIR
    for i, c in enumerate((core, 1 - core)):
        brings[i].wait()
        at = pl.multiple_of(128 * c, 128)
        for b in range(4):
            parts = []
            marks = []
            for j in range(4):
                z = 4 * b + j
                both = pay_ref[z, pl.ds(at, 128), :]
                parts.append(jnp.concatenate([both[0:64], both[64:128]], axis=1))
            for j in range(2):
                z = 4 * b + 2 * j
                both = jnp.where(
                    low, pay_ref[z, 256:264, :].astype(F32), pay_ref[z + 1, 256:264, :].astype(F32)
                )
                mark = jnp.where(c == 0, both[0:1, :], both[4:5, :])
                ids_ref[8 * c + 2 * b + j] = jnp.broadcast_to(mark, (8, 128))
                marks.append(mark)
            rows = jnp.concatenate(parts, axis=0)
            mark = jnp.broadcast_to(jnp.concatenate(marks, axis=1), (RANK, 256))
            total = jnp.zeros((RANK, 256), F32)
            for q in range(8):
                prod = lax.dot_general(
                    pools[i, 256 * q : 256 * q + 256, :], rows, NT, preferred_element_type=F32
                )
                for a in range(4):
                    total = jnp.where(mark == 4 * q + a, prod[64 * a : 64 * a + 64], total)
            out_ref[8 * c + 2 * b] = total[:, 0:128].astype(BF)
            out_ref[8 * c + 2 * b + 1] = total[:, 128:256].astype(BF)


def sum_kernel(p_ref, out_ref):
    total = p_ref[0].astype(F32)
    for t in range(1, TENSOR):
        total = total + p_ref[t].astype(F32)
    mine = total.astype(BF)
    for t in range(TENSOR):
        out_ref[t] = mine


def expand_kernel(core_ref, s_ref, ids_ref, own_hbm, other_hbm, out_ref, m_ref, pools, sem):
    core = core_ref[0]
    brings = [
        pltpu.make_async_copy(pool, pools.at[i], sem.at[i])
        for i, pool in enumerate((own_hbm, other_hbm))
    ]
    for bring in brings:
        bring.start()
    for i, c in enumerate((core, 1 - core)):
        for b in range(4):
            at = 8 * c + 2 * b
            s = jnp.concatenate([s_ref[at], s_ref[at + 1]], axis=1)
            mark = jnp.concatenate([ids_ref[at][0:1], ids_ref[at + 1][0:1]], axis=1)
            mark = jnp.broadcast_to(mark, (RANK, 256)).astype(BF)
            for a in range(HELD):
                m_ref[b % 2, 64 * a : 64 * a + 64, :] = jnp.where(
                    mark == jnp.asarray(a, BF), s, jnp.zeros_like(s)
                )
            if b == 0:
                brings[i].wait()
            et = jnp.dot(pools[i], m_ref[b % 2], preferred_element_type=F32)
            rows = et.T.astype(BF)
            for j in range(4):
                out_ref[4 * b + j, c] = rows[64 * j : 64 * j + 64]


def base_kernel(place_ref, *refs):
    xs, ws, outs = refs[0:4], refs[4:8], refs[8:12]
    place = place_ref[0]
    for s in range(4):
        for half in range(2):
            at = 384 * half
            total = jnp.zeros((384, WIDTH), F32)
            for d in range(4):
                row = pl.multiple_of(((place + d) % 4) * WIDTH, WIDTH)
                total = total + jnp.dot(
                    xs[d][at : at + 384, :],
                    ws[s][pl.ds(row, WIDTH), :],
                    preferred_element_type=F32,
                )
            outs[s][at : at + 384, :] = total.astype(outs[s].dtype)


def final_kernel(dest_ref, p0_hbm, p1_hbm, p2_hbm, p3_hbm, back_ref, out_ref, p0, pn, sem):
    brings = [pltpu.make_async_copy(p0_hbm, p0, sem.at[3])]
    for i, part in enumerate((p1_hbm, p2_hbm, p3_hbm)):
        brings.append(pltpu.make_async_copy(part, pn.at[i], sem.at[i]))
    for bring in brings:
        bring.start()
    for b in range(3):
        lo = 256 * b
        at = lax.broadcasted_iota(I32, (256, BUCKETS), 1)
        pick = (at == dest_ref[lo : lo + 256, :]).astype(F32).astype(BF)
        rows = jnp.dot(pick, back_ref[...], preferred_element_type=F32)
        if b == 0:
            for bring in brings:
                bring.wait()
        base = p0[lo : lo + 256, :]
        for i in range(3):
            base = base + pn[i, lo : lo + 256, :].astype(F32)
        out_ref[lo : lo + 256, :] = (base + SCALE * rows).astype(BF)


def route(row_adapter_index, adapter_pool_slot):
    table_ids = jnp.arange(adapter_pool_slot.shape[0], dtype=I32)
    pool_row = jnp.sum(
        jnp.where(row_adapter_index[:, None] == table_ids[None, :], adapter_pool_slot[None, :], 0),
        axis=1,
    )
    holder = pool_row // HELD
    order = jnp.arange(ROWS, dtype=I32)
    same = pool_row[:, None] == pool_row[None, :]
    place = jnp.sum(same & (order[None, :] < order[:, None]), axis=1)
    first = place == 0
    same_holder = holder[:, None] == holder[None, :]
    rank = jnp.sum(
        first[None, :] & same_holder & (pool_row[None, :] < pool_row[:, None]), axis=1
    )
    return (holder * SLOTS + rank) * RPA + place, pool_row % HELD


def exchange(x, axis):
    return lax.all_to_all(x, axis, split_axis=0, concat_axis=0, tiled=True)


def sibling(x):
    return lax.ppermute(x, "core", [(0, 1), (1, 0)])


def scalar():
    return pl.BlockSpec(memory_space=pltpu.SMEM)


def hbm(n):
    return [pl.BlockSpec(memory_space=pltpu.HBM)] * n


def turn(x, axis, step):
    return lax.ppermute(x, axis, [(i, (i + step) % 4) for i in range(4)])


def body(tokens, weight, a_pool, b_pool, row_adapter_index, adapter_pool_slot):
    tensor = ("y", "x")
    y = lax.axis_index("y")
    core = lax.axis_index("core").astype(I32).reshape(1)
    dest, local = route(row_adapter_index, adapter_pool_slot)
    payload = pl.pallas_call(
        pack_kernel,
        out_shape=jax.ShapeDtypeStruct((CHIPS, PAY, 128), BF),
        in_specs=vmem(2) + hbm(1),
        out_specs=pl.BlockSpec(memory_space=pltpu.VMEM),
        scratch_shapes=[pltpu.VMEM((ROWS, WIDTH), BF), pltpu.SemaphoreType.DMA((1,))],
        compiler_params=params(),
        name="pack",
    )(dest.reshape(1, ROWS), local.reshape(1, ROWS), tokens)
    tokens, weight, a_pool, b_pool, payload = lax.optimization_barrier(
        (tokens, weight, a_pool, b_pool, payload)
    )
    a_own = a_pool.reshape(HELD * RANK, WIDTH)
    b_own = b_pool.reshape(HELD * RANK, WIDTH).T
    a_other, b_other = sibling(a_own), sibling(b_own)
    arrived = exchange(payload, "z")
    xs = [tokens] + [turn(tokens, "x", -d) for d in range(1, 4)]
    ws = []
    for s in range(4):
        mine = lax.dynamic_slice(weight, (((y - s) % 4) * 4 * WIDTH, 0), (4 * WIDTH, WIDTH))
        ws.append(turn(mine, "y", -s) if s else mine)
    parts = pl.pallas_call(
        base_kernel,
        out_shape=tuple(jax.ShapeDtypeStruct((ROWS, WIDTH), BF if s else F32) for s in range(4)),
        in_specs=[scalar()] + vmem(8),
        out_specs=tuple(vmem(4)),
        compiler_params=params(),
        cost_estimate=pl.CostEstimate(
            flops=2 * ROWS * 16 * WIDTH * WIDTH, bytes_accessed=6 * 2**20, transcendentals=0
        ),
        name="base",
    )(lax.axis_index("x").astype(I32).reshape(1), *xs, *ws)
    arrived, *parts = lax.optimization_barrier((arrived, *parts))
    partial, ids = pl.pallas_call(
        shrink_kernel,
        out_shape=(
            jax.ShapeDtypeStruct((TENSOR, RANK, 128), BF),
            jax.ShapeDtypeStruct((TENSOR, 8, 128), F32),
        ),
        in_specs=[scalar()] + vmem(1) + hbm(2),
        out_specs=tuple(vmem(2)),
        scratch_shapes=[pltpu.VMEM((2, HELD * RANK, WIDTH), BF), pltpu.SemaphoreType.DMA((2,))],
        compiler_params=params(),
        name="shrink",
    )(core, arrived, a_own, a_other)
    summed = pl.pallas_call(
        sum_kernel,
        out_shape=jax.ShapeDtypeStruct((TENSOR, RANK, 128), BF),
        in_specs=vmem(1),
        out_specs=pl.BlockSpec(memory_space=pltpu.VMEM),
        compiler_params=params(),
        name="total",
    )(exchange(partial, tensor))
    shrunk = exchange(summed, tensor)
    expanded = pl.pallas_call(
        expand_kernel,
        out_shape=jax.ShapeDtypeStruct((CHIPS, 2, PAIR, WIDTH), BF),
        in_specs=[scalar()] + vmem(2) + hbm(2),
        out_specs=pl.BlockSpec(memory_space=pltpu.VMEM),
        scratch_shapes=[
            pltpu.VMEM((2, HELD * RANK, 256), BF),
            pltpu.VMEM((2, WIDTH, HELD * RANK), BF),
            pltpu.SemaphoreType.DMA((2,)),
        ],
        compiler_params=params(),
        name="expand",
    )(core, shrunk, ids, b_own, b_other)
    p0, p1, p2, p3, expanded = lax.optimization_barrier((*parts, expanded))
    back = exchange(expanded, "z").reshape(BUCKETS, WIDTH)
    sums = [turn(p, "y", s) for s, p in ((1, p1), (2, p2), (3, p3))]
    return pl.pallas_call(
        final_kernel,
        out_shape=jax.ShapeDtypeStruct((ROWS, WIDTH), BF),
        in_specs=vmem(1) + hbm(4) + vmem(1),
        out_specs=pl.BlockSpec(memory_space=pltpu.VMEM),
        scratch_shapes=[
            pltpu.VMEM((ROWS, WIDTH), F32),
            pltpu.VMEM((3, ROWS, WIDTH), BF),
            pltpu.SemaphoreType.DMA((4,)),
        ],
        compiler_params=params(),
        name="final",
    )(dest.reshape(ROWS, 1), p0, *sums, back)


def solution(mesh):
    fine = Mesh(mesh.devices.reshape(CHIPS, 2, 4, 4), ("z", "core", "y", "x"))
    group = ("z", "core")
    tensor = ("y", "x")
    in_specs = (
        P(group, tensor),
        P(None, tensor),
        P(group, None, tensor),
        P(group, None, tensor),
        P(group),
        P(),
    )
    return jax.shard_map(
        body, mesh=fine, in_specs=in_specs, out_specs=P(group, tensor), check_vma=False
    )
```

time: 188 us -> 173 us (0.920)
  the two profiles are of different devices: /device:TPU:32 before, /device:TPU:96 now
where the time goes in v3:
time: 173 us; the launch traced here: 172 us
  starting transfers between devices  65.2 us (38%)
  waiting for transfers between devices  63.8 us (37%)
  Pallas kernels  17.2 us (10%)
  blocking collectives  12.3 us (7%)
  local copies, waits for them, and re-layouts  9.82 us (6%)
  other arithmetic  2.97 us (2%)
    all_to_all x3, waiting for transfers between devices, exchange(): return lax.all_to_all(x, axis, split_axis=0, concat_axis=0, tiled=True)  34.1 us
    ppermute x9, starting transfers between devices, turn(): return lax.ppermute(x, axis, [(i, (i + step) % 4) for i in range(4)])  31.3 us
    all_to_all x3, starting transfers between devices, exchange(): return lax.all_to_all(x, axis, split_axis=0, concat_axis=0, tiled=True)  30 us
    ppermute x9, waiting for transfers between devices, turn(): return lax.ppermute(x, axis, [(i, (i + step) % 4) for i in range(4)])  29.8 us
    all_to_all x1, blocking collectives, exchange(): return lax.all_to_all(x, axis, split_axis=0, concat_axis=0, tiled=True)  12.3 us
    unnamed x16, local copies, waits for them, and re-layouts  5.42 us
    pallas_call x1, Pallas kernels, body(): pl.pallas_call(base_kernel, out_shape=tuple((jax.ShapeDtypeStruct((ROWS,...  4.15 us
    pallas_call x1, Pallas kernels, body(): pl.pallas_call(expand_kernel, out_shape=jax.ShapeDtypeStruct((CHIPS, 2, P...  3.86 us
  transfers between devices with their start and end apart: 14, of which 7 were waited for; matrix products, arithmetic and copies ran while one was open for 3% of the time, Pallas kernels for 4%

profile of v3, /device:TPU:96, one launch (start us, length us, event | category | flops | bytes accessed | tf_op | source)
XLA Modules:
  0.0 171.6 jit_solution(7319686856785337170)
XLA Ops:
  0.0 0.0 copy-start
  0.0 1.4 select_reduce_fusion
  1.4 0.4 convert_reduce_fusion.1
  1.8 0.8 convert_reduce_fusion
  2.6 3.1 %pack.1 = bf16[16,264,128]{2,1,0:T(8,128)(2,1)} custom-call(s32[1,768]{1,0:T(1,128)S(1)} %get-tuple-element.52.dest_ref, s32[1,768]{1,0:T(1,128)S(1)} %get-tuple-element.51.local_ref, bf16[768,256]{1,0:T(8,128)(2,1)} %refs_0_), custom_call_target="tpu_custom_call" | custom-call | tf_op jit(solution)/shard_map/pack/pallas_call | solution.py:217
  5.7 14.3 %all-to-all-start = ((bf16[16,264,128]{2,1,0:T(8,128)(2,1)}), bf16[16,264,128]{2,1,0:T(8,128)(2,1)S(1)}, u32[]{:S(2)}, u32[]{:S(2)}) async-start(bf16[16,264,128]{2,1,0:T(8,128)(2,1)} %pack.1), calls=%async_computation | async-start | bytes 2162688 | tf_op jit(solution)/shard_map/all_to_all | solution.py:193
  20.0 4.7 %collective-permute-start = (bf16[768,256]{1,0:T(8,128)(2,1)}, bf16[768,256]{1,0:T(8,128)(2,1)S(1)}, u32[]{:S(2)}, u32[]{:S(2)}) collective-permute-start(bf16[768,256]{1,0:T(8,128)(2,1)} %refs_0_), channel_id=1, source_target_pairs={{0,3},{1,0},{2,1},{3,2},{4,7},{5,4},{6,5},{7,6},{8,11},{9,8},{10,9... | collective-permute-start | bytes 1179656 | tf_op jit(solution)/shard_map/ppermute | solution.py:209
  24.7 2.7 %collective-permute-start.1 = (bf16[768,256]{1,0:T(8,128)(2,1)}, bf16[768,256]{1,0:T(8,128)(2,1)S(1)}, u32[]{:S(2)}, u32[]{:S(2)}) collective-permute-start(bf16[768,256]{1,0:T(8,128)(2,1)} %refs_0_), channel_id=1, source_target_pairs={{0,2},{1,3},{2,0},{3,1},{4,6},{5,7},{6,4},{7,5},{8,10},{9,11},{10,... | collective-permute-start | bytes 1179656 | tf_op jit(solution)/shard_map/ppermute | solution.py:209
  27.4 0.0 copy-done
  27.4 1.9 %collective-permute-start.6 = (bf16[2048,256]{1,0:T(8,128)(2,1)S(1)}, bf16[2048,256]{1,0:T(8,128)(2,1)}, u32[]{:S(2)}, u32[]{:S(2)}) collective-permute-start(bf16[2048,256]{1,0:T(8,128)(2,1)S(1)} %bitcast.9), channel_id=1, source_target_pairs={{0,16},{16,0},{1,17},{17,1},{2,18},{18,2},{3,19},{19,3},{4,20},{20... | collective-permute-start | bytes 3145736 | tf_op jit(solution)/shard_map/ppermute | solution.py:197
  29.3 2.8 %collective-permute-start.2 = (bf16[768,256]{1,0:T(8,128)(2,1)}, bf16[768,256]{1,0:T(8,128)(2,1)}, u32[]{:S(2)}, u32[]{:S(2)}) collective-permute-start(bf16[768,256]{1,0:T(8,128)(2,1)} %refs_0_), channel_id=1, source_target_pairs={{0,1},{1,2},{2,3},{3,0},{4,5},{5,6},{6,7},{7,4},{8,9},{9,10},{10,1... | collective-permute-start | bytes 1179656 | tf_op jit(solution)/shard_map/ppermute | solution.py:209
  32.2 2.9 %constant_dynamic-slice_fusion.3 = (bf16[1024,256]{1,0:T(8,128)(2,1)}, bf16[1024,256]{1,0:T(8,128)(2,1)}, bf16[1024,256]{1,0:T(8,128)(2,1)}, bf16[1024,256]{1,0:T(8,128)(2,1)}) fusion(bf16[4096,256]{1,0:T(8,128)(2,1)} %param.7, s32[]{:T(128)S(6)} %select_n.89, s32[]{:T(128)S(6)} %select_n.87, s32[]{:T(128)S(6)} %select_n.85, s32[]{:T(128)S(6)} %select_n.83), kind=kLoop, calls=%fused_computation.39 | loop fusion | bytes 4194320 | tf_op jit(solution)/shard_map/dynamic_slice | solution.py:236
  35.1 4.9 %collective-permute-start.3 = (bf16[1024,256]{1,0:T(8,128)(2,1)}, bf16[1024,256]{1,0:T(8,128)(2,1)}, u32[]{:S(2)}, u32[]{:S(2)}) collective-permute-start(bf16[1024,256]{1,0:T(8,128)(2,1)} %get-tuple-element.49), channel_id=1, source_target_pairs={{0,12},{4,0},{8,4},{12,8},{1,13},{5,1},{9,5},{13,9},{2,14},{6,2},{... | collective-permute-start | bytes 1572872 | tf_op jit(solution)/shard_map/ppermute | solution.py:209
  40.0 1.2 collective-permute-done.refs_1_
  41.2 0.0 copy-start.4
  41.2 0.7 copy-done.4
  42.0 5.1 %collective-permute-start.4 = (bf16[1024,256]{1,0:T(8,128)(2,1)}, bf16[1024,256]{1,0:T(8,128)(2,1)}, u32[]{:S(2)}, u32[]{:S(2)}) collective-permute-start(bf16[1024,256]{1,0:T(8,128)(2,1)} %get-tuple-element.48), channel_id=1, source_target_pairs={{0,8},{4,12},{8,0},{12,4},{1,9},{5,13},{9,1},{13,5},{2,10},{6,14},... | collective-permute-start | bytes 1572872 | tf_op jit(solution)/shard_map/ppermute | solution.py:209
  47.1 0.0 collective-permute-done.1.refs_2_
  47.1 0.0 copy-start.6
  47.1 0.7 copy-done.6
  47.8 2.6 %collective-permute-start.5 = (bf16[1024,256]{1,0:T(8,128)(2,1)}, bf16[1024,256]{1,0:T(8,128)(2,1)}, u32[]{:S(2)}, u32[]{:S(2)}) collective-permute-start(bf16[1024,256]{1,0:T(8,128)(2,1)} %get-tuple-element.47), channel_id=1, source_target_pairs={{0,4},{4,8},{8,12},{12,0},{1,5},{5,9},{9,13},{13,1},{2,6},{6,10},{... | collective-permute-start | bytes 1572872 | tf_op jit(solution)/shard_map/ppermute | solution.py:209
  50.4 1.5 copy.29
  51.9 0.0 collective-permute-done.2.refs_3_
  51.9 1.9 %collective-permute-start.7 = (bf16[256,2048]{1,0:T(8,128)(2,1)S(1)}, bf16[256,2048]{1,0:T(8,128)(2,1)}, u32[]{:S(2)}, u32[]{:S(2)}) collective-permute-start(bf16[256,2048]{1,0:T(8,128)(2,1)S(1)} %bitcast.6), channel_id=1, source_target_pairs={{0,16},{16,0},{1,17},{17,1},{2,18},{18,2},{3,19},{19,3},{4,20},{20... | collective-permute-start | bytes 3145736 | tf_op jit(solution)/shard_map/ppermute | solution.py:197
  53.9 9.3 %collective-permute-done.3.refs_5_ = bf16[1024,256]{1,0:T(8,128)(2,1)} collective-permute-done((bf16[1024,256]{1,0:T(8,128)(2,1)}, bf16[1024,256]{1,0:T(8,128)(2,1)}, u32[]{:S(2)}, u32[]{:S(2)}) %collective-permute-start.3) | collective-permute-done | bytes 524320 | tf_op jit(solution)/shard_map/ppermute | solution.py:209
  63.1 0.0 collective-permute-done.4.refs_6_
  63.1 6.4 %collective-permute-done.5.refs_7_ = bf16[1024,256]{1,0:T(8,128)(2,1)} collective-permute-done((bf16[1024,256]{1,0:T(8,128)(2,1)}, bf16[1024,256]{1,0:T(8,128)(2,1)}, u32[]{:S(2)}, u32[]{:S(2)}) %collective-permute-start.5) | collective-permute-done | bytes 524320 | tf_op jit(solution)/shard_map/ppermute | solution.py:209
  69.5 0.0 copy-start.3
  69.5 1.0 copy-done.3
  70.5 0.0 copy-start.5
  70.5 1.0 copy-done.5
  71.5 0.0 copy-start.7
  71.5 1.0 copy-done.7
  72.5 4.2 %base.1 = (f32[768,256]{1,0:T(8,128)S(1)}, bf16[768,256]{1,0:T(8,128)(2,1)}, bf16[768,256]{1,0:T(8,128)(2,1)}, bf16[768,256]{1,0:T(8,128)(2,1)}) custom-call(s32[1]{0:T(128)} %bitcast.place_ref, bf16[768,256]{1,0:T(8,128)(2,1)} %refs_0_, bf16[768,256]{1,0:T(8,128)(2,1)S(1)} %copy-done.5, bf16[768,256]{1,0:T(8,128)(2,1)S(1)} %copy-done.7, ...), custom_call_target="tpu_custom_call" | custom-call | flops 1610612736 | bytes 6291456 | tf_op jit(solution)/shard_map/base/pallas_call | solution.py:238
  76.7 0.0 copy-start.1
  76.7 0.9 copy-done.1
  77.6 0.0 all-to-all-done.pay_ref
  77.6 0.0 collective-permute-done.6.other_hbm
  77.6 2.7 %shrink.1 = (bf16[16,64,128]{2,1,0:T(8,128)(2,1)S(1)}, f32[16,8,128]{2,1,0:T(8,128)S(1)}) custom-call(s32[1]{0:T(128)} %bitcast.1.core_ref, bf16[16,264,128]{2,1,0:T(8,128)(2,1)S(1)} %all-to-all-done.pay_ref, bf16[2048,256]{1,0:T(8,128)(2,1)S(1)} %bitcast.10, bf16[2048,256]{1,0:T(8,128)(2,1)} %collective-permute-done.6.other_hbm), custom_call_target="tpu_custom_call" | custom-call | tf_op jit(solution)/shard_map/shrink/pallas_call | solution.py:250
  80.3 12.3 %all_to_all.20.p_ref = bf16[16,64,128]{2,1,0:T(8,128)(2,1)S(1)} all-to-all(bf16[16,64,128]{2,1,0:T(8,128)(2,1)S(1)} %get-tuple-element.39), channel_id=1, replica_groups=mesh['z'=16,'core'=2,'y'=4,'x'=4] {'y','x'}, dimensions={0} | all-to-all | bytes 524288 | tf_op jit(solution)/shard_map/all_to_all | solution.py:193
  92.6 0.8 total.1
  93.3 3.5 %all-to-all-start.2 = ((bf16[16,64,128]{2,1,0:T(8,128)(2,1)}), bf16[16,64,128]{2,1,0:T(8,128)(2,1)S(1)}, u32[]{:S(2)}, u32[]{:S(2)}) async-start(bf16[16,64,128]{2,1,0:T(8,128)(2,1)} %total.1), calls=%async_computation.2 | async-start | bytes 524288 | tf_op jit(solution)/shard_map/all_to_all | solution.py:193
  96.9 0.0 collective-permute-done.7.other_hbm
  96.9 8.6 %all-to-all-done.2.s_ref = bf16[16,64,128]{2,1,0:T(8,128)(2,1)S(1)} async-done(((bf16[16,64,128]{2,1,0:T(8,128)(2,1)}), bf16[16,64,128]{2,1,0:T(8,128)(2,1)S(1)}, u32[]{:S(2)}, u32[]{:S(2)}) %all-to-all-start.2) | async-done | bytes 262176 | tf_op jit(solution)/shard_map/all_to_all | solution.py:193
  105.5 3.9 %expand.1 = bf16[16,2,64,256]{3,2,1,0:T(8,128)(2,1)} custom-call(s32[1]{0:T(128)} %bitcast.1.core_ref, bf16[16,64,128]{2,1,0:T(8,128)(2,1)S(1)} %all-to-all-done.2.s_ref, f32[16,8,128]{2,1,0:T(8,128)S(1)} %get-tuple-element.40.ids_ref, bf16[256,2048]{1,0:T(8,128)(2,1)S(1)} %bitcast.7, bf16[256,2048]{1,0:T(8,128)(2,1)} %collective-permute-done.7.other_hbm), custom_call_target="tpu_custom_call" | custom-call | tf_op jit(solution)/shard_map/expand/pallas_call | solution.py:271
  109.4 0.0 copy-start.2
  109.4 12.2 %all-to-all-start.3 = ((bf16[16,2,64,256]{3,2,1,0:T(8,128)(2,1)}), bf16[16,2,64,256]{3,2,1,0:T(8,128)(2,1)S(1)}, u32[]{:S(2)}, u32[]{:S(2)}) async-start(bf16[16,2,64,256]{3,2,1,0:T(8,128)(2,1)} %expand.1), calls=%async_computation.3 | async-start | bytes 2097152 | tf_op jit(solution)/shard_map/all_to_all | solution.py:193
  121.6 2.7 %collective-permute-start.10 = (bf16[768,256]{1,0:T(8,128)(2,1)}, bf16[768,256]{1,0:T(8,128)(2,1)S(1)}, u32[]{:S(2)}, u32[]{:S(2)}) collective-permute-start(bf16[768,256]{1,0:T(8,128)(2,1)} %get-tuple-element.45), channel_id=1, source_target_pairs={{0,12},{4,0},{8,4},{12,8},{1,13},{5,1},{9,5},{13,9},{2,14},{6,2},{... | collective-permute-start | bytes 1179656 | tf_op jit(solution)/shard_map/ppermute | solution.py:209
  124.3 3.1 %collective-permute-start.8 = (bf16[768,256]{1,0:T(8,128)(2,1)}, bf16[768,256]{1,0:T(8,128)(2,1)S(1)}, u32[]{:S(2)}, u32[]{:S(2)}) collective-permute-start(bf16[768,256]{1,0:T(8,128)(2,1)} %get-tuple-element.43), channel_id=1, source_target_pairs={{0,4},{4,8},{8,12},{12,0},{1,5},{5,9},{9,13},{13,1},{2,6},{6,10},{... | collective-permute-start | bytes 1179656 | tf_op jit(solution)/shard_map/ppermute | solution.py:209
  127.4 2.7 %collective-permute-start.9 = (bf16[768,256]{1,0:T(8,128)(2,1)}, bf16[768,256]{1,0:T(8,128)(2,1)S(1)}, u32[]{:S(2)}, u32[]{:S(2)}) collective-permute-start(bf16[768,256]{1,0:T(8,128)(2,1)} %get-tuple-element.44), channel_id=1, source_target_pairs={{0,8},{4,12},{8,0},{12,4},{1,9},{5,13},{9,1},{13,5},{2,10},{6,14},... | collective-permute-start | bytes 1179656 | tf_op jit(solution)/shard_map/ppermute | solution.py:209
  130.2 0.4 fusion.8.dest_ref
  130.6 3.2 %collective-permute-done.10.p3_hbm = bf16[768,256]{1,0:T(8,128)(2,1)S(1)} collective-permute-done((bf16[768,256]{1,0:T(8,128)(2,1)}, bf16[768,256]{1,0:T(8,128)(2,1)S(1)}, u32[]{:S(2)}, u32[]{:S(2)}) %collective-permute-start.10) | collective-permute-done | bytes 393248 | tf_op jit(solution)/shard_map/ppermute | solution.py:209
  133.7 9.7 %collective-permute-done.8.p1_hbm = bf16[768,256]{1,0:T(8,128)(2,1)S(1)} collective-permute-done((bf16[768,256]{1,0:T(8,128)(2,1)}, bf16[768,256]{1,0:T(8,128)(2,1)S(1)}, u32[]{:S(2)}, u32[]{:S(2)}) %collective-permute-start.8) | collective-permute-done | bytes 393248 | tf_op jit(solution)/shard_map/ppermute | solution.py:209
  143.5 0.0 collective-permute-done.9.p2_hbm
  143.5 25.4 %all-to-all-done.3 = bf16[16,2,64,256]{3,2,1,0:T(8,128)(2,1)S(1)} async-done(((bf16[16,2,64,256]{3,2,1,0:T(8,128)(2,1)}), bf16[16,2,64,256]{3,2,1,0:T(8,128)(2,1)S(1)}, u32[]{:S(2)}, u32[]{:S(2)}) %all-to-all-start.3) | async-done | bytes 1048608 | tf_op jit(solution)/shard_map/all_to_all | solution.py:193
  168.9 0.0 copy-done.2
  168.9 2.7 %final.1 = bf16[768,256]{1,0:T(8,128)(2,1)} custom-call(s32[768,1]{1,0:T(8,128)S(1)} %fusion.8.dest_ref, f32[768,256]{1,0:T(8,128)S(1)} %copy-done.2, bf16[768,256]{1,0:T(8,128)(2,1)S(1)} %collective-permute-done.8.p1_hbm, bf16[768,256]{1,0:T(8,128)(2,1)S(1)} %collective-permute-done.9.p2_hbm, bf16[768,256]{1,0:T(8,128)(2,1)S(1)} %collective-permute-done.10.p3_hbm, ...), custom_call_target="tpu_custom_call" | custom-call | tf_op jit(solution)/shard_map/final/pallas_call | solution.py:287
  (3 shorter events, 0.0 us)
Async XLA Ops:
  0.0 27.4 %copy-start = (bf16[32,64,256]{2,1,0:T(8,128)(2,1)S(1)}, bf16[32,64,256]{2,1,0:T(8,128)(2,1)}, u32[]{:S(2)}) copy-start(bf16[32,64,256]{2,1,0:T(8,128)(2,1)} %param.8) | copy-start | bytes 3145732
  5.7 71.9 %all-to-all-start = ((bf16[16,264,128]{2,1,0:T(8,128)(2,1)}), bf16[16,264,128]{2,1,0:T(8,128)(2,1)S(1)}, u32[]{:S(2)}, u32[]{:S(2)}) async-start(bf16[16,264,128]{2,1,0:T(8,128)(2,1)} %pack.1), calls=%async_computation | async-start | bytes 2162688 | tf_op jit(solution)/shard_map/all_to_all | solution.py:193
  20.0 21.2 %collective-permute-start = (bf16[768,256]{1,0:T(8,128)(2,1)}, bf16[768,256]{1,0:T(8,128)(2,1)S(1)}, u32[]{:S(2)}, u32[]{:S(2)}) collective-permute-start(bf16[768,256]{1,0:T(8,128)(2,1)} %refs_0_), channel_id=1, source_target_pairs={{0,3},{1,0},{2,1},{3,2},{4,7},{5,4},{6,5},{7,6},{8,11},{9,8},{10,9... | collective-permute-start | bytes 1179656 | tf_op jit(solution)/shard_map/ppermute | solution.py:209
  24.7 22.4 %collective-permute-start.1 = (bf16[768,256]{1,0:T(8,128)(2,1)}, bf16[768,256]{1,0:T(8,128)(2,1)S(1)}, u32[]{:S(2)}, u32[]{:S(2)}) collective-permute-start(bf16[768,256]{1,0:T(8,128)(2,1)} %refs_0_), channel_id=1, source_target_pairs={{0,2},{1,3},{2,0},{3,1},{4,6},{5,7},{6,4},{7,5},{8,10},{9,11},{10,... | collective-permute-start | bytes 1179656 | tf_op jit(solution)/shard_map/ppermute | solution.py:209
  27.4 50.2 %collective-permute-start.6 = (bf16[2048,256]{1,0:T(8,128)(2,1)S(1)}, bf16[2048,256]{1,0:T(8,128)(2,1)}, u32[]{:S(2)}, u32[]{:S(2)}) collective-permute-start(bf16[2048,256]{1,0:T(8,128)(2,1)S(1)} %bitcast.9), channel_id=1, source_target_pairs={{0,16},{16,0},{1,17},{17,1},{2,18},{18,2},{3,19},{19,3},{4,20},{20... | collective-permute-start | bytes 3145736 | tf_op jit(solution)/shard_map/ppermute | solution.py:197
  29.3 22.6 %collective-permute-start.2 = (bf16[768,256]{1,0:T(8,128)(2,1)}, bf16[768,256]{1,0:T(8,128)(2,1)}, u32[]{:S(2)}, u32[]{:S(2)}) collective-permute-start(bf16[768,256]{1,0:T(8,128)(2,1)} %refs_0_), channel_id=1, source_target_pairs={{0,1},{1,2},{2,3},{3,0},{4,5},{5,6},{6,7},{7,4},{8,9},{9,10},{10,1... | collective-permute-start | bytes 1179656 | tf_op jit(solution)/shard_map/ppermute | solution.py:209
  35.1 28.0 %collective-permute-start.3 = (bf16[1024,256]{1,0:T(8,128)(2,1)}, bf16[1024,256]{1,0:T(8,128)(2,1)}, u32[]{:S(2)}, u32[]{:S(2)}) collective-permute-start(bf16[1024,256]{1,0:T(8,128)(2,1)} %get-tuple-element.49), channel_id=1, source_target_pairs={{0,12},{4,0},{8,4},{12,8},{1,13},{5,1},{9,5},{13,9},{2,14},{6,2},{... | collective-permute-start | bytes 1572872 | tf_op jit(solution)/shard_map/ppermute | solution.py:209
  41.2 0.7 copy-start.4
  42.0 21.2 %collective-permute-start.4 = (bf16[1024,256]{1,0:T(8,128)(2,1)}, bf16[1024,256]{1,0:T(8,128)(2,1)}, u32[]{:S(2)}, u32[]{:S(2)}) collective-permute-start(bf16[1024,256]{1,0:T(8,128)(2,1)} %get-tuple-element.48), channel_id=1, source_target_pairs={{0,8},{4,12},{8,0},{12,4},{1,9},{5,13},{9,1},{13,5},{2,10},{6,14},... | collective-permute-start | bytes 1572872 | tf_op jit(solution)/shard_map/ppermute | solution.py:209
  47.1 0.7 copy-start.6
  47.8 21.7 %collective-permute-start.5 = (bf16[1024,256]{1,0:T(8,128)(2,1)}, bf16[1024,256]{1,0:T(8,128)(2,1)}, u32[]{:S(2)}, u32[]{:S(2)}) collective-permute-start(bf16[1024,256]{1,0:T(8,128)(2,1)} %get-tuple-element.47), channel_id=1, source_target_pairs={{0,4},{4,8},{8,12},{12,0},{1,5},{5,9},{9,13},{13,1},{2,6},{6,10},{... | collective-permute-start | bytes 1572872 | tf_op jit(solution)/shard_map/ppermute | solution.py:209
  51.9 45.0 %collective-permute-start.7 = (bf16[256,2048]{1,0:T(8,128)(2,1)S(1)}, bf16[256,2048]{1,0:T(8,128)(2,1)}, u32[]{:S(2)}, u32[]{:S(2)}) collective-permute-start(bf16[256,2048]{1,0:T(8,128)(2,1)S(1)} %bitcast.6), channel_id=1, source_target_pairs={{0,16},{16,0},{1,17},{17,1},{2,18},{18,2},{3,19},{19,3},{4,20},{20... | collective-permute-start | bytes 3145736 | tf_op jit(solution)/shard_map/ppermute | solution.py:197
  69.5 1.0 copy-start.3
  70.5 1.0 copy-start.5
  71.5 1.0 copy-start.7
  76.7 0.9 copy-start.1
  93.3 12.2 %all-to-all-start.2 = ((bf16[16,64,128]{2,1,0:T(8,128)(2,1)}), bf16[16,64,128]{2,1,0:T(8,128)(2,1)S(1)}, u32[]{:S(2)}, u32[]{:S(2)}) async-start(bf16[16,64,128]{2,1,0:T(8,128)(2,1)} %total.1), calls=%async_computation.2 | async-start | bytes 524288 | tf_op jit(solution)/shard_map/all_to_all | solution.py:193
  109.4 59.5 %copy-start.2 = (f32[768,256]{1,0:T(8,128)S(1)}, f32[768,256]{1,0:T(8,128)}, u32[]{:S(2)}) copy-start(f32[768,256]{1,0:T(8,128)} %copy-done.1) | copy-start | bytes 2359300
  109.4 59.5 %all-to-all-start.3 = ((bf16[16,2,64,256]{3,2,1,0:T(8,128)(2,1)}), bf16[16,2,64,256]{3,2,1,0:T(8,128)(2,1)S(1)}, u32[]{:S(2)}, u32[]{:S(2)}) async-start(bf16[16,2,64,256]{3,2,1,0:T(8,128)(2,1)} %expand.1), calls=%async_computation.3 | async-start | bytes 2097152 | tf_op jit(solution)/shard_map/all_to_all | solution.py:193
  121.6 12.2 %collective-permute-start.10 = (bf16[768,256]{1,0:T(8,128)(2,1)}, bf16[768,256]{1,0:T(8,128)(2,1)S(1)}, u32[]{:S(2)}, u32[]{:S(2)}) collective-permute-start(bf16[768,256]{1,0:T(8,128)(2,1)} %get-tuple-element.45), channel_id=1, source_target_pairs={{0,12},{4,0},{8,4},{12,8},{1,13},{5,1},{9,5},{13,9},{2,14},{6,2},{... | collective-permute-start | bytes 1179656 | tf_op jit(solution)/shard_map/ppermute | solution.py:209
  124.3 19.1 %collective-permute-start.8 = (bf16[768,256]{1,0:T(8,128)(2,1)}, bf16[768,256]{1,0:T(8,128)(2,1)S(1)}, u32[]{:S(2)}, u32[]{:S(2)}) collective-permute-start(bf16[768,256]{1,0:T(8,128)(2,1)} %get-tuple-element.43), channel_id=1, source_target_pairs={{0,4},{4,8},{8,12},{12,0},{1,5},{5,9},{9,13},{13,1},{2,6},{6,10},{... | collective-permute-start | bytes 1179656 | tf_op jit(solution)/shard_map/ppermute | solution.py:209
  127.4 16.0 %collective-permute-start.9 = (bf16[768,256]{1,0:T(8,128)(2,1)}, bf16[768,256]{1,0:T(8,128)(2,1)S(1)}, u32[]{:S(2)}, u32[]{:S(2)}) collective-permute-start(bf16[768,256]{1,0:T(8,128)(2,1)} %get-tuple-element.44), channel_id=1, source_target_pairs={{0,8},{4,12},{8,0},{12,4},{1,9},{5,13},{9,1},{13,5},{2,10},{6,14},... | collective-permute-start | bytes 1179656 | tf_op jit(solution)/shard_map/ppermute | solution.py:209

commit v4 on v3

--- a/solution.py
+++ b/solution.py
@@ -33,21 +33,40 @@
     return [pl.BlockSpec(memory_space=pltpu.VMEM)] * n
 
 
-def pack_kernel(dest_ref, local_ref, tokens_hbm, out_ref, tokens_ref, sem):
+def across(row):
+    return jnp.broadcast_to(row, (128, ROWS)).T[:, 0:1]
+
+
+def pack_kernel(index_ref, slot_ref, tokens_hbm, pay_hbm, dest_ref, tokens_ref, pay_ref, sem, out_sem):
     bring = pltpu.make_async_copy(tokens_hbm, tokens_ref, sem.at[0])
     bring.start()
-    dest = dest_ref[...]
-    local = local_ref[...]
-    line = lax.broadcasted_iota(I32, (8 * CHIPS, ROWS), 0)
-    to = (line // 4 == dest // PAIR).astype(F32).astype(BF)
-    lane_slot = (lax.broadcasted_iota(I32, (128, ROWS), 0) % PAIR) // RPA
-    slot = (dest % PAIR) // RPA
-    first = dest % RPA == 0
-    value = jnp.where((lane_slot == slot) & first, local.astype(F32), 0.0).astype(BF)
+    adapters = slot_ref.shape[1]
+    table = slot_ref[...]
+    line = lax.broadcasted_iota(I32, (8, adapters), 0)
+    table = jnp.where(line == 0, table >> 5, table & 31).astype(F32).astype(BF)
+    named = lax.broadcasted_iota(I32, (adapters, ROWS), 0) == index_ref[...]
+    found = jnp.dot(table, named.astype(F32).astype(BF), preferred_element_type=F32)
+    holder, local = found[0:1], found[1:2]
+    pool_row = holder * HELD + local
+    pool_col = across(pool_row)
+    shape = (ROWS, ROWS)
+    before = lax.broadcasted_iota(I32, shape, 0) < lax.broadcasted_iota(I32, shape, 1)
+    same = (pool_col == pool_row) & before
+    place = jnp.sum(same.astype(F32), axis=0, keepdims=True)
+    first_col = jnp.where(across(place) == 0, pool_col, -1.0)
+    lower = (first_col >= holder * HELD) & (first_col < pool_row)
+    rank = jnp.sum(lower.astype(F32), axis=0, keepdims=True)
+    dest = ((holder * SLOTS + rank) * RPA + place).astype(I32)
+    dest_ref[...] = dest
+    line = lax.broadcasted_iota(I32, (8 * CHIPS, ROWS), 0) >> 2
+    to = (line == holder.astype(I32)).astype(F32).astype(BF)
+    lane_slot = (lax.broadcasted_iota(I32, (128, ROWS), 0) & (PAIR - 1)) >> 4
+    value = jnp.where((lane_slot == rank.astype(I32)) & (place == 0), local, 0.0).astype(BF)
     ids = lax.dot_general(to, value, NT, preferred_element_type=F32)
     for z in range(CHIPS):
-        out_ref[z, 256:264, :] = ids[8 * z : 8 * z + 8, :].astype(BF)
+        pay_ref[z, 256:264, :] = ids[8 * z : 8 * z + 8, :].astype(BF)
     bring.wait()
+    sends = []
     for b in range(8):
         at = lax.broadcasted_iota(I32, (256, ROWS), 0) + b * 256
         pick = (at == dest).astype(F32).astype(BF)
@@ -55,8 +74,13 @@
         for j in range(2):
             for c in range(2):
                 at = 128 * j + 64 * c
-                out_ref[2 * b + j, 128 * c : 128 * c + 64, :] = rows[at : at + 64, 0:128]
-                out_ref[2 * b + j, 128 * c + 64 : 128 * c + 128, :] = rows[at : at + 64, 128:256]
+                pay_ref[2 * b + j, 128 * c : 128 * c + 64, :] = rows[at : at + 64, 0:128]
+                pay_ref[2 * b + j, 128 * c + 64 : 128 * c + 128, :] = rows[at : at + 64, 128:256]
+        two = pl.ds(2 * b, 2)
+        sends.append(pltpu.make_async_copy(pay_ref.at[two], pay_hbm.at[two], out_sem.at[b]))
+        sends[-1].start()
+    for send in sends:
+        send.wait()
 
 
 def shrink_kernel(core_ref, pay_ref, own_hbm, other_hbm, out_ref, ids_ref, pools, sem):
@@ -108,7 +132,14 @@
         out_ref[t] = mine
 
 
-def expand_kernel(core_ref, s_ref, ids_ref, own_hbm, other_hbm, out_ref, m_ref, pools, sem):
+def marks_kernel(ids_ref, pool_hbm, out_ref):
+    high = (lax.broadcasted_iota(I32, (128, 128), 1) >= RANK).astype(F32)
+    for t in range(TENSOR):
+        column = jnp.broadcast_to(ids_ref[t][0:1], (128, 128)).T
+        out_ref[t] = (column - high).astype(BF)
+
+
+def expand_kernel(core_ref, s_ref, marks_ref, own_hbm, other_hbm, out_hbm, m_ref, pools, rows_ref, sem, out_sem):
     core = core_ref[0]
     brings = [
         pltpu.make_async_copy(pool, pools.at[i], sem.at[i])
@@ -116,22 +147,31 @@
     ]
     for bring in brings:
         bring.start()
+    sends = []
     for i, c in enumerate((core, 1 - core)):
-        for b in range(4):
-            at = 8 * c + 2 * b
-            s = jnp.concatenate([s_ref[at], s_ref[at + 1]], axis=1)
-            mark = jnp.concatenate([ids_ref[at][0:1], ids_ref[at + 1][0:1]], axis=1)
-            mark = jnp.broadcast_to(mark, (RANK, 256)).astype(BF)
-            for a in range(HELD):
-                m_ref[b % 2, 64 * a : 64 * a + 64, :] = jnp.where(
-                    mark == jnp.asarray(a, BF), s, jnp.zeros_like(s)
+        for h in range(2):
+            for k in range(4):
+                at = 8 * c + 4 * h + k
+                s = s_ref[at].astype(F32)
+                s = jnp.concatenate([s, s], axis=0).T.astype(BF)
+                mark = marks_ref[at]
+                for j in range(HELD // 2):
+                    m_ref[h, 128 * k : 128 * k + 128, 128 * j : 128 * j + 128] = jnp.where(
+                        mark == jnp.asarray(2 * j, BF), s, jnp.zeros_like(s)
+                    )
+            if h == 0:
+                brings[i].wait()
+            e = jnp.dot(m_ref[h], pools[i], preferred_element_type=F32)
+            rows_ref[i, 8 * h : 8 * h + 8] = e.astype(BF).reshape(8, PAIR, WIDTH)
+            part = pl.ds(8 * h, 8)
+            sends.append(
+                pltpu.make_async_copy(
+                    rows_ref.at[i, part], out_hbm.at[part, c], out_sem.at[2 * i + h]
                 )
-            if b == 0:
-                brings[i].wait()
-            et = jnp.dot(pools[i], m_ref[b % 2], preferred_element_type=F32)
-            rows = et.T.astype(BF)
-            for j in range(4):
-                out_ref[4 * b + j, c] = rows[64 * j : 64 * j + 64]
+            )
+            sends[-1].start()
+    for send in sends:
+        send.wait()
 
 
 def base_kernel(place_ref, *refs):
@@ -151,42 +191,20 @@
             outs[s][at : at + 384, :] = total.astype(outs[s].dtype)
 
 
-def final_kernel(dest_ref, p0_hbm, p1_hbm, p2_hbm, p3_hbm, back_ref, out_ref, p0, pn, sem):
-    brings = [pltpu.make_async_copy(p0_hbm, p0, sem.at[3])]
-    for i, part in enumerate((p1_hbm, p2_hbm, p3_hbm)):
-        brings.append(pltpu.make_async_copy(part, pn.at[i], sem.at[i]))
-    for bring in brings:
-        bring.start()
+def ready_kernel(p0_ref, p1_ref, p2_ref, p3_ref, base_ref):
+    base = p0_ref[...]
+    for part_ref in (p1_ref, p2_ref, p3_ref):
+        base = base + part_ref[...].astype(F32)
+    base_ref[...] = base
+
+
+def final_kernel(dest_ref, base_ref, back_ref, out_ref):
     for b in range(3):
         lo = 256 * b
         at = lax.broadcasted_iota(I32, (256, BUCKETS), 1)
         pick = (at == dest_ref[lo : lo + 256, :]).astype(F32).astype(BF)
         rows = jnp.dot(pick, back_ref[...], preferred_element_type=F32)
-        if b == 0:
-            for bring in brings:
-                bring.wait()
-        base = p0[lo : lo + 256, :]
-        for i in range(3):
-            base = base + pn[i, lo : lo + 256, :].astype(F32)
-        out_ref[lo : lo + 256, :] = (base + SCALE * rows).astype(BF)
-
-
-def route(row_adapter_index, adapter_pool_slot):
-    table_ids = jnp.arange(adapter_pool_slot.shape[0], dtype=I32)
-    pool_row = jnp.sum(
-        jnp.where(row_adapter_index[:, None] == table_ids[None, :], adapter_pool_slot[None, :], 0),
-        axis=1,
-    )
-    holder = pool_row // HELD
-    order = jnp.arange(ROWS, dtype=I32)
-    same = pool_row[:, None] == pool_row[None, :]
-    place = jnp.sum(same & (order[None, :] < order[:, None]), axis=1)
-    first = place == 0
-    same_holder = holder[:, None] == holder[None, :]
-    rank = jnp.sum(
-        first[None, :] & same_holder & (pool_row[None, :] < pool_row[:, None]), axis=1
-    )
-    return (holder * SLOTS + rank) * RPA + place, pool_row % HELD
+        out_ref[lo : lo + 256, :] = (base_ref[lo : lo + 256, :] + SCALE * rows).astype(BF)
 
 
 def exchange(x, axis):
@@ -213,21 +231,28 @@
     tensor = ("y", "x")
     y = lax.axis_index("y")
     core = lax.axis_index("core").astype(I32).reshape(1)
-    dest, local = route(row_adapter_index, adapter_pool_slot)
-    payload = pl.pallas_call(
+    payload, dest = pl.pallas_call(
         pack_kernel,
-        out_shape=jax.ShapeDtypeStruct((CHIPS, PAY, 128), BF),
+        out_shape=(
+            jax.ShapeDtypeStruct((CHIPS, PAY, 128), BF),
+            jax.ShapeDtypeStruct((1, ROWS), I32),
+        ),
         in_specs=vmem(2) + hbm(1),
-        out_specs=pl.BlockSpec(memory_space=pltpu.VMEM),
-        scratch_shapes=[pltpu.VMEM((ROWS, WIDTH), BF), pltpu.SemaphoreType.DMA((1,))],
+        out_specs=tuple(hbm(1) + vmem(1)),
+        scratch_shapes=[
+            pltpu.VMEM((ROWS, WIDTH), BF),
+            pltpu.VMEM((CHIPS, PAY, 128), BF),
+            pltpu.SemaphoreType.DMA((1,)),
+            pltpu.SemaphoreType.DMA((8,)),
+        ],
         compiler_params=params(),
         name="pack",
-    )(dest.reshape(1, ROWS), local.reshape(1, ROWS), tokens)
+    )(row_adapter_index.reshape(1, ROWS), adapter_pool_slot.reshape(1, -1), tokens)
     tokens, weight, a_pool, b_pool, payload = lax.optimization_barrier(
         (tokens, weight, a_pool, b_pool, payload)
     )
     a_own = a_pool.reshape(HELD * RANK, WIDTH)
-    b_own = b_pool.reshape(HELD * RANK, WIDTH).T
+    b_own = b_pool.reshape(HELD * RANK, WIDTH)
     a_other, b_other = sibling(a_own), sibling(b_own)
     arrived = exchange(payload, "z")
     xs = [tokens] + [turn(tokens, "x", -d) for d in range(1, 4)]
@@ -246,7 +271,6 @@
         ),
         name="base",
     )(lax.axis_index("x").astype(I32).reshape(1), *xs, *ws)
-    arrived, *parts = lax.optimization_barrier((arrived, *parts))
     partial, ids = pl.pallas_call(
         shrink_kernel,
         out_shape=(
@@ -268,35 +292,48 @@
         name="total",
     )(exchange(partial, tensor))
     shrunk = exchange(summed, tensor)
+    marks = pl.pallas_call(
+        marks_kernel,
+        out_shape=jax.ShapeDtypeStruct((TENSOR, 128, 128), BF),
+        in_specs=vmem(1) + hbm(1),
+        out_specs=pl.BlockSpec(memory_space=pltpu.VMEM),
+        compiler_params=params(),
+        name="marks",
+    )(ids, b_own)
     expanded = pl.pallas_call(
         expand_kernel,
         out_shape=jax.ShapeDtypeStruct((CHIPS, 2, PAIR, WIDTH), BF),
         in_specs=[scalar()] + vmem(2) + hbm(2),
-        out_specs=pl.BlockSpec(memory_space=pltpu.VMEM),
+        out_specs=pl.BlockSpec(memory_space=pltpu.HBM),
         scratch_shapes=[
-            pltpu.VMEM((2, HELD * RANK, 256), BF),
-            pltpu.VMEM((2, WIDTH, HELD * RANK), BF),
+            pltpu.VMEM((2, 512, HELD * RANK), BF),
+            pltpu.VMEM((2, HELD * RANK, WIDTH), BF),
+            pltpu.VMEM((2, CHIPS, PAIR, WIDTH), BF),
             pltpu.SemaphoreType.DMA((2,)),
+            pltpu.SemaphoreType.DMA((4,)),
         ],
         compiler_params=params(),
         name="expand",
-    )(core, shrunk, ids, b_own, b_other)
+    )(core, shrunk, marks, b_own, b_other)
     p0, p1, p2, p3, expanded = lax.optimization_barrier((*parts, expanded))
     back = exchange(expanded, "z").reshape(BUCKETS, WIDTH)
     sums = [turn(p, "y", s) for s, p in ((1, p1), (2, p2), (3, p3))]
+    base = pl.pallas_call(
+        ready_kernel,
+        out_shape=jax.ShapeDtypeStruct((ROWS, WIDTH), F32),
+        in_specs=vmem(4),
+        out_specs=pl.BlockSpec(memory_space=pltpu.VMEM),
+        compiler_params=params(),
+        name="ready",
+    )(p0, *sums)
     return pl.pallas_call(
         final_kernel,
         out_shape=jax.ShapeDtypeStruct((ROWS, WIDTH), BF),
-        in_specs=vmem(1) + hbm(4) + vmem(1),
+        in_specs=vmem(3),
         out_specs=pl.BlockSpec(memory_space=pltpu.VMEM),
-        scratch_shapes=[
-            pltpu.VMEM((ROWS, WIDTH), F32),
-            pltpu.VMEM((3, ROWS, WIDTH), BF),
-            pltpu.SemaphoreType.DMA((4,)),
-        ],
         compiler_params=params(),
         name="final",
-    )(dest.reshape(ROWS, 1), p0, *sums, back)
+    )(dest.reshape(ROWS, 1), base, back)
 
 
 def solution(mesh):

time: 173 us -> 166 us (0.960)
  the two profiles are of different devices: /device:TPU:96 before, /device:TPU:32 now
where the time goes in v4:
time: 166 us; the launch traced here: 165 us
  starting transfers between devices  61.8 us (37%)
  waiting for transfers between devices  59.4 us (36%)
  Pallas kernels  18.7 us (11%)
  blocking collectives  15.5 us (9%)
  local copies, waits for them, and re-layouts  9.14 us (6%)
    all_to_all x3, waiting for transfers between devices, exchange(): return lax.all_to_all(x, axis, split_axis=0, concat_axis=0, tiled=True)  40.3 us
    ppermute x9, starting transfers between devices, turn(): return lax.ppermute(x, axis, [(i, (i + step) % 4) for i in range(4)])  30.5 us
    all_to_all x3, starting transfers between devices, exchange(): return lax.all_to_all(x, axis, split_axis=0, concat_axis=0, tiled=True)  27.5 us
    ppermute x9, waiting for transfers between devices, turn(): return lax.ppermute(x, axis, [(i, (i + step) % 4) for i in range(4)])  19.1 us
    all_to_all x1, blocking collectives, exchange(): return lax.all_to_all(x, axis, split_axis=0, concat_axis=0, tiled=True)  15.5 us
    unnamed x16, local copies, waits for them, and re-layouts  5.2 us
    pallas_call x1, Pallas kernels, body(): pl.pallas_call(expand_kernel, out_shape=jax.ShapeDtypeStruct((CHIPS, 2, P...  4.73 us
    pallas_call x1, Pallas kernels, body(): pl.pallas_call(base_kernel, out_shape=tuple((jax.ShapeDtypeStruct((ROWS,...  4.39 us
  transfers between devices with their start and end apart: 14, of which 6 were waited for; matrix products, arithmetic and copies ran while one was open for 2% of the time, Pallas kernels for 5%

profile of v4, /device:TPU:32, one launch (start us, length us, event | category | flops | bytes accessed | tf_op | source)
XLA Modules:
  0.0 164.9 jit_solution(5459716178551491268)
XLA Ops:
  0.0 0.0 copy-start.1
  0.0 0.0 copy-start
  0.0 0.8 reshape.24.index_ref
  0.8 0.0 copy-start.7
  0.8 0.7 copy-done.7
  1.5 3.9 %pack.1 = (bf16[16,264,128]{2,1,0:T(8,128)(2,1)}, s32[1,768]{1,0:T(1,128)S(1)}) custom-call(s32[1,768]{1,0:T(1,128)S(1)} %reshape.24.index_ref, s32[1,1024]{1,0:T(1,128)S(1)} %bitcast.13, bf16[768,256]{1,0:T(8,128)(2,1)} %refs_0_), custom_call_target="tpu_custom_call" | custom-call | tf_op jit(solution)/shard_map/pack/pallas_call | solution.py:234
  5.5 15.2 %all-to-all-start = ((bf16[16,264,128]{2,1,0:T(8,128)(2,1)}), bf16[16,264,128]{2,1,0:T(8,128)(2,1)S(1)}, u32[]{:S(2)}, u32[]{:S(2)}) async-start(bf16[16,264,128]{2,1,0:T(8,128)(2,1)} %get-tuple-element.31), calls=%async_computation | async-start | bytes 2162688 | tf_op jit(solution)/shard_map/all_to_all | solution.py:211
  20.7 0.0 copy-done.1
  20.7 1.9 %collective-permute-start.6 = (bf16[2048,256]{1,0:T(8,128)(2,1)S(1)}, bf16[2048,256]{1,0:T(8,128)(2,1)}, u32[]{:S(2)}, u32[]{:S(2)}) collective-permute-start(bf16[2048,256]{1,0:T(8,128)(2,1)S(1)} %bitcast.11), channel_id=1, source_target_pairs={{0,16},{16,0},{1,17},{17,1},{2,18},{18,2},{3,19},{19,3},{4,20},{20... | collective-permute-start | bytes 3145736 | tf_op jit(solution)/shard_map/ppermute | solution.py:215
  22.6 4.7 %collective-permute-start = (bf16[768,256]{1,0:T(8,128)(2,1)}, bf16[768,256]{1,0:T(8,128)(2,1)}, u32[]{:S(2)}, u32[]{:S(2)}) collective-permute-start(bf16[768,256]{1,0:T(8,128)(2,1)} %refs_0_), channel_id=1, source_target_pairs={{0,3},{1,0},{2,1},{3,2},{4,7},{5,4},{6,5},{7,6},{8,11},{9,8},{10,9... | collective-permute-start | bytes 1179656 | tf_op jit(solution)/shard_map/ppermute | solution.py:227
  27.3 2.7 %collective-permute-start.1 = (bf16[768,256]{1,0:T(8,128)(2,1)}, bf16[768,256]{1,0:T(8,128)(2,1)}, u32[]{:S(2)}, u32[]{:S(2)}) collective-permute-start(bf16[768,256]{1,0:T(8,128)(2,1)} %refs_0_), channel_id=1, source_target_pairs={{0,2},{1,3},{2,0},{3,1},{4,6},{5,7},{6,4},{7,5},{8,10},{9,11},{10,... | collective-permute-start | bytes 1179656 | tf_op jit(solution)/shard_map/ppermute | solution.py:227
  30.0 0.0 copy-done
  30.0 1.9 %collective-permute-start.7 = (bf16[2048,256]{1,0:T(8,128)(2,1)S(1)}, bf16[2048,256]{1,0:T(8,128)(2,1)}, u32[]{:S(2)}, u32[]{:S(2)}) collective-permute-start(bf16[2048,256]{1,0:T(8,128)(2,1)S(1)} %bitcast.8), channel_id=1, source_target_pairs={{0,16},{16,0},{1,17},{17,1},{2,18},{18,2},{3,19},{19,3},{4,20},{20... | collective-permute-start | bytes 3145736 | tf_op jit(solution)/shard_map/ppermute | solution.py:215
  32.0 2.9 %constant_dynamic-slice_fusion = (bf16[1024,256]{1,0:T(8,128)(2,1)}, bf16[1024,256]{1,0:T(8,128)(2,1)}, bf16[1024,256]{1,0:T(8,128)(2,1)}, bf16[1024,256]{1,0:T(8,128)(2,1)}) fusion(bf16[4096,256]{1,0:T(8,128)(2,1)} %param.7, s32[]{:T(128)S(6)} %select_n.38, s32[]{:T(128)S(6)} %select_n.36, s32[]{:T(128)S(6)} %select_n.34, s32[]{:T(128)S(6)} %select_n.32), kind=kLoop, calls=%fused_computation | loop fusion | bytes 4194320 | tf_op jit(solution)/shard_map/dynamic_slice | solution.py:261
  34.9 4.9 %collective-permute-start.3 = (bf16[1024,256]{1,0:T(8,128)(2,1)}, bf16[1024,256]{1,0:T(8,128)(2,1)}, u32[]{:S(2)}, u32[]{:S(2)}) collective-permute-start(bf16[1024,256]{1,0:T(8,128)(2,1)} %get-tuple-element.43), channel_id=1, source_target_pairs={{0,12},{4,0},{8,4},{12,8},{1,13},{5,1},{9,5},{13,9},{2,14},{6,2},{... | collective-permute-start | bytes 1572872 | tf_op jit(solution)/shard_map/ppermute | solution.py:227
  39.9 5.2 %collective-permute-done.refs_1_ = bf16[768,256]{1,0:T(8,128)(2,1)} collective-permute-done((bf16[768,256]{1,0:T(8,128)(2,1)}, bf16[768,256]{1,0:T(8,128)(2,1)}, u32[]{:S(2)}, u32[]{:S(2)}) %collective-permute-start) | collective-permute-done | bytes 393248 | tf_op jit(solution)/shard_map/ppermute | solution.py:227
  45.1 5.1 %collective-permute-start.4 = (bf16[1024,256]{1,0:T(8,128)(2,1)}, bf16[1024,256]{1,0:T(8,128)(2,1)}, u32[]{:S(2)}, u32[]{:S(2)}) collective-permute-start(bf16[1024,256]{1,0:T(8,128)(2,1)} %get-tuple-element.42), channel_id=1, source_target_pairs={{0,8},{4,12},{8,0},{12,4},{1,9},{5,13},{9,1},{13,5},{2,10},{6,14},... | collective-permute-start | bytes 1572872 | tf_op jit(solution)/shard_map/ppermute | solution.py:227
  50.2 0.0 collective-permute-done.1.refs_2_
  50.2 2.6 %collective-permute-start.5 = (bf16[1024,256]{1,0:T(8,128)(2,1)}, bf16[1024,256]{1,0:T(8,128)(2,1)}, u32[]{:S(2)}, u32[]{:S(2)}) collective-permute-start(bf16[1024,256]{1,0:T(8,128)(2,1)} %get-tuple-element.41), channel_id=1, source_target_pairs={{0,4},{4,8},{8,12},{12,0},{1,5},{5,9},{9,13},{13,1},{2,6},{6,10},{... | collective-permute-start | bytes 1572872 | tf_op jit(solution)/shard_map/ppermute | solution.py:227
  52.8 0.0 collective-permute-done.6.other_hbm
  52.8 1.9 %collective-permute-start.2 = (bf16[768,256]{1,0:T(8,128)(2,1)}, bf16[768,256]{1,0:T(8,128)(2,1)}, u32[]{:S(2)}, u32[]{:S(2)}) collective-permute-start(bf16[768,256]{1,0:T(8,128)(2,1)} %refs_0_), channel_id=1, source_target_pairs={{0,1},{1,2},{2,3},{3,0},{4,5},{5,6},{6,7},{7,4},{8,9},{9,10},{10,1... | collective-permute-start | bytes 1179656 | tf_op jit(solution)/shard_map/ppermute | solution.py:227
  54.7 16.7 %all-to-all-done.pay_ref = bf16[16,264,128]{2,1,0:T(8,128)(2,1)S(1)} async-done(((bf16[16,264,128]{2,1,0:T(8,128)(2,1)}), bf16[16,264,128]{2,1,0:T(8,128)(2,1)S(1)}, u32[]{:S(2)}, u32[]{:S(2)}) %all-to-all-start) | async-done | bytes 1081376 | tf_op jit(solution)/shard_map/all_to_all | solution.py:211
  71.4 2.7 %shrink.1 = (bf16[16,64,128]{2,1,0:T(8,128)(2,1)S(1)}, f32[16,8,128]{2,1,0:T(8,128)S(1)}) custom-call(s32[1]{0:T(128)} %bitcast.3.core_ref, bf16[16,264,128]{2,1,0:T(8,128)(2,1)S(1)} %all-to-all-done.pay_ref, bf16[2048,256]{1,0:T(8,128)(2,1)S(1)} %bitcast.12, bf16[2048,256]{1,0:T(8,128)(2,1)} %collective-permute-done.6.other_hbm), custom_call_target="tpu_custom_call" | custom-call | tf_op jit(solution)/shard_map/shrink/pallas_call | solution.py:274
  74.1 15.5 %all_to_all.20.p_ref = bf16[16,64,128]{2,1,0:T(8,128)(2,1)S(1)} all-to-all(bf16[16,64,128]{2,1,0:T(8,128)(2,1)S(1)} %get-tuple-element.33), channel_id=1, replica_groups=mesh['z'=16,'core'=2,'y'=4,'x'=4] {'y','x'}, dimensions={0} | all-to-all | bytes 524288 | tf_op jit(solution)/shard_map/all_to_all | solution.py:211
  89.6 0.8 total.1
  90.4 3.5 %all-to-all-start.2 = ((bf16[16,64,128]{2,1,0:T(8,128)(2,1)}), bf16[16,64,128]{2,1,0:T(8,128)(2,1)S(1)}, u32[]{:S(2)}, u32[]{:S(2)}) async-start(bf16[16,64,128]{2,1,0:T(8,128)(2,1)} %total.1), calls=%async_computation.2 | async-start | bytes 524288 | tf_op jit(solution)/shard_map/all_to_all | solution.py:211
  93.9 0.0 collective-permute-done.2.refs_3_
  93.9 0.0 collective-permute-done.3.refs_5_
  93.9 0.0 collective-permute-done.4.refs_6_
  93.9 0.0 collective-permute-done.5.refs_7_
  94.0 0.0 copy-start.2
  94.0 1.0 copy-done.2
  95.0 4.4 %base.1 = (f32[768,256]{1,0:T(8,128)S(1)}, bf16[768,256]{1,0:T(8,128)(2,1)}, bf16[768,256]{1,0:T(8,128)(2,1)}, bf16[768,256]{1,0:T(8,128)(2,1)}) custom-call(s32[1]{0:T(128)} %bitcast.2.place_ref, bf16[768,256]{1,0:T(8,128)(2,1)} %refs_0_, bf16[768,256]{1,0:T(8,128)(2,1)} %collective-permute-done.refs_1_, bf16[768,256]{1,0:T(8,128)(2,1)} %collective-permute-done.1.refs_2_, ...), custom_call_target="tpu_custom_call" | custom-call | flops 1610612736 | bytes 6291456 | tf_op jit(solution)/shard_map/base/pallas_call | solution.py:263
  99.4 0.3 marks.1.marks_ref
  99.7 0.0 collective-permute-done.7.other_hbm
  99.7 2.8 %all-to-all-done.2.s_ref = bf16[16,64,128]{2,1,0:T(8,128)(2,1)S(1)} async-done(((bf16[16,64,128]{2,1,0:T(8,128)(2,1)}), bf16[16,64,128]{2,1,0:T(8,128)(2,1)S(1)}, u32[]{:S(2)}, u32[]{:S(2)}) %all-to-all-start.2) | async-done | bytes 262176 | tf_op jit(solution)/shard_map/all_to_all | solution.py:211
  102.6 4.7 %expand.1 = bf16[16,2,64,256]{3,2,1,0:T(8,128)(2,1)} custom-call(s32[1]{0:T(128)} %bitcast.3.core_ref, bf16[16,64,128]{2,1,0:T(8,128)(2,1)S(1)} %all-to-all-done.2.s_ref, bf16[16,128,128]{2,1,0:T(8,128)(2,1)S(1)} %marks.1.marks_ref, bf16[2048,256]{1,0:T(8,128)(2,1)S(1)} %bitcast.10, bf16[2048,256]{1,0:T(8,128)(2,1)} %collective-permute-done.7.other_hbm), custom_call_target="tpu_custom_call" | custom-call | tf_op jit(solution)/shard_map/expand/pallas_call | solution.py:303
  107.3 8.7 %all-to-all-start.3 = ((bf16[16,2,64,256]{3,2,1,0:T(8,128)(2,1)}), bf16[16,2,64,256]{3,2,1,0:T(8,128)(2,1)S(1)}, u32[]{:S(2)}, u32[]{:S(2)}) async-start(bf16[16,2,64,256]{3,2,1,0:T(8,128)(2,1)} %expand.1), calls=%async_computation.3 | async-start | bytes 2097152 | tf_op jit(solution)/shard_map/all_to_all | solution.py:211
  116.0 2.7 %collective-permute-start.10 = (bf16[768,256]{1,0:T(8,128)(2,1)}, bf16[768,256]{1,0:T(8,128)(2,1)S(1)}, u32[]{:S(2)}, u32[]{:S(2)}) collective-permute-start(bf16[768,256]{1,0:T(8,128)(2,1)} %get-tuple-element.39), channel_id=1, source_target_pairs={{0,12},{4,0},{8,4},{12,8},{1,13},{5,1},{9,5},{13,9},{2,14},{6,2},{... | collective-permute-start | bytes 1179656 | tf_op jit(solution)/shard_map/ppermute | solution.py:227
  118.8 3.1 %collective-permute-start.8 = (bf16[768,256]{1,0:T(8,128)(2,1)}, bf16[768,256]{1,0:T(8,128)(2,1)S(1)}, u32[]{:S(2)}, u32[]{:S(2)}) collective-permute-start(bf16[768,256]{1,0:T(8,128)(2,1)} %get-tuple-element.37), channel_id=1, source_target_pairs={{0,4},{4,8},{8,12},{12,0},{1,5},{5,9},{9,13},{13,1},{2,6},{6,10},{... | collective-permute-start | bytes 1179656 | tf_op jit(solution)/shard_map/ppermute | solution.py:227
  121.9 2.7 %collective-permute-start.9 = (bf16[768,256]{1,0:T(8,128)(2,1)}, bf16[768,256]{1,0:T(8,128)(2,1)S(1)}, u32[]{:S(2)}, u32[]{:S(2)}) collective-permute-start(bf16[768,256]{1,0:T(8,128)(2,1)} %get-tuple-element.38), channel_id=1, source_target_pairs={{0,8},{4,12},{8,0},{12,4},{1,9},{5,13},{9,1},{13,5},{2,10},{6,14},... | collective-permute-start | bytes 1179656 | tf_op jit(solution)/shard_map/ppermute | solution.py:227
  124.6 0.2 copy.7.dest_ref
  124.8 3.5 %collective-permute-done.10.p3_ref = bf16[768,256]{1,0:T(8,128)(2,1)S(1)} collective-permute-done((bf16[768,256]{1,0:T(8,128)(2,1)}, bf16[768,256]{1,0:T(8,128)(2,1)S(1)}, u32[]{:S(2)}, u32[]{:S(2)}) %collective-permute-start.10) | collective-permute-done | bytes 393248 | tf_op jit(solution)/shard_map/ppermute | solution.py:227
  128.3 10.4 %collective-permute-done.8.p1_ref = bf16[768,256]{1,0:T(8,128)(2,1)S(1)} collective-permute-done((bf16[768,256]{1,0:T(8,128)(2,1)}, bf16[768,256]{1,0:T(8,128)(2,1)S(1)}, u32[]{:S(2)}, u32[]{:S(2)}) %collective-permute-start.8) | collective-permute-done | bytes 393248 | tf_op jit(solution)/shard_map/ppermute | solution.py:227
  138.7 0.0 copy-start.3
  138.7 0.7 copy-done.3
  139.4 0.0 collective-permute-done.9.p2_ref
  139.4 0.0 copy-start.5
  139.4 0.7 copy-done.5
  140.2 0.0 copy-start.4
  140.2 1.0 copy-done.4
  141.2 0.0 copy-start.6
  141.2 1.0 copy-done.6
  142.2 0.2 ready.1.base_ref
  142.3 20.8 %all-to-all-done.3 = bf16[16,2,64,256]{3,2,1,0:T(8,128)(2,1)S(1)} async-done(((bf16[16,2,64,256]{3,2,1,0:T(8,128)(2,1)}), bf16[16,2,64,256]{3,2,1,0:T(8,128)(2,1)S(1)}, u32[]{:S(2)}, u32[]{:S(2)}) %all-to-all-start.3) | async-done | bytes 1048608 | tf_op jit(solution)/shard_map/all_to_all | solution.py:211
  163.1 1.8 %final.1 = bf16[768,256]{1,0:T(8,128)(2,1)} custom-call(s32[768,1]{1,0:T(8,128)S(1)} %copy.7.dest_ref, f32[768,256]{1,0:T(8,128)S(1)} %ready.1.base_ref, bf16[2048,256]{1,0:T(8,128)(2,1)S(1)} %bitcast.7), custom_call_target="tpu_custom_call" | custom-call | tf_op jit(solution)/shard_map/final/pallas_call | solution.py:329
Async XLA Ops:
  0.0 20.7 %copy-start.1 = (bf16[32,64,256]{2,1,0:T(8,128)(2,1)S(1)}, bf16[32,64,256]{2,1,0:T(8,128)(2,1)}, u32[]{:S(2)}) copy-start(bf16[32,64,256]{2,1,0:T(8,128)(2,1)} %param.8) | copy-start | bytes 3145732
  0.0 30.0 %copy-start = (bf16[32,64,256]{2,1,0:T(8,128)(2,1)S(1)}, bf16[32,64,256]{2,1,0:T(8,128)(2,1)}, u32[]{:S(2)}) copy-start(bf16[32,64,256]{2,1,0:T(8,128)(2,1)} %param.9) | copy-start | bytes 3145732
  0.8 0.7 copy-start.7
  5.5 65.9 %all-to-all-start = ((bf16[16,264,128]{2,1,0:T(8,128)(2,1)}), bf16[16,264,128]{2,1,0:T(8,128)(2,1)S(1)}, u32[]{:S(2)}, u32[]{:S(2)}) async-start(bf16[16,264,128]{2,1,0:T(8,128)(2,1)} %get-tuple-element.31), calls=%async_computation | async-start | bytes 2162688 | tf_op jit(solution)/shard_map/all_to_all | solution.py:211
  20.7 32.1 %collective-permute-start.6 = (bf16[2048,256]{1,0:T(8,128)(2,1)S(1)}, bf16[2048,256]{1,0:T(8,128)(2,1)}, u32[]{:S(2)}, u32[]{:S(2)}) collective-permute-start(bf16[2048,256]{1,0:T(8,128)(2,1)S(1)} %bitcast.11), channel_id=1, source_target_pairs={{0,16},{16,0},{1,17},{17,1},{2,18},{18,2},{3,19},{19,3},{4,20},{20... | collective-permute-start | bytes 3145736 | tf_op jit(solution)/shard_map/ppermute | solution.py:215
  22.6 22.5 %collective-permute-start = (bf16[768,256]{1,0:T(8,128)(2,1)}, bf16[768,256]{1,0:T(8,128)(2,1)}, u32[]{:S(2)}, u32[]{:S(2)}) collective-permute-start(bf16[768,256]{1,0:T(8,128)(2,1)} %refs_0_), channel_id=1, source_target_pairs={{0,3},{1,0},{2,1},{3,2},{4,7},{5,4},{6,5},{7,6},{8,11},{9,8},{10,9... | collective-permute-start | bytes 1179656 | tf_op jit(solution)/shard_map/ppermute | solution.py:227
  27.3 22.9 %collective-permute-start.1 = (bf16[768,256]{1,0:T(8,128)(2,1)}, bf16[768,256]{1,0:T(8,128)(2,1)}, u32[]{:S(2)}, u32[]{:S(2)}) collective-permute-start(bf16[768,256]{1,0:T(8,128)(2,1)} %refs_0_), channel_id=1, source_target_pairs={{0,2},{1,3},{2,0},{3,1},{4,6},{5,7},{6,4},{7,5},{8,10},{9,11},{10,... | collective-permute-start | bytes 1179656 | tf_op jit(solution)/shard_map/ppermute | solution.py:227
  30.0 69.7 %collective-permute-start.7 = (bf16[2048,256]{1,0:T(8,128)(2,1)S(1)}, bf16[2048,256]{1,0:T(8,128)(2,1)}, u32[]{:S(2)}, u32[]{:S(2)}) collective-permute-start(bf16[2048,256]{1,0:T(8,128)(2,1)S(1)} %bitcast.8), channel_id=1, source_target_pairs={{0,16},{16,0},{1,17},{17,1},{2,18},{18,2},{3,19},{19,3},{4,20},{20... | collective-permute-start | bytes 3145736 | tf_op jit(solution)/shard_map/ppermute | solution.py:215
  34.9 59.0 %collective-permute-start.3 = (bf16[1024,256]{1,0:T(8,128)(2,1)}, bf16[1024,256]{1,0:T(8,128)(2,1)}, u32[]{:S(2)}, u32[]{:S(2)}) collective-permute-start(bf16[1024,256]{1,0:T(8,128)(2,1)} %get-tuple-element.43), channel_id=1, source_target_pairs={{0,12},{4,0},{8,4},{12,8},{1,13},{5,1},{9,5},{13,9},{2,14},{6,2},{... | collective-permute-start | bytes 1572872 | tf_op jit(solution)/shard_map/ppermute | solution.py:227
  45.1 48.9 %collective-permute-start.4 = (bf16[1024,256]{1,0:T(8,128)(2,1)}, bf16[1024,256]{1,0:T(8,128)(2,1)}, u32[]{:S(2)}, u32[]{:S(2)}) collective-permute-start(bf16[1024,256]{1,0:T(8,128)(2,1)} %get-tuple-element.42), channel_id=1, source_target_pairs={{0,8},{4,12},{8,0},{12,4},{1,9},{5,13},{9,1},{13,5},{2,10},{6,14},... | collective-permute-start | bytes 1572872 | tf_op jit(solution)/shard_map/ppermute | solution.py:227
  50.2 43.8 %collective-permute-start.5 = (bf16[1024,256]{1,0:T(8,128)(2,1)}, bf16[1024,256]{1,0:T(8,128)(2,1)}, u32[]{:S(2)}, u32[]{:S(2)}) collective-permute-start(bf16[1024,256]{1,0:T(8,128)(2,1)} %get-tuple-element.41), channel_id=1, source_target_pairs={{0,4},{4,8},{8,12},{12,0},{1,5},{5,9},{9,13},{13,1},{2,6},{6,10},{... | collective-permute-start | bytes 1572872 | tf_op jit(solution)/shard_map/ppermute | solution.py:227
  52.8 41.1 %collective-permute-start.2 = (bf16[768,256]{1,0:T(8,128)(2,1)}, bf16[768,256]{1,0:T(8,128)(2,1)}, u32[]{:S(2)}, u32[]{:S(2)}) collective-permute-start(bf16[768,256]{1,0:T(8,128)(2,1)} %refs_0_), channel_id=1, source_target_pairs={{0,1},{1,2},{2,3},{3,0},{4,5},{5,6},{6,7},{7,4},{8,9},{9,10},{10,1... | collective-permute-start | bytes 1179656 | tf_op jit(solution)/shard_map/ppermute | solution.py:227
  90.4 12.2 %all-to-all-start.2 = ((bf16[16,64,128]{2,1,0:T(8,128)(2,1)}), bf16[16,64,128]{2,1,0:T(8,128)(2,1)S(1)}, u32[]{:S(2)}, u32[]{:S(2)}) async-start(bf16[16,64,128]{2,1,0:T(8,128)(2,1)} %total.1), calls=%async_computation.2 | async-start | bytes 524288 | tf_op jit(solution)/shard_map/all_to_all | solution.py:211
  94.0 1.0 copy-start.2
  107.3 55.8 %all-to-all-start.3 = ((bf16[16,2,64,256]{3,2,1,0:T(8,128)(2,1)}), bf16[16,2,64,256]{3,2,1,0:T(8,128)(2,1)S(1)}, u32[]{:S(2)}, u32[]{:S(2)}) async-start(bf16[16,2,64,256]{3,2,1,0:T(8,128)(2,1)} %expand.1), calls=%async_computation.3 | async-start | bytes 2097152 | tf_op jit(solution)/shard_map/all_to_all | solution.py:211
  116.0 12.3 %collective-permute-start.10 = (bf16[768,256]{1,0:T(8,128)(2,1)}, bf16[768,256]{1,0:T(8,128)(2,1)S(1)}, u32[]{:S(2)}, u32[]{:S(2)}) collective-permute-start(bf16[768,256]{1,0:T(8,128)(2,1)} %get-tuple-element.39), channel_id=1, source_target_pairs={{0,12},{4,0},{8,4},{12,8},{1,13},{5,1},{9,5},{13,9},{2,14},{6,2},{... | collective-permute-start | bytes 1179656 | tf_op jit(solution)/shard_map/ppermute | solution.py:227
  118.8 19.9 %collective-permute-start.8 = (bf16[768,256]{1,0:T(8,128)(2,1)}, bf16[768,256]{1,0:T(8,128)(2,1)S(1)}, u32[]{:S(2)}, u32[]{:S(2)}) collective-permute-start(bf16[768,256]{1,0:T(8,128)(2,1)} %get-tuple-element.37), channel_id=1, source_target_pairs={{0,4},{4,8},{8,12},{12,0},{1,5},{5,9},{9,13},{13,1},{2,6},{6,10},{... | collective-permute-start | bytes 1179656 | tf_op jit(solution)/shard_map/ppermute | solution.py:227
  121.9 17.6 %collective-permute-start.9 = (bf16[768,256]{1,0:T(8,128)(2,1)}, bf16[768,256]{1,0:T(8,128)(2,1)S(1)}, u32[]{:S(2)}, u32[]{:S(2)}) collective-permute-start(bf16[768,256]{1,0:T(8,128)(2,1)} %get-tuple-element.38), channel_id=1, source_target_pairs={{0,8},{4,12},{8,0},{12,4},{1,9},{5,13},{9,1},{13,5},{2,10},{6,14},... | collective-permute-start | bytes 1179656 | tf_op jit(solution)/shard_map/ppermute | solution.py:227
  138.7 0.7 copy-start.3
  139.4 0.7 copy-start.5
  140.2 1.0 copy-start.4
  141.2 1.0 copy-start.6

commit v5 on v4

--- a/solution.py
+++ b/solution.py
@@ -37,14 +37,15 @@
     return jnp.broadcast_to(row, (128, ROWS)).T[:, 0:1]
 
 
-def pack_kernel(index_ref, slot_ref, tokens_hbm, pay_hbm, dest_ref, tokens_ref, pay_ref, sem, out_sem):
+def pack_kernel(table_ref, tokens_hbm, pay_hbm, dest_ref, tokens_ref, pay_ref, sem, out_sem):
     bring = pltpu.make_async_copy(tokens_hbm, tokens_ref, sem.at[0])
     bring.start()
-    adapters = slot_ref.shape[1]
-    table = slot_ref[...]
+    adapters = table_ref.shape[1] - ROWS
+    index = table_ref[:, 0:ROWS]
+    table = table_ref[:, ROWS:]
     line = lax.broadcasted_iota(I32, (8, adapters), 0)
     table = jnp.where(line == 0, table >> 5, table & 31).astype(F32).astype(BF)
-    named = lax.broadcasted_iota(I32, (adapters, ROWS), 0) == index_ref[...]
+    named = lax.broadcasted_iota(I32, (adapters, ROWS), 0) == index
     found = jnp.dot(table, named.astype(F32).astype(BF), preferred_element_type=F32)
     holder, local = found[0:1], found[1:2]
     pool_row = holder * HELD + local
@@ -83,17 +84,14 @@
         send.wait()
 
 
-def shrink_kernel(core_ref, pay_ref, own_hbm, other_hbm, out_ref, ids_ref, pools, sem):
+def shrink_kernel(core_ref, pay_ref, own_ref, other_hbm, out_ref, ids_ref, other_ref, sem):
     core = core_ref[0]
-    brings = [
-        pltpu.make_async_copy(pool, pools.at[i], sem.at[i])
-        for i, pool in enumerate((own_hbm, other_hbm))
-    ]
-    for bring in brings:
-        bring.start()
+    bring = pltpu.make_async_copy(other_hbm, other_ref, sem.at[0])
+    bring.start()
     low = lax.broadcasted_iota(I32, (8, 128), 1) < PAIR
-    for i, c in enumerate((core, 1 - core)):
-        brings[i].wait()
+    for pool_ref, c in ((own_ref, core), (other_ref, 1 - core)):
+        if pool_ref is other_ref:
+            bring.wait()
         at = pl.multiple_of(128 * c, 128)
         for b in range(4):
             parts = []
@@ -115,7 +113,7 @@
             total = jnp.zeros((RANK, 256), F32)
             for q in range(8):
                 prod = lax.dot_general(
-                    pools[i, 256 * q : 256 * q + 256, :], rows, NT, preferred_element_type=F32
+                    pool_ref[256 * q : 256 * q + 256, :], rows, NT, preferred_element_type=F32
                 )
                 for a in range(4):
                     total = jnp.where(mark == 4 * q + a, prod[64 * a : 64 * a + 64], total)
@@ -139,34 +137,37 @@
         out_ref[t] = (column - high).astype(BF)
 
 
-def expand_kernel(core_ref, s_ref, marks_ref, own_hbm, other_hbm, out_hbm, m_ref, pools, rows_ref, sem, out_sem):
+def expand_kernel(
+    core_ref, s_ref, marks_ref, own_ref, other_hbm, out_hbm, other_ref, rows_ref, sem, out_sem
+):
     core = core_ref[0]
-    brings = [
-        pltpu.make_async_copy(pool, pools.at[i], sem.at[i])
-        for i, pool in enumerate((own_hbm, other_hbm))
-    ]
-    for bring in brings:
-        bring.start()
+    bring = pltpu.make_async_copy(other_hbm, other_ref, sem.at[0])
+    bring.start()
     sends = []
-    for i, c in enumerate((core, 1 - core)):
-        for h in range(2):
-            for k in range(4):
-                at = 8 * c + 4 * h + k
-                s = s_ref[at].astype(F32)
-                s = jnp.concatenate([s, s], axis=0).T.astype(BF)
-                mark = marks_ref[at]
-                for j in range(HELD // 2):
-                    m_ref[h, 128 * k : 128 * k + 128, 128 * j : 128 * j + 128] = jnp.where(
-                        mark == jnp.asarray(2 * j, BF), s, jnp.zeros_like(s)
-                    )
-            if h == 0:
-                brings[i].wait()
-            e = jnp.dot(m_ref[h], pools[i], preferred_element_type=F32)
-            rows_ref[i, 8 * h : 8 * h + 8] = e.astype(BF).reshape(8, PAIR, WIDTH)
-            part = pl.ds(8 * h, 8)
+    for i, (pool_ref, c) in enumerate(((own_ref, core), (other_ref, 1 - core))):
+        if i:
+            bring.wait()
+        for b in range(4):
+            at = 8 * c + 2 * b
+            s, mark = [], []
+            for k in range(2):
+                one = s_ref[at + k].astype(F32)
+                s.append(jnp.concatenate([one, one], axis=0).T.astype(BF))
+                mark.append(marks_ref[at + k])
+            s, mark = jnp.concatenate(s, axis=0), jnp.concatenate(mark, axis=0)
+            m = jnp.concatenate(
+                [
+                    jnp.where(mark == jnp.asarray(2 * j, BF), s, jnp.zeros_like(s))
+                    for j in range(HELD // 2)
+                ],
+                axis=1,
+            )
+            e = jnp.dot(m, pool_ref[...], preferred_element_type=F32)
+            part = pl.ds(4 * b, 4)
+            rows_ref[i, part] = e.astype(BF).reshape(4, PAIR, WIDTH)
             sends.append(
                 pltpu.make_async_copy(
-                    rows_ref.at[i, part], out_hbm.at[part, c], out_sem.at[2 * i + h]
+                    rows_ref.at[i, part], out_hbm.at[part, c], out_sem.at[4 * i + b]
                 )
             )
             sends[-1].start()
@@ -175,17 +176,26 @@
 
 
 def base_kernel(place_ref, *refs):
-    xs, ws, outs = refs[0:4], refs[4:8], refs[8:12]
+    outs, (xs, ws, sem) = refs[8:12], refs[12:15]
+    brings = [
+        pltpu.make_async_copy(refs[i], xs.at[i] if i < 4 else ws.at[i - 4], sem.at[i])
+        for i in range(8)
+    ]
+    for i in (0, 1, 2, 3, 4, 5, 6, 7):
+        brings[i].start()
+    for bring in brings[0:4]:
+        bring.wait()
     place = place_ref[0]
     for s in range(4):
+        brings[4 + s].wait()
         for half in range(2):
             at = 384 * half
             total = jnp.zeros((384, WIDTH), F32)
             for d in range(4):
-                row = pl.multiple_of(((place + d) % 4) * WIDTH, WIDTH)
+                row = pl.multiple_of(((place + d) & 3) * WIDTH, WIDTH)
                 total = total + jnp.dot(
-                    xs[d][at : at + 384, :],
-                    ws[s][pl.ds(row, WIDTH), :],
+                    xs[d, at : at + 384, :],
+                    ws[s, pl.ds(row, WIDTH), :],
                     preferred_element_type=F32,
                 )
             outs[s][at : at + 384, :] = total.astype(outs[s].dtype)
@@ -237,7 +247,7 @@
             jax.ShapeDtypeStruct((CHIPS, PAY, 128), BF),
             jax.ShapeDtypeStruct((1, ROWS), I32),
         ),
-        in_specs=vmem(2) + hbm(1),
+        in_specs=vmem(1) + hbm(1),
         out_specs=tuple(hbm(1) + vmem(1)),
         scratch_shapes=[
             pltpu.VMEM((ROWS, WIDTH), BF),
@@ -247,7 +257,7 @@
         ],
         compiler_params=params(),
         name="pack",
-    )(row_adapter_index.reshape(1, ROWS), adapter_pool_slot.reshape(1, -1), tokens)
+    )(jnp.concatenate([row_adapter_index, adapter_pool_slot]).reshape(1, -1), tokens)
     tokens, weight, a_pool, b_pool, payload = lax.optimization_barrier(
         (tokens, weight, a_pool, b_pool, payload)
     )
@@ -263,8 +273,13 @@
     parts = pl.pallas_call(
         base_kernel,
         out_shape=tuple(jax.ShapeDtypeStruct((ROWS, WIDTH), BF if s else F32) for s in range(4)),
-        in_specs=[scalar()] + vmem(8),
+        in_specs=[scalar()] + hbm(8),
         out_specs=tuple(vmem(4)),
+        scratch_shapes=[
+            pltpu.VMEM((4, ROWS, WIDTH), BF),
+            pltpu.VMEM((4, 4 * WIDTH, WIDTH), BF),
+            pltpu.SemaphoreType.DMA((8,)),
+        ],
         compiler_params=params(),
         cost_estimate=pl.CostEstimate(
             flops=2 * ROWS * 16 * WIDTH * WIDTH, bytes_accessed=6 * 2**20, transcendentals=0
@@ -277,9 +292,9 @@
             jax.ShapeDtypeStruct((TENSOR, RANK, 128), BF),
             jax.ShapeDtypeStruct((TENSOR, 8, 128), F32),
         ),
-        in_specs=[scalar()] + vmem(1) + hbm(2),
+        in_specs=[scalar()] + vmem(2) + hbm(1),
         out_specs=tuple(vmem(2)),
-        scratch_shapes=[pltpu.VMEM((2, HELD * RANK, WIDTH), BF), pltpu.SemaphoreType.DMA((2,))],
+        scratch_shapes=[pltpu.VMEM((HELD * RANK, WIDTH), BF), pltpu.SemaphoreType.DMA((1,))],
         compiler_params=params(),
         name="shrink",
     )(core, arrived, a_own, a_other)
@@ -303,14 +318,13 @@
     expanded = pl.pallas_call(
         expand_kernel,
         out_shape=jax.ShapeDtypeStruct((CHIPS, 2, PAIR, WIDTH), BF),
-        in_specs=[scalar()] + vmem(2) + hbm(2),
+        in_specs=[scalar()] + vmem(3) + hbm(1),
         out_specs=pl.BlockSpec(memory_space=pltpu.HBM),
         scratch_shapes=[
-            pltpu.VMEM((2, 512, HELD * RANK), BF),
-            pltpu.VMEM((2, HELD * RANK, WIDTH), BF),
+            pltpu.VMEM((HELD * RANK, WIDTH), BF),
             pltpu.VMEM((2, CHIPS, PAIR, WIDTH), BF),
-            pltpu.SemaphoreType.DMA((2,)),
-            pltpu.SemaphoreType.DMA((4,)),
+            pltpu.SemaphoreType.DMA((1,)),
+            pltpu.SemaphoreType.DMA((8,)),
         ],
         compiler_params=params(),
         name="expand",

time: 166 us -> 165 us (level)
    unnamed x16 -> x14, local copies, waits for them, and re-layouts: 5.2 us -> 4.52 us
  transfers between devices with their start and end apart: 14 -> 14, of which waited for: 6 -> 6; matrix products, arithmetic and copies ran while one was open for 2% -> 2% of each run, Pallas kernels for 5% -> 6%
where the time goes in v5:
time: 165 us; the launch traced here: 164 us
  starting transfers between devices  61.8 us (37%)
  waiting for transfers between devices  59.3 us (36%)
  Pallas kernels  18.4 us (11%)
  blocking collectives  15.5 us (9%)
  local copies, waits for them, and re-layouts  7.61 us (5%)
    all_to_all x3, waiting for transfers between devices, exchange(): return lax.all_to_all(x, axis, split_axis=0, concat_axis=0, tiled=True)  40.1 us
    ppermute x9, starting transfers between devices, turn(): return lax.ppermute(x, axis, [(i, (i + step) % 4) for i in range(4)])  30.5 us
    all_to_all x3, starting transfers between devices, exchange(): return lax.all_to_all(x, axis, split_axis=0, concat_axis=0, tiled=True)  27.5 us
    ppermute x9, waiting for transfers between devices, turn(): return lax.ppermute(x, axis, [(i, (i + step) % 4) for i in range(4)])  19.2 us
    all_to_all x1, blocking collectives, exchange(): return lax.all_to_all(x, axis, split_axis=0, concat_axis=0, tiled=True)  15.5 us
    unnamed x14, local copies, waits for them, and re-layouts  4.52 us
    pallas_call x1, Pallas kernels, body(): pl.pallas_call(base_kernel, out_shape=tuple((jax.ShapeDtypeStruct((ROWS,...  4.48 us
    pallas_call x1, Pallas kernels, body(): pl.pallas_call(pack_kernel, out_shape=(jax.ShapeDtypeStruct((CHIPS, PAY,...  3.92 us
  transfers between devices with their start and end apart: 14, of which 6 were waited for; matrix products, arithmetic and copies ran while one was open for 2% of the time, Pallas kernels for 6%

profile of v5, /device:TPU:32, one launch (start us, length us, event | category | flops | bytes accessed | tf_op | source)
XLA Modules:
  0.0 163.8 jit_solution(4213298314823921230)
XLA Ops:
  0.0 0.0 copy-start.1
  0.0 0.0 copy-start
  0.0 0.9 pad_add_fusion
  0.9 3.9 %pack.1 = (bf16[16,264,128]{2,1,0:T(8,128)(2,1)}, s32[1,768]{1,0:T(1,128)S(1)}) custom-call(s32[1,1792]{1,0:T(1,128)S(1)} %reshape.21.table_ref, bf16[768,256]{1,0:T(8,128)(2,1)} %refs_0_), custom_call_target="tpu_custom_call" | custom-call | tf_op jit(solution)/shard_map/pack/pallas_call | solution.py:244
  4.8 15.2 %all-to-all-start = ((bf16[16,264,128]{2,1,0:T(8,128)(2,1)}), bf16[16,264,128]{2,1,0:T(8,128)(2,1)S(1)}, u32[]{:S(2)}, u32[]{:S(2)}) async-start(bf16[16,264,128]{2,1,0:T(8,128)(2,1)} %get-tuple-element.31), calls=%async_computation | async-start | bytes 2162688 | tf_op jit(solution)/shard_map/all_to_all | solution.py:221
  20.0 0.0 copy-done.1
  20.0 1.9 %collective-permute-start.6 = (bf16[2048,256]{1,0:T(8,128)(2,1)S(1)}, bf16[2048,256]{1,0:T(8,128)(2,1)}, u32[]{:S(2)}, u32[]{:S(2)}) collective-permute-start(bf16[2048,256]{1,0:T(8,128)(2,1)S(1)} %bitcast.10), channel_id=1, source_target_pairs={{0,16},{16,0},{1,17},{17,1},{2,18},{18,2},{3,19},{19,3},{4,20},{20... | collective-permute-start | bytes 3145736 | tf_op jit(solution)/shard_map/ppermute | solution.py:225
  22.0 4.7 %collective-permute-start = (bf16[768,256]{1,0:T(8,128)(2,1)}, bf16[768,256]{1,0:T(8,128)(2,1)}, u32[]{:S(2)}, u32[]{:S(2)}) collective-permute-start(bf16[768,256]{1,0:T(8,128)(2,1)} %refs_0_), channel_id=1, source_target_pairs={{0,3},{1,0},{2,1},{3,2},{4,7},{5,4},{6,5},{7,6},{8,11},{9,8},{10,9... | collective-permute-start | bytes 1179656 | tf_op jit(solution)/shard_map/ppermute | solution.py:237
  26.6 2.7 %collective-permute-start.1 = (bf16[768,256]{1,0:T(8,128)(2,1)}, bf16[768,256]{1,0:T(8,128)(2,1)}, u32[]{:S(2)}, u32[]{:S(2)}) collective-permute-start(bf16[768,256]{1,0:T(8,128)(2,1)} %refs_0_), channel_id=1, source_target_pairs={{0,2},{1,3},{2,0},{3,1},{4,6},{5,7},{6,4},{7,5},{8,10},{9,11},{10,... | collective-permute-start | bytes 1179656 | tf_op jit(solution)/shard_map/ppermute | solution.py:237
  29.3 0.0 copy-done
  29.4 1.9 %collective-permute-start.7 = (bf16[2048,256]{1,0:T(8,128)(2,1)S(1)}, bf16[2048,256]{1,0:T(8,128)(2,1)}, u32[]{:S(2)}, u32[]{:S(2)}) collective-permute-start(bf16[2048,256]{1,0:T(8,128)(2,1)S(1)} %bitcast.7), channel_id=1, source_target_pairs={{0,16},{16,0},{1,17},{17,1},{2,18},{18,2},{3,19},{19,3},{4,20},{20... | collective-permute-start | bytes 3145736 | tf_op jit(solution)/shard_map/ppermute | solution.py:225
  31.4 2.9 %constant_dynamic-slice_fusion = (bf16[1024,256]{1,0:T(8,128)(2,1)}, bf16[1024,256]{1,0:T(8,128)(2,1)}, bf16[1024,256]{1,0:T(8,128)(2,1)}, bf16[1024,256]{1,0:T(8,128)(2,1)}) fusion(bf16[4096,256]{1,0:T(8,128)(2,1)} %param.7, s32[]{:T(128)S(6)} %select_n.38, s32[]{:T(128)S(6)} %select_n.36, s32[]{:T(128)S(6)} %select_n.34, s32[]{:T(128)S(6)} %select_n.32), kind=kLoop, calls=%fused_computation.1 | loop fusion | bytes 4194320 | tf_op jit(solution)/shard_map/dynamic_slice | solution.py:271
  34.3 4.9 %collective-permute-start.3 = (bf16[1024,256]{1,0:T(8,128)(2,1)}, bf16[1024,256]{1,0:T(8,128)(2,1)}, u32[]{:S(2)}, u32[]{:S(2)}) collective-permute-start(bf16[1024,256]{1,0:T(8,128)(2,1)} %get-tuple-element.43), channel_id=1, source_target_pairs={{0,12},{4,0},{8,4},{12,8},{1,13},{5,1},{9,5},{13,9},{2,14},{6,2},{... | collective-permute-start | bytes 1572872 | tf_op jit(solution)/shard_map/ppermute | solution.py:237
  39.2 5.2 %collective-permute-done.refs_1_ = bf16[768,256]{1,0:T(8,128)(2,1)} collective-permute-done((bf16[768,256]{1,0:T(8,128)(2,1)}, bf16[768,256]{1,0:T(8,128)(2,1)}, u32[]{:S(2)}, u32[]{:S(2)}) %collective-permute-start) | collective-permute-done | bytes 393248 | tf_op jit(solution)/shard_map/ppermute | solution.py:237
  44.4 5.1 %collective-permute-start.4 = (bf16[1024,256]{1,0:T(8,128)(2,1)}, bf16[1024,256]{1,0:T(8,128)(2,1)}, u32[]{:S(2)}, u32[]{:S(2)}) collective-permute-start(bf16[1024,256]{1,0:T(8,128)(2,1)} %get-tuple-element.42), channel_id=1, source_target_pairs={{0,8},{4,12},{8,0},{12,4},{1,9},{5,13},{9,1},{13,5},{2,10},{6,14},... | collective-permute-start | bytes 1572872 | tf_op jit(solution)/shard_map/ppermute | solution.py:237
  49.5 0.0 collective-permute-done.1.refs_2_
  49.5 2.6 %collective-permute-start.5 = (bf16[1024,256]{1,0:T(8,128)(2,1)}, bf16[1024,256]{1,0:T(8,128)(2,1)}, u32[]{:S(2)}, u32[]{:S(2)}) collective-permute-start(bf16[1024,256]{1,0:T(8,128)(2,1)} %get-tuple-element.41), channel_id=1, source_target_pairs={{0,4},{4,8},{8,12},{12,0},{1,5},{5,9},{9,13},{13,1},{2,6},{6,10},{... | collective-permute-start | bytes 1572872 | tf_op jit(solution)/shard_map/ppermute | solution.py:237
  52.1 0.0 collective-permute-done.6.other_hbm
  52.1 1.9 %collective-permute-start.2 = (bf16[768,256]{1,0:T(8,128)(2,1)}, bf16[768,256]{1,0:T(8,128)(2,1)}, u32[]{:S(2)}, u32[]{:S(2)}) collective-permute-start(bf16[768,256]{1,0:T(8,128)(2,1)} %refs_0_), channel_id=1, source_target_pairs={{0,1},{1,2},{2,3},{3,0},{4,5},{5,6},{6,7},{7,4},{8,9},{9,10},{10,1... | collective-permute-start | bytes 1179656 | tf_op jit(solution)/shard_map/ppermute | solution.py:237
  54.1 16.7 %all-to-all-done.pay_ref = bf16[16,264,128]{2,1,0:T(8,128)(2,1)S(1)} async-done(((bf16[16,264,128]{2,1,0:T(8,128)(2,1)}), bf16[16,264,128]{2,1,0:T(8,128)(2,1)S(1)}, u32[]{:S(2)}, u32[]{:S(2)}) %all-to-all-start) | async-done | bytes 1081376 | tf_op jit(solution)/shard_map/all_to_all | solution.py:221
  70.7 3.6 %shrink.1 = (bf16[16,64,128]{2,1,0:T(8,128)(2,1)S(1)}, f32[16,8,128]{2,1,0:T(8,128)S(1)}) custom-call(s32[1]{0:T(128)} %bitcast.2.core_ref, bf16[16,264,128]{2,1,0:T(8,128)(2,1)S(1)} %all-to-all-done.pay_ref, bf16[2048,256]{1,0:T(8,128)(2,1)S(1)} %bitcast.11, bf16[2048,256]{1,0:T(8,128)(2,1)} %collective-permute-done.6.other_hbm), custom_call_target="tpu_custom_call" | custom-call | tf_op jit(solution)/shard_map/shrink/pallas_call | solution.py:289
  74.3 15.5 %all_to_all.20.p_ref = bf16[16,64,128]{2,1,0:T(8,128)(2,1)S(1)} all-to-all(bf16[16,64,128]{2,1,0:T(8,128)(2,1)S(1)} %get-tuple-element.33), channel_id=1, replica_groups=mesh['z'=16,'core'=2,'y'=4,'x'=4] {'y','x'}, dimensions={0} | all-to-all | bytes 524288 | tf_op jit(solution)/shard_map/all_to_all | solution.py:221
  89.8 0.8 total.1
  90.6 3.5 %all-to-all-start.2 = ((bf16[16,64,128]{2,1,0:T(8,128)(2,1)}), bf16[16,64,128]{2,1,0:T(8,128)(2,1)S(1)}, u32[]{:S(2)}, u32[]{:S(2)}) async-start(bf16[16,64,128]{2,1,0:T(8,128)(2,1)} %total.1), calls=%async_computation.2 | async-start | bytes 524288 | tf_op jit(solution)/shard_map/all_to_all | solution.py:221
  94.1 0.0 collective-permute-done.2.refs_3_
  94.2 0.0 collective-permute-done.3.refs_5_
  94.2 0.0 collective-permute-done.4.refs_6_
  94.2 0.0 collective-permute-done.5.refs_7_
  94.2 0.0 copy-start.2
  94.2 1.0 copy-done.2
  95.2 4.5 %base.1 = (f32[768,256]{1,0:T(8,128)S(1)}, bf16[768,256]{1,0:T(8,128)(2,1)}, bf16[768,256]{1,0:T(8,128)(2,1)}, bf16[768,256]{1,0:T(8,128)(2,1)}) custom-call(s32[1]{0:T(128)} %bitcast.1.place_ref, bf16[768,256]{1,0:T(8,128)(2,1)} %refs_0_, bf16[768,256]{1,0:T(8,128)(2,1)} %collective-permute-done.refs_1_, bf16[768,256]{1,0:T(8,128)(2,1)} %collective-permute-done.1.refs_2_, ...), custom_call_target="tpu_custom_call" | custom-call | flops 1610612736 | bytes 6291456 | tf_op jit(solution)/shard_map/base/pallas_call | solution.py:273
  99.7 0.3 marks.1.marks_ref
  100.1 0.0 collective-permute-done.7.other_hbm
  100.1 2.7 %all-to-all-done.2.s_ref = bf16[16,64,128]{2,1,0:T(8,128)(2,1)S(1)} async-done(((bf16[16,64,128]{2,1,0:T(8,128)(2,1)}), bf16[16,64,128]{2,1,0:T(8,128)(2,1)S(1)}, u32[]{:S(2)}, u32[]{:S(2)}) %all-to-all-start.2) | async-done | bytes 262176 | tf_op jit(solution)/shard_map/all_to_all | solution.py:221
  102.8 3.4 %expand.1 = bf16[16,2,64,256]{3,2,1,0:T(8,128)(2,1)} custom-call(s32[1]{0:T(128)} %bitcast.2.core_ref, bf16[16,64,128]{2,1,0:T(8,128)(2,1)S(1)} %all-to-all-done.2.s_ref, bf16[16,128,128]{2,1,0:T(8,128)(2,1)S(1)} %marks.1.marks_ref, bf16[2048,256]{1,0:T(8,128)(2,1)S(1)} %bitcast.9, bf16[2048,256]{1,0:T(8,128)(2,1)} %collective-permute-done.7.other_hbm), custom_call_target="tpu_custom_call" | custom-call | tf_op jit(solution)/shard_map/expand/pallas_call | solution.py:318
  106.2 8.7 %all-to-all-start.3 = ((bf16[16,2,64,256]{3,2,1,0:T(8,128)(2,1)}), bf16[16,2,64,256]{3,2,1,0:T(8,128)(2,1)S(1)}, u32[]{:S(2)}, u32[]{:S(2)}) async-start(bf16[16,2,64,256]{3,2,1,0:T(8,128)(2,1)} %expand.1), calls=%async_computation.3 | async-start | bytes 2097152 | tf_op jit(solution)/shard_map/all_to_all | solution.py:221
  114.9 2.7 %collective-permute-start.10 = (bf16[768,256]{1,0:T(8,128)(2,1)}, bf16[768,256]{1,0:T(8,128)(2,1)S(1)}, u32[]{:S(2)}, u32[]{:S(2)}) collective-permute-start(bf16[768,256]{1,0:T(8,128)(2,1)} %get-tuple-element.39), channel_id=1, source_target_pairs={{0,12},{4,0},{8,4},{12,8},{1,13},{5,1},{9,5},{13,9},{2,14},{6,2},{... | collective-permute-start | bytes 1179656 | tf_op jit(solution)/shard_map/ppermute | solution.py:237
  117.7 3.1 %collective-permute-start.8 = (bf16[768,256]{1,0:T(8,128)(2,1)}, bf16[768,256]{1,0:T(8,128)(2,1)S(1)}, u32[]{:S(2)}, u32[]{:S(2)}) collective-permute-start(bf16[768,256]{1,0:T(8,128)(2,1)} %get-tuple-element.37), channel_id=1, source_target_pairs={{0,4},{4,8},{8,12},{12,0},{1,5},{5,9},{9,13},{13,1},{2,6},{6,10},{... | collective-permute-start | bytes 1179656 | tf_op jit(solution)/shard_map/ppermute | solution.py:237
  120.8 2.7 %collective-permute-start.9 = (bf16[768,256]{1,0:T(8,128)(2,1)}, bf16[768,256]{1,0:T(8,128)(2,1)S(1)}, u32[]{:S(2)}, u32[]{:S(2)}) collective-permute-start(bf16[768,256]{1,0:T(8,128)(2,1)} %get-tuple-element.38), channel_id=1, source_target_pairs={{0,8},{4,12},{8,0},{12,4},{1,9},{5,13},{9,1},{13,5},{2,10},{6,14},... | collective-permute-start | bytes 1179656 | tf_op jit(solution)/shard_map/ppermute | solution.py:237
  123.5 0.2 copy.7.dest_ref
  123.7 3.4 %collective-permute-done.10.p3_ref = bf16[768,256]{1,0:T(8,128)(2,1)S(1)} collective-permute-done((bf16[768,256]{1,0:T(8,128)(2,1)}, bf16[768,256]{1,0:T(8,128)(2,1)S(1)}, u32[]{:S(2)}, u32[]{:S(2)}) %collective-permute-start.10) | collective-permute-done | bytes 393248 | tf_op jit(solution)/shard_map/ppermute | solution.py:237
  127.1 10.5 %collective-permute-done.8.p1_ref = bf16[768,256]{1,0:T(8,128)(2,1)S(1)} collective-permute-done((bf16[768,256]{1,0:T(8,128)(2,1)}, bf16[768,256]{1,0:T(8,128)(2,1)S(1)}, u32[]{:S(2)}, u32[]{:S(2)}) %collective-permute-start.8) | collective-permute-done | bytes 393248 | tf_op jit(solution)/shard_map/ppermute | solution.py:237
  137.7 0.0 copy-start.3
  137.7 0.7 copy-done.3
  138.4 0.0 collective-permute-done.9.p2_ref
  138.4 0.0 copy-start.5
  138.4 0.7 copy-done.5
  139.2 0.0 copy-start.4
  139.2 1.0 copy-done.4
  140.2 0.0 copy-start.6
  140.2 1.0 copy-done.6
  141.2 0.2 ready.1.base_ref
  141.3 20.7 %all-to-all-done.3 = bf16[16,2,64,256]{3,2,1,0:T(8,128)(2,1)S(1)} async-done(((bf16[16,2,64,256]{3,2,1,0:T(8,128)(2,1)}), bf16[16,2,64,256]{3,2,1,0:T(8,128)(2,1)S(1)}, u32[]{:S(2)}, u32[]{:S(2)}) %all-to-all-start.3) | async-done | bytes 1048608 | tf_op jit(solution)/shard_map/all_to_all | solution.py:221
  162.0 1.8 %final.1 = bf16[768,256]{1,0:T(8,128)(2,1)} custom-call(s32[768,1]{1,0:T(8,128)S(1)} %copy.7.dest_ref, f32[768,256]{1,0:T(8,128)S(1)} %ready.1.base_ref, bf16[2048,256]{1,0:T(8,128)(2,1)S(1)} %bitcast.6), custom_call_target="tpu_custom_call" | custom-call | tf_op jit(solution)/shard_map/final/pallas_call | solution.py:343
  (1 shorter events, 0.0 us)
Async XLA Ops:
  0.0 20.0 %copy-start.1 = (bf16[32,64,256]{2,1,0:T(8,128)(2,1)S(1)}, bf16[32,64,256]{2,1,0:T(8,128)(2,1)}, u32[]{:S(2)}) copy-start(bf16[32,64,256]{2,1,0:T(8,128)(2,1)} %param.8) | copy-start | bytes 3145732
  0.0 29.3 %copy-start = (bf16[32,64,256]{2,1,0:T(8,128)(2,1)S(1)}, bf16[32,64,256]{2,1,0:T(8,128)(2,1)}, u32[]{:S(2)}) copy-start(bf16[32,64,256]{2,1,0:T(8,128)(2,1)} %param.9) | copy-start | bytes 3145732
  4.8 65.9 %all-to-all-start = ((bf16[16,264,128]{2,1,0:T(8,128)(2,1)}), bf16[16,264,128]{2,1,0:T(8,128)(2,1)S(1)}, u32[]{:S(2)}, u32[]{:S(2)}) async-start(bf16[16,264,128]{2,1,0:T(8,128)(2,1)} %get-tuple-element.31), calls=%async_computation | async-start | bytes 2162688 | tf_op jit(solution)/shard_map/all_to_all | solution.py:221
  20.0 32.1 %collective-permute-start.6 = (bf16[2048,256]{1,0:T(8,128)(2,1)S(1)}, bf16[2048,256]{1,0:T(8,128)(2,1)}, u32[]{:S(2)}, u32[]{:S(2)}) collective-permute-start(bf16[2048,256]{1,0:T(8,128)(2,1)S(1)} %bitcast.10), channel_id=1, source_target_pairs={{0,16},{16,0},{1,17},{17,1},{2,18},{18,2},{3,19},{19,3},{4,20},{20... | collective-permute-start | bytes 3145736 | tf_op jit(solution)/shard_map/ppermute | solution.py:225
  22.0 22.5 %collective-permute-start = (bf16[768,256]{1,0:T(8,128)(2,1)}, bf16[768,256]{1,0:T(8,128)(2,1)}, u32[]{:S(2)}, u32[]{:S(2)}) collective-permute-start(bf16[768,256]{1,0:T(8,128)(2,1)} %refs_0_), channel_id=1, source_target_pairs={{0,3},{1,0},{2,1},{3,2},{4,7},{5,4},{6,5},{7,6},{8,11},{9,8},{10,9... | collective-permute-start | bytes 1179656 | tf_op jit(solution)/shard_map/ppermute | solution.py:237
  26.6 22.9 %collective-permute-start.1 = (bf16[768,256]{1,0:T(8,128)(2,1)}, bf16[768,256]{1,0:T(8,128)(2,1)}, u32[]{:S(2)}, u32[]{:S(2)}) collective-permute-start(bf16[768,256]{1,0:T(8,128)(2,1)} %refs_0_), channel_id=1, source_target_pairs={{0,2},{1,3},{2,0},{3,1},{4,6},{5,7},{6,4},{7,5},{8,10},{9,11},{10,... | collective-permute-start | bytes 1179656 | tf_op jit(solution)/shard_map/ppermute | solution.py:237
  29.4 70.7 %collective-permute-start.7 = (bf16[2048,256]{1,0:T(8,128)(2,1)S(1)}, bf16[2048,256]{1,0:T(8,128)(2,1)}, u32[]{:S(2)}, u32[]{:S(2)}) collective-permute-start(bf16[2048,256]{1,0:T(8,128)(2,1)S(1)} %bitcast.7), channel_id=1, source_target_pairs={{0,16},{16,0},{1,17},{17,1},{2,18},{18,2},{3,19},{19,3},{4,20},{20... | collective-permute-start | bytes 3145736 | tf_op jit(solution)/shard_map/ppermute | solution.py:225
  34.3 59.9 %collective-permute-start.3 = (bf16[1024,256]{1,0:T(8,128)(2,1)}, bf16[1024,256]{1,0:T(8,128)(2,1)}, u32[]{:S(2)}, u32[]{:S(2)}) collective-permute-start(bf16[1024,256]{1,0:T(8,128)(2,1)} %get-tuple-element.43), channel_id=1, source_target_pairs={{0,12},{4,0},{8,4},{12,8},{1,13},{5,1},{9,5},{13,9},{2,14},{6,2},{... | collective-permute-start | bytes 1572872 | tf_op jit(solution)/shard_map/ppermute | solution.py:237
  44.4 49.8 %collective-permute-start.4 = (bf16[1024,256]{1,0:T(8,128)(2,1)}, bf16[1024,256]{1,0:T(8,128)(2,1)}, u32[]{:S(2)}, u32[]{:S(2)}) collective-permute-start(bf16[1024,256]{1,0:T(8,128)(2,1)} %get-tuple-element.42), channel_id=1, source_target_pairs={{0,8},{4,12},{8,0},{12,4},{1,9},{5,13},{9,1},{13,5},{2,10},{6,14},... | collective-permute-start | bytes 1572872 | tf_op jit(solution)/shard_map/ppermute | solution.py:237
  49.5 44.7 %collective-permute-start.5 = (bf16[1024,256]{1,0:T(8,128)(2,1)}, bf16[1024,256]{1,0:T(8,128)(2,1)}, u32[]{:S(2)}, u32[]{:S(2)}) collective-permute-start(bf16[1024,256]{1,0:T(8,128)(2,1)} %get-tuple-element.41), channel_id=1, source_target_pairs={{0,4},{4,8},{8,12},{12,0},{1,5},{5,9},{9,13},{13,1},{2,6},{6,10},{... | collective-permute-start | bytes 1572872 | tf_op jit(solution)/shard_map/ppermute | solution.py:237
  52.1 42.0 %collective-permute-start.2 = (bf16[768,256]{1,0:T(8,128)(2,1)}, bf16[768,256]{1,0:T(8,128)(2,1)}, u32[]{:S(2)}, u32[]{:S(2)}) collective-permute-start(bf16[768,256]{1,0:T(8,128)(2,1)} %refs_0_), channel_id=1, source_target_pairs={{0,1},{1,2},{2,3},{3,0},{4,5},{5,6},{6,7},{7,4},{8,9},{9,10},{10,1... | collective-permute-start | bytes 1179656 | tf_op jit(solution)/shard_map/ppermute | solution.py:237
  90.6 12.2 %all-to-all-start.2 = ((bf16[16,64,128]{2,1,0:T(8,128)(2,1)}), bf16[16,64,128]{2,1,0:T(8,128)(2,1)S(1)}, u32[]{:S(2)}, u32[]{:S(2)}) async-start(bf16[16,64,128]{2,1,0:T(8,128)(2,1)} %total.1), calls=%async_computation.2 | async-start | bytes 524288 | tf_op jit(solution)/shard_map/all_to_all | solution.py:221
  94.2 1.0 copy-start.2
  106.2 55.8 %all-to-all-start.3 = ((bf16[16,2,64,256]{3,2,1,0:T(8,128)(2,1)}), bf16[16,2,64,256]{3,2,1,0:T(8,128)(2,1)S(1)}, u32[]{:S(2)}, u32[]{:S(2)}) async-start(bf16[16,2,64,256]{3,2,1,0:T(8,128)(2,1)} %expand.1), calls=%async_computation.3 | async-start | bytes 2097152 | tf_op jit(solution)/shard_map/all_to_all | solution.py:221
  114.9 12.2 %collective-permute-start.10 = (bf16[768,256]{1,0:T(8,128)(2,1)}, bf16[768,256]{1,0:T(8,128)(2,1)S(1)}, u32[]{:S(2)}, u32[]{:S(2)}) collective-permute-start(bf16[768,256]{1,0:T(8,128)(2,1)} %get-tuple-element.39), channel_id=1, source_target_pairs={{0,12},{4,0},{8,4},{12,8},{1,13},{5,1},{9,5},{13,9},{2,14},{6,2},{... | collective-permute-start | bytes 1179656 | tf_op jit(solution)/shard_map/ppermute | solution.py:237
  117.7 20.0 %collective-permute-start.8 = (bf16[768,256]{1,0:T(8,128)(2,1)}, bf16[768,256]{1,0:T(8,128)(2,1)S(1)}, u32[]{:S(2)}, u32[]{:S(2)}) collective-permute-start(bf16[768,256]{1,0:T(8,128)(2,1)} %get-tuple-element.37), channel_id=1, source_target_pairs={{0,4},{4,8},{8,12},{12,0},{1,5},{5,9},{9,13},{13,1},{2,6},{6,10},{... | collective-permute-start | bytes 1179656 | tf_op jit(solution)/shard_map/ppermute | solution.py:237
  120.8 17.6 %collective-permute-start.9 = (bf16[768,256]{1,0:T(8,128)(2,1)}, bf16[768,256]{1,0:T(8,128)(2,1)S(1)}, u32[]{:S(2)}, u32[]{:S(2)}) collective-permute-start(bf16[768,256]{1,0:T(8,128)(2,1)} %get-tuple-element.38), channel_id=1, source_target_pairs={{0,8},{4,12},{8,0},{12,4},{1,9},{5,13},{9,1},{13,5},{2,10},{6,14},... | collective-permute-start | bytes 1179656 | tf_op jit(solution)/shard_map/ppermute | solution.py:237
  137.7 0.7 copy-start.3
  138.4 0.7 copy-start.5
  139.2 1.0 copy-start.4
  140.2 1.0 copy-start.6

commit v6 on v5

--- a/solution.py
+++ b/solution.py
@@ -84,14 +84,17 @@
         send.wait()
 
 
-def shrink_kernel(core_ref, pay_ref, own_ref, other_hbm, out_ref, ids_ref, other_ref, sem):
+def shrink_kernel(core_ref, pay_ref, own_hbm, other_hbm, out_ref, ids_ref, pools, sem):
     core = core_ref[0]
-    bring = pltpu.make_async_copy(other_hbm, other_ref, sem.at[0])
-    bring.start()
+    brings = [
+        pltpu.make_async_copy(pool, pools.at[i], sem.at[i])
+        for i, pool in enumerate((own_hbm, other_hbm))
+    ]
+    for bring in brings:
+        bring.start()
     low = lax.broadcasted_iota(I32, (8, 128), 1) < PAIR
-    for pool_ref, c in ((own_ref, core), (other_ref, 1 - core)):
-        if pool_ref is other_ref:
-            bring.wait()
+    for i, c in enumerate((core, 1 - core)):
+        brings[i].wait()
         at = pl.multiple_of(128 * c, 128)
         for b in range(4):
             parts = []
@@ -113,7 +116,7 @@
             total = jnp.zeros((RANK, 256), F32)
             for q in range(8):
                 prod = lax.dot_general(
-                    pool_ref[256 * q : 256 * q + 256, :], rows, NT, preferred_element_type=F32
+                    pools[i, 256 * q : 256 * q + 256, :], rows, NT, preferred_element_type=F32
                 )
                 for a in range(4):
                     total = jnp.where(mark == 4 * q + a, prod[64 * a : 64 * a + 64], total)
@@ -176,17 +179,17 @@
 
 
 def base_kernel(place_ref, *refs):
-    outs, (xs, ws, sem) = refs[8:12], refs[12:15]
+    outs, (xs, ws, sem) = refs[6:8], refs[8:11]
     brings = [
         pltpu.make_async_copy(refs[i], xs.at[i] if i < 4 else ws.at[i - 4], sem.at[i])
-        for i in range(8)
+        for i in range(6)
     ]
-    for i in (0, 1, 2, 3, 4, 5, 6, 7):
-        brings[i].start()
+    for bring in brings:
+        bring.start()
     for bring in brings[0:4]:
         bring.wait()
     place = place_ref[0]
-    for s in range(4):
+    for s in range(2):
         brings[4 + s].wait()
         for half in range(2):
             at = 384 * half
@@ -270,34 +273,41 @@
     for s in range(4):
         mine = lax.dynamic_slice(weight, (((y - s) % 4) * 4 * WIDTH, 0), (4 * WIDTH, WIDTH))
         ws.append(turn(mine, "y", -s) if s else mine)
-    parts = pl.pallas_call(
-        base_kernel,
-        out_shape=tuple(jax.ShapeDtypeStruct((ROWS, WIDTH), BF if s else F32) for s in range(4)),
-        in_specs=[scalar()] + hbm(8),
-        out_specs=tuple(vmem(4)),
-        scratch_shapes=[
-            pltpu.VMEM((4, ROWS, WIDTH), BF),
-            pltpu.VMEM((4, 4 * WIDTH, WIDTH), BF),
-            pltpu.SemaphoreType.DMA((8,)),
-        ],
-        compiler_params=params(),
-        cost_estimate=pl.CostEstimate(
-            flops=2 * ROWS * 16 * WIDTH * WIDTH, bytes_accessed=6 * 2**20, transcendentals=0
-        ),
-        name="base",
-    )(lax.axis_index("x").astype(I32).reshape(1), *xs, *ws)
+    place = lax.axis_index("x").astype(I32).reshape(1)
+
+    def base_parts(first):
+        return pl.pallas_call(
+            base_kernel,
+            out_shape=tuple(
+                jax.ShapeDtypeStruct((ROWS, WIDTH), BF if s else F32) for s in (first, first + 1)
+            ),
+            in_specs=[scalar()] + hbm(6),
+            out_specs=tuple(vmem(2)),
+            scratch_shapes=[
+                pltpu.VMEM((4, ROWS, WIDTH), BF),
+                pltpu.VMEM((2, 4 * WIDTH, WIDTH), BF),
+                pltpu.SemaphoreType.DMA((6,)),
+            ],
+            compiler_params=params(),
+            cost_estimate=pl.CostEstimate(
+                flops=2 * ROWS * 8 * WIDTH * WIDTH, bytes_accessed=4 * 2**20, transcendentals=0
+            ),
+            name="base",
+        )(place, *xs, ws[first], ws[first + 1])
+
     partial, ids = pl.pallas_call(
         shrink_kernel,
         out_shape=(
             jax.ShapeDtypeStruct((TENSOR, RANK, 128), BF),
             jax.ShapeDtypeStruct((TENSOR, 8, 128), F32),
         ),
-        in_specs=[scalar()] + vmem(2) + hbm(1),
+        in_specs=[scalar()] + vmem(1) + hbm(2),
         out_specs=tuple(vmem(2)),
-        scratch_shapes=[pltpu.VMEM((HELD * RANK, WIDTH), BF), pltpu.SemaphoreType.DMA((1,))],
+        scratch_shapes=[pltpu.VMEM((2, HELD * RANK, WIDTH), BF), pltpu.SemaphoreType.DMA((2,))],
         compiler_params=params(),
         name="shrink",
     )(core, arrived, a_own, a_other)
+    gathered, p0, p1 = lax.optimization_barrier((exchange(partial, tensor), *base_parts(0)))
     summed = pl.pallas_call(
         sum_kernel,
         out_shape=jax.ShapeDtypeStruct((TENSOR, RANK, 128), BF),
@@ -305,7 +315,7 @@
         out_specs=pl.BlockSpec(memory_space=pltpu.VMEM),
         compiler_params=params(),
         name="total",
-    )(exchange(partial, tensor))
+    )(gathered)
     shrunk = exchange(summed, tensor)
     marks = pl.pallas_call(
         marks_kernel,
@@ -329,7 +339,7 @@
         compiler_params=params(),
         name="expand",
     )(core, shrunk, marks, b_own, b_other)
-    p0, p1, p2, p3, expanded = lax.optimization_barrier((*parts, expanded))
+    p0, p1, p2, p3, expanded = lax.optimization_barrier((p0, p1, *base_parts(2), expanded))
     back = exchange(expanded, "z").reshape(BUCKETS, WIDTH)
     sums = [turn(p, "y", s) for s, p in ((1, p1), (2, p2), (3, p3))]
     base = pl.pallas_call(

time: 165 us -> 165 us (level)
  blocking collectives: 15.5 us -> 0 us
  starting transfers between devices: 61.8 us -> 69.7 us
  waiting for transfers between devices: 59.3 us -> 65.7 us
    all_to_all x1 -> x0, blocking collectives: 15.5 us -> none  [exchange(): return lax.all_to_all(x, axis, split_axis=0, concat_axis=0, tiled=True)]
    all_to_all x3 -> x4, waiting for transfers between devices: 40.1 us -> 48.2 us  [exchange(): return lax.all_to_all(x, axis, split_axis=0, concat_axis=0, tiled=True)]
    all_to_all x3 -> x4, starting transfers between devices: 27.5 us -> 34.6 us  [exchange(): return lax.all_to_all(x, axis, split_axis=0, concat_axis=0, tiled=True)]
    ppermute x9, waiting for transfers between devices: 19.2 us -> 17.4 us  [turn(): return lax.ppermute(x, axis, [(i, (i + step) % 4) for i in range(4)])]
    pallas_call x1 -> x2, Pallas kernels: 4.48 us -> 6.04 us  [base_parts(): pl.pallas_call(base_kernel, out_shape=tuple((jax.ShapeDtypeStruct((ROWS,...]
    unnamed x14 -> x16, local copies, waits for them, and re-layouts: 4.52 us -> 4.52 us
  transfers between devices with their start and end apart: 14 -> 15, of which waited for: 6 -> 7; matrix products, arithmetic and copies ran while one was open for 2% -> 2% of each run, Pallas kernels for 6% -> 7%
where the time goes in v6:
time: 165 us; the launch traced here: 164 us
  starting transfers between devices  69.7 us (42%)
  waiting for transfers between devices  65.7 us (40%)
  Pallas kernels  19.8 us (12%)
  local copies, waits for them, and re-layouts  7.62 us (5%)
    all_to_all x4, waiting for transfers between devices, exchange(): return lax.all_to_all(x, axis, split_axis=0, concat_axis=0, tiled=True)  48.2 us
    all_to_all x4, starting transfers between devices, exchange(): return lax.all_to_all(x, axis, split_axis=0, concat_axis=0, tiled=True)  34.6 us
    ppermute x9, starting transfers between devices, turn(): return lax.ppermute(x, axis, [(i, (i + step) % 4) for i in range(4)])  31.1 us
    ppermute x9, waiting for transfers between devices, turn(): return lax.ppermute(x, axis, [(i, (i + step) % 4) for i in range(4)])  17.4 us
    pallas_call x2, Pallas kernels, base_parts(): pl.pallas_call(base_kernel, out_shape=tuple((jax.ShapeDtypeStruct((ROWS,...  6.04 us
    unnamed x16, local copies, waits for them, and re-layouts  4.52 us
    ppermute x2, starting transfers between devices, sibling(): return lax.ppermute(x, 'core', [(0, 1), (1, 0)])  4.05 us
    pallas_call x1, Pallas kernels, body(): pl.pallas_call(pack_kernel, out_shape=(jax.ShapeDtypeStruct((CHIPS, PAY,...  3.92 us
  transfers between devices with their start and end apart: 15, of which 7 were waited for; matrix products, arithmetic and copies ran while one was open for 2% of the time, Pallas kernels for 7%

profile of v6, /device:TPU:32, one launch (start us, length us, event | category | flops | bytes accessed | tf_op | source)
XLA Modules:
  0.0 164.0 jit_solution(10937442047038206367)
XLA Ops:
  0.0 0.0 copy-start.1
  0.0 0.0 copy-start
  0.0 0.9 pad_add_fusion
  0.9 3.9 %pack.1 = (bf16[16,264,128]{2,1,0:T(8,128)(2,1)}, s32[1,768]{1,0:T(1,128)S(1)}) custom-call(s32[1,1792]{1,0:T(1,128)S(1)} %reshape.21.table_ref, bf16[768,256]{1,0:T(8,128)(2,1)} %refs_0_.1), custom_call_target="tpu_custom_call" | custom-call | tf_op jit(solution)/shard_map/pack/pallas_call | solution.py:247
  4.8 15.2 %all-to-all-start = ((bf16[16,264,128]{2,1,0:T(8,128)(2,1)}), bf16[16,264,128]{2,1,0:T(8,128)(2,1)S(1)}, u32[]{:S(2)}, u32[]{:S(2)}) async-start(bf16[16,264,128]{2,1,0:T(8,128)(2,1)} %get-tuple-element.28), calls=%async_computation | async-start | bytes 2162688 | tf_op jit(solution)/shard_map/all_to_all | solution.py:224
  20.0 0.0 copy-done.1
  20.0 1.9 %collective-permute-start = (bf16[2048,256]{1,0:T(8,128)(2,1)S(1)}, bf16[2048,256]{1,0:T(8,128)(2,1)}, u32[]{:S(2)}, u32[]{:S(2)}) collective-permute-start(bf16[2048,256]{1,0:T(8,128)(2,1)S(1)} %bitcast.10), channel_id=1, source_target_pairs={{0,16},{16,0},{1,17},{17,1},{2,18},{18,2},{3,19},{19,3},{4,20},{20... | collective-permute-start | bytes 3145736 | tf_op jit(solution)/shard_map/ppermute | solution.py:228
  22.0 4.7 %collective-permute-start.1 = (bf16[768,256]{1,0:T(8,128)(2,1)}, bf16[768,256]{1,0:T(8,128)(2,1)}, u32[]{:S(2)}, u32[]{:S(2)}) collective-permute-start(bf16[768,256]{1,0:T(8,128)(2,1)} %refs_0_.1), channel_id=1, source_target_pairs={{0,3},{1,0},{2,1},{3,2},{4,7},{5,4},{6,5},{7,6},{8,11},{9,8},{10,9... | collective-permute-start | bytes 1179656 | tf_op jit(solution)/shard_map/ppermute | solution.py:240
  26.6 0.0 copy-done
  26.6 2.1 %collective-permute-start.7 = (bf16[2048,256]{1,0:T(8,128)(2,1)S(1)}, bf16[2048,256]{1,0:T(8,128)(2,1)}, u32[]{:S(2)}, u32[]{:S(2)}) collective-permute-start(bf16[2048,256]{1,0:T(8,128)(2,1)S(1)} %bitcast.7), channel_id=1, source_target_pairs={{0,16},{16,0},{1,17},{17,1},{2,18},{18,2},{3,19},{19,3},{4,20},{20... | collective-permute-start | bytes 3145736 | tf_op jit(solution)/shard_map/ppermute | solution.py:228
  28.8 2.7 %collective-permute-start.2 = (bf16[768,256]{1,0:T(8,128)(2,1)}, bf16[768,256]{1,0:T(8,128)(2,1)}, u32[]{:S(2)}, u32[]{:S(2)}) collective-permute-start(bf16[768,256]{1,0:T(8,128)(2,1)} %refs_0_.1), channel_id=1, source_target_pairs={{0,2},{1,3},{2,0},{3,1},{4,6},{5,7},{6,4},{7,5},{8,10},{9,11},{10,... | collective-permute-start | bytes 1179656 | tf_op jit(solution)/shard_map/ppermute | solution.py:240
  31.6 2.9 %constant_dynamic-slice_fusion = (bf16[1024,256]{1,0:T(8,128)(2,1)}, bf16[1024,256]{1,0:T(8,128)(2,1)}, bf16[1024,256]{1,0:T(8,128)(2,1)}, bf16[1024,256]{1,0:T(8,128)(2,1)}) fusion(bf16[4096,256]{1,0:T(8,128)(2,1)} %param.7, s32[]{:T(128)S(6)} %select_n.38, s32[]{:T(128)S(6)} %select_n.36, s32[]{:T(128)S(6)} %select_n.34, s32[]{:T(128)S(6)} %select_n.32), kind=kLoop, calls=%fused_computation.1 | loop fusion | bytes 4194320 | tf_op jit(solution)/shard_map/dynamic_slice | solution.py:274
  34.5 4.9 %collective-permute-start.4 = (bf16[1024,256]{1,0:T(8,128)(2,1)}, bf16[1024,256]{1,0:T(8,128)(2,1)}, u32[]{:S(2)}, u32[]{:S(2)}) collective-permute-start(bf16[1024,256]{1,0:T(8,128)(2,1)} %get-tuple-element.49), channel_id=1, source_target_pairs={{0,12},{4,0},{8,4},{12,8},{1,13},{5,1},{9,5},{13,9},{2,14},{6,2},{... | collective-permute-start | bytes 1572872 | tf_op jit(solution)/shard_map/ppermute | solution.py:240
  39.4 5.0 %collective-permute-done.1.refs_1_ = bf16[768,256]{1,0:T(8,128)(2,1)} collective-permute-done((bf16[768,256]{1,0:T(8,128)(2,1)}, bf16[768,256]{1,0:T(8,128)(2,1)}, u32[]{:S(2)}, u32[]{:S(2)}) %collective-permute-start.1) | collective-permute-done | bytes 393248 | tf_op jit(solution)/shard_map/ppermute | solution.py:240
  44.4 1.9 %collective-permute-start.3 = (bf16[768,256]{1,0:T(8,128)(2,1)}, bf16[768,256]{1,0:T(8,128)(2,1)}, u32[]{:S(2)}, u32[]{:S(2)}) collective-permute-start(bf16[768,256]{1,0:T(8,128)(2,1)} %refs_0_.1), channel_id=1, source_target_pairs={{0,1},{1,2},{2,3},{3,0},{4,5},{5,6},{6,7},{7,4},{8,9},{9,10},{10,1... | collective-permute-start | bytes 1179656 | tf_op jit(solution)/shard_map/ppermute | solution.py:240
  46.3 0.0 collective-permute-done.2.refs_2_
  46.4 5.1 %collective-permute-start.5 = (bf16[1024,256]{1,0:T(8,128)(2,1)}, bf16[1024,256]{1,0:T(8,128)(2,1)}, u32[]{:S(2)}, u32[]{:S(2)}) collective-permute-start(bf16[1024,256]{1,0:T(8,128)(2,1)} %get-tuple-element.48), channel_id=1, source_target_pairs={{0,8},{4,12},{8,0},{12,4},{1,9},{5,13},{9,1},{13,5},{2,10},{6,14},... | collective-permute-start | bytes 1572872 | tf_op jit(solution)/shard_map/ppermute | solution.py:240
  51.5 0.0 collective-permute-done.other_hbm
  51.5 2.6 %collective-permute-start.6 = (bf16[1024,256]{1,0:T(8,128)(2,1)}, bf16[1024,256]{1,0:T(8,128)(2,1)}, u32[]{:S(2)}, u32[]{:S(2)}) collective-permute-start(bf16[1024,256]{1,0:T(8,128)(2,1)} %get-tuple-element.47), channel_id=1, source_target_pairs={{0,4},{4,8},{8,12},{12,0},{1,5},{5,9},{9,13},{13,1},{2,6},{6,10},{... | collective-permute-start | bytes 1572872 | tf_op jit(solution)/shard_map/ppermute | solution.py:240
  54.1 16.7 %all-to-all-done.pay_ref = bf16[16,264,128]{2,1,0:T(8,128)(2,1)S(1)} async-done(((bf16[16,264,128]{2,1,0:T(8,128)(2,1)}), bf16[16,264,128]{2,1,0:T(8,128)(2,1)S(1)}, u32[]{:S(2)}, u32[]{:S(2)}) %all-to-all-start) | async-done | bytes 1081376 | tf_op jit(solution)/shard_map/all_to_all | solution.py:224
  70.7 3.4 %shrink.1 = (bf16[16,64,128]{2,1,0:T(8,128)(2,1)}, f32[16,8,128]{2,1,0:T(8,128)S(1)}) custom-call(s32[1]{0:T(128)} %bitcast.1.core_ref, bf16[16,264,128]{2,1,0:T(8,128)(2,1)S(1)} %all-to-all-done.pay_ref, bf16[2048,256]{1,0:T(8,128)(2,1)S(1)} %bitcast.11, bf16[2048,256]{1,0:T(8,128)(2,1)} %collective-permute-done.other_hbm), custom_call_target="tpu_custom_call" | custom-call | tf_op jit(solution)/shard_map/shrink/pallas_call | solution.py:298
  74.1 7.0 %all-to-all-start.1 = ((bf16[16,64,128]{2,1,0:T(8,128)(2,1)}), bf16[16,64,128]{2,1,0:T(8,128)(2,1)S(1)}, u32[]{:S(2)}, u32[]{:S(2)}) async-start(bf16[16,64,128]{2,1,0:T(8,128)(2,1)} %get-tuple-element.30), calls=%async_computation.1 | async-start | bytes 524288 | tf_op jit(solution)/shard_map/all_to_all | solution.py:224
  81.2 0.0 collective-permute-done.3.refs_3_
  81.2 0.0 collective-permute-done.4.refs_5_
  81.2 0.0 copy-start.2
  81.2 1.0 copy-done.2
  82.3 2.6 %base.2 = (f32[768,256]{1,0:T(8,128)S(1)}, bf16[768,256]{1,0:T(8,128)(2,1)S(1)}) custom-call(s32[1]{0:T(128)} %bitcast.3.place_ref, bf16[768,256]{1,0:T(8,128)(2,1)} %refs_0_.1, bf16[768,256]{1,0:T(8,128)(2,1)} %collective-permute-done.1.refs_1_, bf16[768,256]{1,0:T(8,128)(2,1)} %collective-permute-done.2.refs_2_, ...), custom_call_target="tpu_custom_call" | custom-call | flops 805306368 | bytes 4194304 | tf_op jit(solution)/shard_map/base/pallas_call | solution.py:279
  84.8 0.0 copy-start.7
  84.8 5.1 %all-to-all-done.1.p_ref = bf16[16,64,128]{2,1,0:T(8,128)(2,1)S(1)} async-done(((bf16[16,64,128]{2,1,0:T(8,128)(2,1)}), bf16[16,64,128]{2,1,0:T(8,128)(2,1)S(1)}, u32[]{:S(2)}, u32[]{:S(2)}) %all-to-all-start.1) | async-done | bytes 262176 | tf_op jit(solution)/shard_map/all_to_all | solution.py:224
  89.9 0.8 total.1
  90.6 0.0 copy-done.7
  90.6 3.5 %all-to-all-start.2 = ((bf16[16,64,128]{2,1,0:T(8,128)(2,1)}), bf16[16,64,128]{2,1,0:T(8,128)(2,1)S(1)}, u32[]{:S(2)}, u32[]{:S(2)}) async-start(bf16[16,64,128]{2,1,0:T(8,128)(2,1)} %total.1), calls=%async_computation.2 | async-start | bytes 524288 | tf_op jit(solution)/shard_map/all_to_all | solution.py:224
  94.2 0.0 collective-permute-done.5.refs_4_
  94.2 0.0 collective-permute-done.6.refs_5_
  94.2 3.5 %base.3 = (bf16[768,256]{1,0:T(8,128)(2,1)}, bf16[768,256]{1,0:T(8,128)(2,1)}) custom-call(s32[1]{0:T(128)} %bitcast.3.place_ref, bf16[768,256]{1,0:T(8,128)(2,1)} %refs_0_.1, bf16[768,256]{1,0:T(8,128)(2,1)} %collective-permute-done.1.refs_1_, bf16[768,256]{1,0:T(8,128)(2,1)} %collective-permute-done.2.refs_2_, ...), custom_call_target="tpu_custom_call" | custom-call | flops 805306368 | bytes 4194304 | tf_op jit(solution)/shard_map/base/pallas_call | solution.py:279
  97.7 0.3 marks.1.marks_ref
  98.0 0.0 collective-permute-done.7.other_hbm
  98.0 4.8 %all-to-all-done.2.s_ref = bf16[16,64,128]{2,1,0:T(8,128)(2,1)S(1)} async-done(((bf16[16,64,128]{2,1,0:T(8,128)(2,1)}), bf16[16,64,128]{2,1,0:T(8,128)(2,1)S(1)}, u32[]{:S(2)}, u32[]{:S(2)}) %all-to-all-start.2) | async-done | bytes 262176 | tf_op jit(solution)/shard_map/all_to_all | solution.py:224
  102.8 3.4 %expand.1 = bf16[16,2,64,256]{3,2,1,0:T(8,128)(2,1)} custom-call(s32[1]{0:T(128)} %bitcast.1.core_ref, bf16[16,64,128]{2,1,0:T(8,128)(2,1)S(1)} %all-to-all-done.2.s_ref, bf16[16,128,128]{2,1,0:T(8,128)(2,1)S(1)} %marks.1.marks_ref, bf16[2048,256]{1,0:T(8,128)(2,1)S(1)} %bitcast.9, bf16[2048,256]{1,0:T(8,128)(2,1)} %collective-permute-done.7.other_hbm), custom_call_target="tpu_custom_call" | custom-call | tf_op jit(solution)/shard_map/expand/pallas_call | solution.py:328
  106.3 8.8 %all-to-all-start.3 = ((bf16[16,2,64,256]{3,2,1,0:T(8,128)(2,1)}), bf16[16,2,64,256]{3,2,1,0:T(8,128)(2,1)S(1)}, u32[]{:S(2)}, u32[]{:S(2)}) async-start(bf16[16,2,64,256]{3,2,1,0:T(8,128)(2,1)} %expand.1), calls=%async_computation.3 | async-start | bytes 2097152 | tf_op jit(solution)/shard_map/all_to_all | solution.py:224
  115.1 1.9 %collective-permute-start.8 = (bf16[768,256]{1,0:T(8,128)(2,1)}, bf16[768,256]{1,0:T(8,128)(2,1)S(1)}, u32[]{:S(2)}, u32[]{:S(2)}) collective-permute-start(bf16[768,256]{1,0:T(8,128)(2,1)} %copy-done.7), channel_id=1, source_target_pairs={{0,4},{4,8},{8,12},{12,0},{1,5},{5,9},{9,13},{13,1},{2,6},{6,10},{... | collective-permute-start | bytes 1179656 | tf_op jit(solution)/shard_map/ppermute | solution.py:240
  117.0 4.2 %collective-permute-start.9 = (bf16[768,256]{1,0:T(8,128)(2,1)}, bf16[768,256]{1,0:T(8,128)(2,1)S(1)}, u32[]{:S(2)}, u32[]{:S(2)}) collective-permute-start(bf16[768,256]{1,0:T(8,128)(2,1)} %get-tuple-element.44), channel_id=1, source_target_pairs={{0,8},{4,12},{8,0},{12,4},{1,9},{5,13},{9,1},{13,5},{2,10},{6,14},... | collective-permute-start | bytes 1179656 | tf_op jit(solution)/shard_map/ppermute | solution.py:240
  121.2 3.1 %collective-permute-start.10 = (bf16[768,256]{1,0:T(8,128)(2,1)}, bf16[768,256]{1,0:T(8,128)(2,1)S(1)}, u32[]{:S(2)}, u32[]{:S(2)}) collective-permute-start(bf16[768,256]{1,0:T(8,128)(2,1)} %get-tuple-element.45), channel_id=1, source_target_pairs={{0,12},{4,0},{8,4},{12,8},{1,13},{5,1},{9,5},{13,9},{2,14},{6,2},{... | collective-permute-start | bytes 1179656 | tf_op jit(solution)/shard_map/ppermute | solution.py:240
  124.3 0.2 copy.7.dest_ref
  124.5 10.6 %collective-permute-done.8.p1_ref = bf16[768,256]{1,0:T(8,128)(2,1)S(1)} collective-permute-done((bf16[768,256]{1,0:T(8,128)(2,1)}, bf16[768,256]{1,0:T(8,128)(2,1)S(1)}, u32[]{:S(2)}, u32[]{:S(2)}) %collective-permute-start.8) | collective-permute-done | bytes 393248 | tf_op jit(solution)/shard_map/ppermute | solution.py:240
  135.0 0.0 collective-permute-done.9.p2_ref
  135.1 0.0 copy-start.3
  135.1 0.7 copy-done.3
  135.8 1.8 %collective-permute-done.10.p3_ref = bf16[768,256]{1,0:T(8,128)(2,1)S(1)} collective-permute-done((bf16[768,256]{1,0:T(8,128)(2,1)}, bf16[768,256]{1,0:T(8,128)(2,1)S(1)}, u32[]{:S(2)}, u32[]{:S(2)}) %collective-permute-start.10) | collective-permute-done | bytes 393248 | tf_op jit(solution)/shard_map/ppermute | solution.py:240
  137.6 0.0 copy-start.5
  137.6 0.7 copy-done.5
  138.3 0.0 copy-start.4
  138.3 1.0 copy-done.4
  139.3 0.0 copy-start.6
  139.3 1.0 copy-done.6
  140.3 0.2 ready.1.base_ref
  140.5 21.7 %all-to-all-done.3 = bf16[16,2,64,256]{3,2,1,0:T(8,128)(2,1)S(1)} async-done(((bf16[16,2,64,256]{3,2,1,0:T(8,128)(2,1)}), bf16[16,2,64,256]{3,2,1,0:T(8,128)(2,1)S(1)}, u32[]{:S(2)}, u32[]{:S(2)}) %all-to-all-start.3) | async-done | bytes 1048608 | tf_op jit(solution)/shard_map/all_to_all | solution.py:224
  162.2 1.8 %final.1 = bf16[768,256]{1,0:T(8,128)(2,1)} custom-call(s32[768,1]{1,0:T(8,128)S(1)} %copy.7.dest_ref, f32[768,256]{1,0:T(8,128)S(1)} %ready.1.base_ref, bf16[2048,256]{1,0:T(8,128)(2,1)S(1)} %bitcast.6), custom_call_target="tpu_custom_call" | custom-call | tf_op jit(solution)/shard_map/final/pallas_call | solution.py:353
  (1 shorter events, 0.0 us)
Async XLA Ops:
  0.0 20.0 %copy-start.1 = (bf16[32,64,256]{2,1,0:T(8,128)(2,1)S(1)}, bf16[32,64,256]{2,1,0:T(8,128)(2,1)}, u32[]{:S(2)}) copy-start(bf16[32,64,256]{2,1,0:T(8,128)(2,1)} %param.8) | copy-start | bytes 3145732
  0.0 26.6 %copy-start = (bf16[32,64,256]{2,1,0:T(8,128)(2,1)S(1)}, bf16[32,64,256]{2,1,0:T(8,128)(2,1)}, u32[]{:S(2)}) copy-start(bf16[32,64,256]{2,1,0:T(8,128)(2,1)} %param.9) | copy-start | bytes 3145732
  4.8 65.9 %all-to-all-start = ((bf16[16,264,128]{2,1,0:T(8,128)(2,1)}), bf16[16,264,128]{2,1,0:T(8,128)(2,1)S(1)}, u32[]{:S(2)}, u32[]{:S(2)}) async-start(bf16[16,264,128]{2,1,0:T(8,128)(2,1)} %get-tuple-element.28), calls=%async_computation | async-start | bytes 2162688 | tf_op jit(solution)/shard_map/all_to_all | solution.py:224
  20.0 31.4 %collective-permute-start = (bf16[2048,256]{1,0:T(8,128)(2,1)S(1)}, bf16[2048,256]{1,0:T(8,128)(2,1)}, u32[]{:S(2)}, u32[]{:S(2)}) collective-permute-start(bf16[2048,256]{1,0:T(8,128)(2,1)S(1)} %bitcast.10), channel_id=1, source_target_pairs={{0,16},{16,0},{1,17},{17,1},{2,18},{18,2},{3,19},{19,3},{4,20},{20... | collective-permute-start | bytes 3145736 | tf_op jit(solution)/shard_map/ppermute | solution.py:228
  22.0 22.5 %collective-permute-start.1 = (bf16[768,256]{1,0:T(8,128)(2,1)}, bf16[768,256]{1,0:T(8,128)(2,1)}, u32[]{:S(2)}, u32[]{:S(2)}) collective-permute-start(bf16[768,256]{1,0:T(8,128)(2,1)} %refs_0_.1), channel_id=1, source_target_pairs={{0,3},{1,0},{2,1},{3,2},{4,7},{5,4},{6,5},{7,6},{8,11},{9,8},{10,9... | collective-permute-start | bytes 1179656 | tf_op jit(solution)/shard_map/ppermute | solution.py:240
  26.6 71.4 %collective-permute-start.7 = (bf16[2048,256]{1,0:T(8,128)(2,1)S(1)}, bf16[2048,256]{1,0:T(8,128)(2,1)}, u32[]{:S(2)}, u32[]{:S(2)}) collective-permute-start(bf16[2048,256]{1,0:T(8,128)(2,1)S(1)} %bitcast.7), channel_id=1, source_target_pairs={{0,16},{16,0},{1,17},{17,1},{2,18},{18,2},{3,19},{19,3},{4,20},{20... | collective-permute-start | bytes 3145736 | tf_op jit(solution)/shard_map/ppermute | solution.py:228
  28.8 17.6 %collective-permute-start.2 = (bf16[768,256]{1,0:T(8,128)(2,1)}, bf16[768,256]{1,0:T(8,128)(2,1)}, u32[]{:S(2)}, u32[]{:S(2)}) collective-permute-start(bf16[768,256]{1,0:T(8,128)(2,1)} %refs_0_.1), channel_id=1, source_target_pairs={{0,2},{1,3},{2,0},{3,1},{4,6},{5,7},{6,4},{7,5},{8,10},{9,11},{10,... | collective-permute-start | bytes 1179656 | tf_op jit(solution)/shard_map/ppermute | solution.py:240
  34.5 46.7 %collective-permute-start.4 = (bf16[1024,256]{1,0:T(8,128)(2,1)}, bf16[1024,256]{1,0:T(8,128)(2,1)}, u32[]{:S(2)}, u32[]{:S(2)}) collective-permute-start(bf16[1024,256]{1,0:T(8,128)(2,1)} %get-tuple-element.49), channel_id=1, source_target_pairs={{0,12},{4,0},{8,4},{12,8},{1,13},{5,1},{9,5},{13,9},{2,14},{6,2},{... | collective-permute-start | bytes 1572872 | tf_op jit(solution)/shard_map/ppermute | solution.py:240
  44.4 36.8 %collective-permute-start.3 = (bf16[768,256]{1,0:T(8,128)(2,1)}, bf16[768,256]{1,0:T(8,128)(2,1)}, u32[]{:S(2)}, u32[]{:S(2)}) collective-permute-start(bf16[768,256]{1,0:T(8,128)(2,1)} %refs_0_.1), channel_id=1, source_target_pairs={{0,1},{1,2},{2,3},{3,0},{4,5},{5,6},{6,7},{7,4},{8,9},{9,10},{10,1... | collective-permute-start | bytes 1179656 | tf_op jit(solution)/shard_map/ppermute | solution.py:240
  46.4 47.8 %collective-permute-start.5 = (bf16[1024,256]{1,0:T(8,128)(2,1)}, bf16[1024,256]{1,0:T(8,128)(2,1)}, u32[]{:S(2)}, u32[]{:S(2)}) collective-permute-start(bf16[1024,256]{1,0:T(8,128)(2,1)} %get-tuple-element.48), channel_id=1, source_target_pairs={{0,8},{4,12},{8,0},{12,4},{1,9},{5,13},{9,1},{13,5},{2,10},{6,14},... | collective-permute-start | bytes 1572872 | tf_op jit(solution)/shard_map/ppermute | solution.py:240
  51.5 42.7 %collective-permute-start.6 = (bf16[1024,256]{1,0:T(8,128)(2,1)}, bf16[1024,256]{1,0:T(8,128)(2,1)}, u32[]{:S(2)}, u32[]{:S(2)}) collective-permute-start(bf16[1024,256]{1,0:T(8,128)(2,1)} %get-tuple-element.47), channel_id=1, source_target_pairs={{0,4},{4,8},{8,12},{12,0},{1,5},{5,9},{9,13},{13,1},{2,6},{6,10},{... | collective-permute-start | bytes 1572872 | tf_op jit(solution)/shard_map/ppermute | solution.py:240
  74.1 15.7 %all-to-all-start.1 = ((bf16[16,64,128]{2,1,0:T(8,128)(2,1)}), bf16[16,64,128]{2,1,0:T(8,128)(2,1)S(1)}, u32[]{:S(2)}, u32[]{:S(2)}) async-start(bf16[16,64,128]{2,1,0:T(8,128)(2,1)} %get-tuple-element.30), calls=%async_computation.1 | async-start | bytes 524288 | tf_op jit(solution)/shard_map/all_to_all | solution.py:224
  81.2 1.0 copy-start.2
  84.8 5.8 %copy-start.7 = (bf16[768,256]{1,0:T(8,128)(2,1)}, bf16[768,256]{1,0:T(8,128)(2,1)S(1)}, u32[]{:S(2)}) copy-start(bf16[768,256]{1,0:T(8,128)(2,1)S(1)} %get-tuple-element.43) | copy-start | bytes 1179652
  90.6 12.2 %all-to-all-start.2 = ((bf16[16,64,128]{2,1,0:T(8,128)(2,1)}), bf16[16,64,128]{2,1,0:T(8,128)(2,1)S(1)}, u32[]{:S(2)}, u32[]{:S(2)}) async-start(bf16[16,64,128]{2,1,0:T(8,128)(2,1)} %total.1), calls=%async_computation.2 | async-start | bytes 524288 | tf_op jit(solution)/shard_map/all_to_all | solution.py:224
  106.3 55.9 %all-to-all-start.3 = ((bf16[16,2,64,256]{3,2,1,0:T(8,128)(2,1)}), bf16[16,2,64,256]{3,2,1,0:T(8,128)(2,1)S(1)}, u32[]{:S(2)}, u32[]{:S(2)}) async-start(bf16[16,2,64,256]{3,2,1,0:T(8,128)(2,1)} %expand.1), calls=%async_computation.3 | async-start | bytes 2097152 | tf_op jit(solution)/shard_map/all_to_all | solution.py:224
  115.1 20.0 %collective-permute-start.8 = (bf16[768,256]{1,0:T(8,128)(2,1)}, bf16[768,256]{1,0:T(8,128)(2,1)S(1)}, u32[]{:S(2)}, u32[]{:S(2)}) collective-permute-start(bf16[768,256]{1,0:T(8,128)(2,1)} %copy-done.7), channel_id=1, source_target_pairs={{0,4},{4,8},{8,12},{12,0},{1,5},{5,9},{9,13},{13,1},{2,6},{6,10},{... | collective-permute-start | bytes 1179656 | tf_op jit(solution)/shard_map/ppermute | solution.py:240
  117.0 18.0 %collective-permute-start.9 = (bf16[768,256]{1,0:T(8,128)(2,1)}, bf16[768,256]{1,0:T(8,128)(2,1)S(1)}, u32[]{:S(2)}, u32[]{:S(2)}) collective-permute-start(bf16[768,256]{1,0:T(8,128)(2,1)} %get-tuple-element.44), channel_id=1, source_target_pairs={{0,8},{4,12},{8,0},{12,4},{1,9},{5,13},{9,1},{13,5},{2,10},{6,14},... | collective-permute-start | bytes 1179656 | tf_op jit(solution)/shard_map/ppermute | solution.py:240
  121.2 16.4 %collective-permute-start.10 = (bf16[768,256]{1,0:T(8,128)(2,1)}, bf16[768,256]{1,0:T(8,128)(2,1)S(1)}, u32[]{:S(2)}, u32[]{:S(2)}) collective-permute-start(bf16[768,256]{1,0:T(8,128)(2,1)} %get-tuple-element.45), channel_id=1, source_target_pairs={{0,12},{4,0},{8,4},{12,8},{1,13},{5,1},{9,5},{13,9},{2,14},{6,2},{... | collective-permute-start | bytes 1179656 | tf_op jit(solution)/shard_map/ppermute | solution.py:240
  135.1 0.7 copy-start.3
  137.6 0.7 copy-start.5
  138.3 1.0 copy-start.4
  139.3 1.0 copy-start.6

commit v7 on v6

--- a/solution.py
+++ b/solution.py
@@ -273,9 +273,10 @@
     for s in range(4):
         mine = lax.dynamic_slice(weight, (((y - s) % 4) * 4 * WIDTH, 0), (4 * WIDTH, WIDTH))
         ws.append(turn(mine, "y", -s) if s else mine)
+    arrived, *xs = lax.optimization_barrier((arrived, *xs))
     place = lax.axis_index("x").astype(I32).reshape(1)
 
-    def base_parts(first):
+    def base_parts(first, xs, ws):
         return pl.pallas_call(
             base_kernel,
             out_shape=tuple(
@@ -307,7 +308,7 @@
         compiler_params=params(),
         name="shrink",
     )(core, arrived, a_own, a_other)
-    gathered, p0, p1 = lax.optimization_barrier((exchange(partial, tensor), *base_parts(0)))
+    gathered = exchange(partial, tensor)
     summed = pl.pallas_call(
         sum_kernel,
         out_shape=jax.ShapeDtypeStruct((TENSOR, RANK, 128), BF),
@@ -339,8 +340,9 @@
         compiler_params=params(),
         name="expand",
     )(core, shrunk, marks, b_own, b_other)
-    p0, p1, p2, p3, expanded = lax.optimization_barrier((p0, p1, *base_parts(2), expanded))
+    p0, p1, expanded, xs, ws = lax.optimization_barrier((*base_parts(0, xs, ws), expanded, xs, ws))
     back = exchange(expanded, "z").reshape(BUCKETS, WIDTH)
+    p2, p3 = base_parts(2, xs, ws)
     sums = [turn(p, "y", s) for s, p in ((1, p1), (2, p2), (3, p3))]
     base = pl.pallas_call(
         ready_kernel,

time: 165 us -> 165 us (level)
  blocking collectives: 0 us -> 15.6 us
  waiting for transfers between devices: 65.7 us -> 51.2 us
  starting transfers between devices: 69.7 us -> 65.7 us
  local copies, waits for them, and re-layouts: 7.62 us -> 9.59 us
    all_to_all x0 -> x1, blocking collectives: none -> 15.6 us  [exchange(): return lax.all_to_all(x, axis, split_axis=0, concat_axis=0, tiled=True)]
    all_to_all x4 -> x3, waiting for transfers between devices: 48.2 us -> 34.2 us  [exchange(): return lax.all_to_all(x, axis, split_axis=0, concat_axis=0, tiled=True)]
    all_to_all x4 -> x3, starting transfers between devices: 34.6 us -> 27.6 us  [exchange(): return lax.all_to_all(x, axis, split_axis=0, concat_axis=0, tiled=True)]
    ppermute x9, starting transfers between devices: 31.1 us -> 33.8 us  [turn(): return lax.ppermute(x, axis, [(i, (i + step) % 4) for i in range(4)])]
    unnamed x16 -> x20, local copies, waits for them, and re-layouts: 4.52 us -> 6.49 us
  transfers between devices with their start and end apart: 15 -> 14, of which waited for: 7 -> 7; matrix products, arithmetic and copies ran while one was open for 2% -> 2% of each run, Pallas kernels for 7% -> 9%
where the time goes in v7:
time: 165 us; the launch traced here: 164 us
  starting transfers between devices  65.7 us (40%)
  waiting for transfers between devices  51.2 us (31%)
  Pallas kernels  20.4 us (12%)
  blocking collectives  15.6 us (9%)
  local copies, waits for them, and re-layouts  9.59 us (6%)
    all_to_all x3, waiting for transfers between devices, exchange(): return lax.all_to_all(x, axis, split_axis=0, concat_axis=0, tiled=True)  34.2 us
    ppermute x9, starting transfers between devices, turn(): return lax.ppermute(x, axis, [(i, (i + step) % 4) for i in range(4)])  33.8 us
    all_to_all x3, starting transfers between devices, exchange(): return lax.all_to_all(x, axis, split_axis=0, concat_axis=0, tiled=True)  27.6 us
    ppermute x9, waiting for transfers between devices, turn(): return lax.ppermute(x, axis, [(i, (i + step) % 4) for i in range(4)])  16.9 us
    all_to_all x1, blocking collectives, exchange(): return lax.all_to_all(x, axis, split_axis=0, concat_axis=0, tiled=True)  15.6 us
    pallas_call x2, Pallas kernels, base_parts(): pl.pallas_call(base_kernel, out_shape=tuple((jax.ShapeDtypeStruct((ROWS,...  6.88 us
    unnamed x20, local copies, waits for them, and re-layouts  6.49 us
    ppermute x2, starting transfers between devices, sibling(): return lax.ppermute(x, 'core', [(0, 1), (1, 0)])  4.33 us
  transfers between devices with their start and end apart: 14, of which 7 were waited for; matrix products, arithmetic and copies ran while one was open for 2% of the time, Pallas kernels for 9%

profile of v7, /device:TPU:32, one launch (start us, length us, event | category | flops | bytes accessed | tf_op | source)
XLA Modules:
  0.0 163.7 jit_solution(3024489683159436385)
XLA Ops:
  0.0 0.0 copy-start
  0.0 0.0 copy-start.1
  0.0 0.9 pad_add_fusion
  0.9 0.0 copy-start.3
  0.9 1.0 copy-done.3
  1.9 3.4 %pack.1 = (bf16[16,264,128]{2,1,0:T(8,128)(2,1)}, s32[1,768]{1,0:T(1,128)S(1)}) custom-call(s32[1,1792]{1,0:T(1,128)S(1)} %reshape.21.table_ref, bf16[768,256]{1,0:T(8,128)(2,1)S(1)} %copy-done.3), custom_call_target="tpu_custom_call" | custom-call | tf_op jit(solution)/shard_map/pack/pallas_call | solution.py:247
  5.2 15.2 %all-to-all-start = ((bf16[16,264,128]{2,1,0:T(8,128)(2,1)}), bf16[16,264,128]{2,1,0:T(8,128)(2,1)S(1)}, u32[]{:S(2)}, u32[]{:S(2)}) async-start(bf16[16,264,128]{2,1,0:T(8,128)(2,1)} %get-tuple-element.34), calls=%async_computation | async-start | bytes 2162688 | tf_op jit(solution)/shard_map/all_to_all | solution.py:224
  20.5 0.0 copy-done.1
  20.5 1.9 %collective-permute-start.4 = (bf16[2048,256]{1,0:T(8,128)(2,1)S(1)}, bf16[2048,256]{1,0:T(8,128)(2,1)}, u32[]{:S(2)}, u32[]{:S(2)}) collective-permute-start(bf16[2048,256]{1,0:T(8,128)(2,1)S(1)} %bitcast.10), channel_id=1, source_target_pairs={{0,16},{16,0},{1,17},{17,1},{2,18},{18,2},{3,19},{19,3},{4,20},{20... | collective-permute-start | bytes 3145736 | tf_op jit(solution)/shard_map/ppermute | solution.py:228
  22.4 0.0 copy-done
  22.4 2.4 %collective-permute-start.5 = (bf16[2048,256]{1,0:T(8,128)(2,1)S(1)}, bf16[2048,256]{1,0:T(8,128)(2,1)}, u32[]{:S(2)}, u32[]{:S(2)}) collective-permute-start(bf16[2048,256]{1,0:T(8,128)(2,1)S(1)} %bitcast.7), channel_id=1, source_target_pairs={{0,16},{16,0},{1,17},{17,1},{2,18},{18,2},{3,19},{19,3},{4,20},{20... | collective-permute-start | bytes 3145736 | tf_op jit(solution)/shard_map/ppermute | solution.py:228
  24.8 3.4 %collective-permute-start.2 = (bf16[768,256]{1,0:T(8,128)(2,1)}, bf16[768,256]{1,0:T(8,128)(2,1)}, u32[]{:S(2)}, u32[]{:S(2)}) collective-permute-start(bf16[768,256]{1,0:T(8,128)(2,1)} %refs_0_.1), channel_id=1, source_target_pairs={{0,1},{1,2},{2,3},{3,0},{4,5},{5,6},{6,7},{7,4},{8,9},{9,10},{10,1... | collective-permute-start | bytes 1179656 | tf_op jit(solution)/shard_map/ppermute | solution.py:240
  28.2 4.6 %collective-permute-start.1 = (bf16[768,256]{1,0:T(8,128)(2,1)}, bf16[768,256]{1,0:T(8,128)(2,1)}, u32[]{:S(2)}, u32[]{:S(2)}) collective-permute-start(bf16[768,256]{1,0:T(8,128)(2,1)} %refs_0_.1), channel_id=1, source_target_pairs={{0,2},{1,3},{2,0},{3,1},{4,6},{5,7},{6,4},{7,5},{8,10},{9,11},{10,... | collective-permute-start | bytes 1179656 | tf_op jit(solution)/shard_map/ppermute | solution.py:240
  32.9 3.3 %collective-permute-start = (bf16[768,256]{1,0:T(8,128)(2,1)}, bf16[768,256]{1,0:T(8,128)(2,1)}, u32[]{:S(2)}, u32[]{:S(2)}) collective-permute-start(bf16[768,256]{1,0:T(8,128)(2,1)} %refs_0_.1), channel_id=1, source_target_pairs={{0,3},{1,0},{2,1},{3,2},{4,7},{5,4},{6,5},{7,6},{8,11},{9,8},{10,9... | collective-permute-start | bytes 1179656 | tf_op jit(solution)/shard_map/ppermute | solution.py:240
  36.3 2.9 %constant_dynamic-slice_fusion = (bf16[1024,256]{1,0:T(8,128)(2,1)}, bf16[1024,256]{1,0:T(8,128)(2,1)}, bf16[1024,256]{1,0:T(8,128)(2,1)}, bf16[1024,256]{1,0:T(8,128)(2,1)}) fusion(bf16[4096,256]{1,0:T(8,128)(2,1)} %param.7, s32[]{:T(128)S(6)} %select_n.38, s32[]{:T(128)S(6)} %select_n.36, s32[]{:T(128)S(6)} %select_n.34, s32[]{:T(128)S(6)} %select_n.32), kind=kLoop, calls=%fused_computation.1 | loop fusion | bytes 4194320 | tf_op jit(solution)/shard_map/dynamic_slice | solution.py:274
  39.2 0.1 collective-permute-done.2.refs_3_
  39.3 4.9 %collective-permute-start.3 = (bf16[1024,256]{1,0:T(8,128)(2,1)}, bf16[1024,256]{1,0:T(8,128)(2,1)}, u32[]{:S(2)}, u32[]{:S(2)}) collective-permute-start(bf16[1024,256]{1,0:T(8,128)(2,1)} %get-tuple-element.61), channel_id=1, source_target_pairs={{0,12},{4,0},{8,4},{12,8},{1,13},{5,1},{9,5},{13,9},{2,14},{6,2},{... | collective-permute-start | bytes 1572872 | tf_op jit(solution)/shard_map/ppermute | solution.py:240
  44.2 4.5 %collective-permute-done.1.refs_2_ = bf16[768,256]{1,0:T(8,128)(2,1)} collective-permute-done((bf16[768,256]{1,0:T(8,128)(2,1)}, bf16[768,256]{1,0:T(8,128)(2,1)}, u32[]{:S(2)}, u32[]{:S(2)}) %collective-permute-start.1) | collective-permute-done | bytes 393248 | tf_op jit(solution)/shard_map/ppermute | solution.py:240
  48.7 3.5 %collective-permute-start.7 = (bf16[1024,256]{1,0:T(8,128)(2,1)}, bf16[1024,256]{1,0:T(8,128)(2,1)}, u32[]{:S(2)}, u32[]{:S(2)}) collective-permute-start(bf16[1024,256]{1,0:T(8,128)(2,1)} %get-tuple-element.59), channel_id=1, source_target_pairs={{0,4},{4,8},{8,12},{12,0},{1,5},{5,9},{9,13},{13,1},{2,6},{6,10},{... | collective-permute-start | bytes 1572872 | tf_op jit(solution)/shard_map/ppermute | solution.py:240
  52.2 0.0 collective-permute-done.refs_1_
  52.2 4.8 %collective-permute-start.6 = (bf16[1024,256]{1,0:T(8,128)(2,1)}, bf16[1024,256]{1,0:T(8,128)(2,1)}, u32[]{:S(2)}, u32[]{:S(2)}) collective-permute-start(bf16[1024,256]{1,0:T(8,128)(2,1)} %get-tuple-element.60), channel_id=1, source_target_pairs={{0,8},{4,12},{8,0},{12,4},{1,9},{5,13},{9,1},{13,5},{2,10},{6,14},... | collective-permute-start | bytes 1572872 | tf_op jit(solution)/shard_map/ppermute | solution.py:240
  57.0 14.2 %all-to-all-done.pay_ref = bf16[16,264,128]{2,1,0:T(8,128)(2,1)S(1)} async-done(((bf16[16,264,128]{2,1,0:T(8,128)(2,1)}), bf16[16,264,128]{2,1,0:T(8,128)(2,1)S(1)}, u32[]{:S(2)}, u32[]{:S(2)}) %all-to-all-start) | async-done | bytes 1081376 | tf_op jit(solution)/shard_map/all_to_all | solution.py:224
  71.2 0.0 collective-permute-done.4.other_hbm
  71.2 2.7 %shrink.1 = (bf16[16,64,128]{2,1,0:T(8,128)(2,1)S(1)}, f32[16,8,128]{2,1,0:T(8,128)S(1)}) custom-call(s32[1]{0:T(128)} %bitcast.2.core_ref, bf16[16,264,128]{2,1,0:T(8,128)(2,1)S(1)} %all-to-all-done.pay_ref, bf16[2048,256]{1,0:T(8,128)(2,1)S(1)} %bitcast.11, bf16[2048,256]{1,0:T(8,128)(2,1)} %collective-permute-done.4.other_hbm), custom_call_target="tpu_custom_call" | custom-call | tf_op jit(solution)/shard_map/shrink/pallas_call | solution.py:299
  73.9 0.0 copy-start.2
  73.9 15.6 %all_to_all.20.p_ref = bf16[16,64,128]{2,1,0:T(8,128)(2,1)S(1)} all-to-all(bf16[16,64,128]{2,1,0:T(8,128)(2,1)S(1)} %get-tuple-element.45), channel_id=1, replica_groups=mesh['z'=16,'core'=2,'y'=4,'x'=4] {'y','x'}, dimensions={0} | all-to-all | bytes 524288 | tf_op jit(solution)/shard_map/all_to_all | solution.py:224
  89.6 0.8 total.1
  90.3 3.5 %all-to-all-start.2 = ((bf16[16,64,128]{2,1,0:T(8,128)(2,1)}), bf16[16,64,128]{2,1,0:T(8,128)(2,1)S(1)}, u32[]{:S(2)}, u32[]{:S(2)}) async-start(bf16[16,64,128]{2,1,0:T(8,128)(2,1)} %total.1), calls=%async_computation.2 | async-start | bytes 524288 | tf_op jit(solution)/shard_map/all_to_all | solution.py:224
  93.9 0.3 marks.1.marks_ref
  94.2 0.0 collective-permute-done.3.refs_5_
  94.2 0.0 copy-done.2
  94.2 0.0 copy-start.4
  94.2 1.0 copy-done.4
  95.2 3.4 %base.2 = (f32[768,256]{1,0:T(8,128)S(1)}, bf16[768,256]{1,0:T(8,128)(2,1)}) custom-call(s32[1]{0:T(128)} %bitcast.1.place_ref, bf16[768,256]{1,0:T(8,128)(2,1)S(1)} %copy-done.4, bf16[768,256]{1,0:T(8,128)(2,1)} %collective-permute-done.refs_1_, bf16[768,256]{1,0:T(8,128)(2,1)} %collective-permute-done.1.refs_2_, ...), custom_call_target="tpu_custom_call" | custom-call | flops 805306368 | bytes 4194304 | tf_op jit(solution)/shard_map/base/pallas_call | solution.py:280
  98.6 0.0 collective-permute-done.5.other_hbm
  98.6 3.9 %all-to-all-done.2.s_ref = bf16[16,64,128]{2,1,0:T(8,128)(2,1)S(1)} async-done(((bf16[16,64,128]{2,1,0:T(8,128)(2,1)}), bf16[16,64,128]{2,1,0:T(8,128)(2,1)S(1)}, u32[]{:S(2)}, u32[]{:S(2)}) %all-to-all-start.2) | async-done | bytes 262176 | tf_op jit(solution)/shard_map/all_to_all | solution.py:224
  102.5 3.4 %expand.1 = bf16[16,2,64,256]{3,2,1,0:T(8,128)(2,1)} custom-call(s32[1]{0:T(128)} %bitcast.2.core_ref, bf16[16,64,128]{2,1,0:T(8,128)(2,1)S(1)} %all-to-all-done.2.s_ref, bf16[16,128,128]{2,1,0:T(8,128)(2,1)S(1)} %marks.1.marks_ref, bf16[2048,256]{1,0:T(8,128)(2,1)S(1)} %bitcast.9, bf16[2048,256]{1,0:T(8,128)(2,1)} %collective-permute-done.5.other_hbm), custom_call_target="tpu_custom_call" | custom-call | tf_op jit(solution)/shard_map/expand/pallas_call | solution.py:329
  106.0 0.0 collective-permute-done.7.refs_5_
  106.0 0.0 collective-permute-done.6.refs_4_
  106.0 8.8 %all-to-all-start.3 = ((bf16[16,2,64,256]{3,2,1,0:T(8,128)(2,1)}), bf16[16,2,64,256]{3,2,1,0:T(8,128)(2,1)S(1)}, u32[]{:S(2)}, u32[]{:S(2)}) async-start(bf16[16,2,64,256]{3,2,1,0:T(8,128)(2,1)} %expand.1), calls=%async_computation.3 | async-start | bytes 2097152 | tf_op jit(solution)/shard_map/all_to_all | solution.py:224
  114.8 1.9 %collective-permute-start.8 = (bf16[768,256]{1,0:T(8,128)(2,1)}, bf16[768,256]{1,0:T(8,128)(2,1)}, u32[]{:S(2)}, u32[]{:S(2)}) collective-permute-start(bf16[768,256]{1,0:T(8,128)(2,1)} %get-tuple-element.49), channel_id=1, source_target_pairs={{0,4},{4,8},{8,12},{12,0},{1,5},{5,9},{9,13},{13,1},{2,6},{6,10},{... | collective-permute-start | bytes 1179656 | tf_op jit(solution)/shard_map/ppermute | solution.py:240
  116.8 0.0 copy-start.5
  116.8 1.0 copy-done.5
  117.8 3.5 %base.3 = (bf16[768,256]{1,0:T(8,128)(2,1)}, bf16[768,256]{1,0:T(8,128)(2,1)}) custom-call(s32[1]{0:T(128)} %bitcast.1.place_ref, bf16[768,256]{1,0:T(8,128)(2,1)S(1)} %copy-done.5, bf16[768,256]{1,0:T(8,128)(2,1)} %collective-permute-done.refs_1_, bf16[768,256]{1,0:T(8,128)(2,1)} %collective-permute-done.1.refs_2_, ...), custom_call_target="tpu_custom_call" | custom-call | flops 805306368 | bytes 4194304 | tf_op jit(solution)/shard_map/base/pallas_call | solution.py:280
  121.3 4.2 %collective-permute-start.9 = (bf16[768,256]{1,0:T(8,128)(2,1)}, bf16[768,256]{1,0:T(8,128)(2,1)S(1)}, u32[]{:S(2)}, u32[]{:S(2)}) collective-permute-start(bf16[768,256]{1,0:T(8,128)(2,1)} %get-tuple-element.56), channel_id=1, source_target_pairs={{0,8},{4,12},{8,0},{12,4},{1,9},{5,13},{9,1},{13,5},{2,10},{6,14},... | collective-permute-start | bytes 1179656 | tf_op jit(solution)/shard_map/ppermute | solution.py:240
  125.5 3.1 %collective-permute-start.10 = (bf16[768,256]{1,0:T(8,128)(2,1)}, bf16[768,256]{1,0:T(8,128)(2,1)S(1)}, u32[]{:S(2)}, u32[]{:S(2)}) collective-permute-start(bf16[768,256]{1,0:T(8,128)(2,1)} %get-tuple-element.57), channel_id=1, source_target_pairs={{0,12},{4,0},{8,4},{12,8},{1,13},{5,1},{9,5},{13,9},{2,14},{6,2},{... | collective-permute-start | bytes 1179656 | tf_op jit(solution)/shard_map/ppermute | solution.py:240
  128.5 0.2 copy.7.dest_ref
  128.7 6.2 %collective-permute-done.8.p1_ref = bf16[768,256]{1,0:T(8,128)(2,1)} collective-permute-done((bf16[768,256]{1,0:T(8,128)(2,1)}, bf16[768,256]{1,0:T(8,128)(2,1)}, u32[]{:S(2)}, u32[]{:S(2)}) %collective-permute-start.8) | collective-permute-done | bytes 393248 | tf_op jit(solution)/shard_map/ppermute | solution.py:240
  134.9 0.0 collective-permute-done.9.p2_ref
  134.9 0.0 copy-start.6
  134.9 0.7 copy-done.6
  135.6 6.2 %collective-permute-done.10.p3_ref = bf16[768,256]{1,0:T(8,128)(2,1)S(1)} collective-permute-done((bf16[768,256]{1,0:T(8,128)(2,1)}, bf16[768,256]{1,0:T(8,128)(2,1)S(1)}, u32[]{:S(2)}, u32[]{:S(2)}) %collective-permute-start.10) | collective-permute-done | bytes 393248 | tf_op jit(solution)/shard_map/ppermute | solution.py:240
  141.8 0.0 copy-start.8
  141.9 0.8 copy-done.8
  142.6 0.0 copy-start.7
  142.6 1.0 copy-done.7
  143.6 0.0 copy-start.9
  143.6 1.0 copy-done.9
  144.6 1.2 ready.1.base_ref
  145.8 16.1 %all-to-all-done.3 = bf16[16,2,64,256]{3,2,1,0:T(8,128)(2,1)S(1)} async-done(((bf16[16,2,64,256]{3,2,1,0:T(8,128)(2,1)}), bf16[16,2,64,256]{3,2,1,0:T(8,128)(2,1)S(1)}, u32[]{:S(2)}, u32[]{:S(2)}) %all-to-all-start.3) | async-done | bytes 1048608 | tf_op jit(solution)/shard_map/all_to_all | solution.py:224
  161.9 1.8 %final.1 = bf16[768,256]{1,0:T(8,128)(2,1)} custom-call(s32[768,1]{1,0:T(8,128)S(1)} %copy.7.dest_ref, f32[768,256]{1,0:T(8,128)S(1)} %ready.1.base_ref, bf16[2048,256]{1,0:T(8,128)(2,1)S(1)} %bitcast.6), custom_call_target="tpu_custom_call" | custom-call | tf_op jit(solution)/shard_map/final/pallas_call | solution.py:355
  (1 shorter events, 0.0 us)
Async XLA Ops:
  0.0 22.4 %copy-start = (bf16[32,64,256]{2,1,0:T(8,128)(2,1)S(1)}, bf16[32,64,256]{2,1,0:T(8,128)(2,1)}, u32[]{:S(2)}) copy-start(bf16[32,64,256]{2,1,0:T(8,128)(2,1)} %param.9) | copy-start | bytes 3145732
  0.0 20.5 %copy-start.1 = (bf16[32,64,256]{2,1,0:T(8,128)(2,1)S(1)}, bf16[32,64,256]{2,1,0:T(8,128)(2,1)}, u32[]{:S(2)}) copy-start(bf16[32,64,256]{2,1,0:T(8,128)(2,1)} %param.8) | copy-start | bytes 3145732
  0.9 1.0 copy-start.3
  5.2 66.0 %all-to-all-start = ((bf16[16,264,128]{2,1,0:T(8,128)(2,1)}), bf16[16,264,128]{2,1,0:T(8,128)(2,1)S(1)}, u32[]{:S(2)}, u32[]{:S(2)}) async-start(bf16[16,264,128]{2,1,0:T(8,128)(2,1)} %get-tuple-element.34), calls=%async_computation | async-start | bytes 2162688 | tf_op jit(solution)/shard_map/all_to_all | solution.py:224
  20.5 50.7 %collective-permute-start.4 = (bf16[2048,256]{1,0:T(8,128)(2,1)S(1)}, bf16[2048,256]{1,0:T(8,128)(2,1)}, u32[]{:S(2)}, u32[]{:S(2)}) collective-permute-start(bf16[2048,256]{1,0:T(8,128)(2,1)S(1)} %bitcast.10), channel_id=1, source_target_pairs={{0,16},{16,0},{1,17},{17,1},{2,18},{18,2},{3,19},{19,3},{4,20},{20... | collective-permute-start | bytes 3145736 | tf_op jit(solution)/shard_map/ppermute | solution.py:228
  22.4 76.2 %collective-permute-start.5 = (bf16[2048,256]{1,0:T(8,128)(2,1)S(1)}, bf16[2048,256]{1,0:T(8,128)(2,1)}, u32[]{:S(2)}, u32[]{:S(2)}) collective-permute-start(bf16[2048,256]{1,0:T(8,128)(2,1)S(1)} %bitcast.7), channel_id=1, source_target_pairs={{0,16},{16,0},{1,17},{17,1},{2,18},{18,2},{3,19},{19,3},{4,20},{20... | collective-permute-start | bytes 3145736 | tf_op jit(solution)/shard_map/ppermute | solution.py:228
  24.8 14.5 %collective-permute-start.2 = (bf16[768,256]{1,0:T(8,128)(2,1)}, bf16[768,256]{1,0:T(8,128)(2,1)}, u32[]{:S(2)}, u32[]{:S(2)}) collective-permute-start(bf16[768,256]{1,0:T(8,128)(2,1)} %refs_0_.1), channel_id=1, source_target_pairs={{0,1},{1,2},{2,3},{3,0},{4,5},{5,6},{6,7},{7,4},{8,9},{9,10},{10,1... | collective-permute-start | bytes 1179656 | tf_op jit(solution)/shard_map/ppermute | solution.py:240
  28.2 20.5 %collective-permute-start.1 = (bf16[768,256]{1,0:T(8,128)(2,1)}, bf16[768,256]{1,0:T(8,128)(2,1)}, u32[]{:S(2)}, u32[]{:S(2)}) collective-permute-start(bf16[768,256]{1,0:T(8,128)(2,1)} %refs_0_.1), channel_id=1, source_target_pairs={{0,2},{1,3},{2,0},{3,1},{4,6},{5,7},{6,4},{7,5},{8,10},{9,11},{10,... | collective-permute-start | bytes 1179656 | tf_op jit(solution)/shard_map/ppermute | solution.py:240
  32.9 19.3 %collective-permute-start = (bf16[768,256]{1,0:T(8,128)(2,1)}, bf16[768,256]{1,0:T(8,128)(2,1)}, u32[]{:S(2)}, u32[]{:S(2)}) collective-permute-start(bf16[768,256]{1,0:T(8,128)(2,1)} %refs_0_.1), channel_id=1, source_target_pairs={{0,3},{1,0},{2,1},{3,2},{4,7},{5,4},{6,5},{7,6},{8,11},{9,8},{10,9... | collective-permute-start | bytes 1179656 | tf_op jit(solution)/shard_map/ppermute | solution.py:240
  39.3 54.9 %collective-permute-start.3 = (bf16[1024,256]{1,0:T(8,128)(2,1)}, bf16[1024,256]{1,0:T(8,128)(2,1)}, u32[]{:S(2)}, u32[]{:S(2)}) collective-permute-start(bf16[1024,256]{1,0:T(8,128)(2,1)} %get-tuple-element.61), channel_id=1, source_target_pairs={{0,12},{4,0},{8,4},{12,8},{1,13},{5,1},{9,5},{13,9},{2,14},{6,2},{... | collective-permute-start | bytes 1572872 | tf_op jit(solution)/shard_map/ppermute | solution.py:240
  48.7 57.3 %collective-permute-start.7 = (bf16[1024,256]{1,0:T(8,128)(2,1)}, bf16[1024,256]{1,0:T(8,128)(2,1)}, u32[]{:S(2)}, u32[]{:S(2)}) collective-permute-start(bf16[1024,256]{1,0:T(8,128)(2,1)} %get-tuple-element.59), channel_id=1, source_target_pairs={{0,4},{4,8},{8,12},{12,0},{1,5},{5,9},{9,13},{13,1},{2,6},{6,10},{... | collective-permute-start | bytes 1572872 | tf_op jit(solution)/shard_map/ppermute | solution.py:240
  52.2 53.8 %collective-permute-start.6 = (bf16[1024,256]{1,0:T(8,128)(2,1)}, bf16[1024,256]{1,0:T(8,128)(2,1)}, u32[]{:S(2)}, u32[]{:S(2)}) collective-permute-start(bf16[1024,256]{1,0:T(8,128)(2,1)} %get-tuple-element.60), channel_id=1, source_target_pairs={{0,8},{4,12},{8,0},{12,4},{1,9},{5,13},{9,1},{13,5},{2,10},{6,14},... | collective-permute-start | bytes 1572872 | tf_op jit(solution)/shard_map/ppermute | solution.py:240
  73.9 20.3 %copy-start.2 = (bf16[1024,256]{1,0:T(8,128)(2,1)S(1)}, bf16[1024,256]{1,0:T(8,128)(2,1)}, u32[]{:S(2)}) copy-start(bf16[1024,256]{1,0:T(8,128)(2,1)} %get-tuple-element.62.refs_4_) | copy-start | bytes 1572868
  90.3 12.2 %all-to-all-start.2 = ((bf16[16,64,128]{2,1,0:T(8,128)(2,1)}), bf16[16,64,128]{2,1,0:T(8,128)(2,1)S(1)}, u32[]{:S(2)}, u32[]{:S(2)}) async-start(bf16[16,64,128]{2,1,0:T(8,128)(2,1)} %total.1), calls=%async_computation.2 | async-start | bytes 524288 | tf_op jit(solution)/shard_map/all_to_all | solution.py:224
  94.2 1.0 copy-start.4
  106.0 56.0 %all-to-all-start.3 = ((bf16[16,2,64,256]{3,2,1,0:T(8,128)(2,1)}), bf16[16,2,64,256]{3,2,1,0:T(8,128)(2,1)S(1)}, u32[]{:S(2)}, u32[]{:S(2)}) async-start(bf16[16,2,64,256]{3,2,1,0:T(8,128)(2,1)} %expand.1), calls=%async_computation.3 | async-start | bytes 2097152 | tf_op jit(solution)/shard_map/all_to_all | solution.py:224
  114.8 20.1 %collective-permute-start.8 = (bf16[768,256]{1,0:T(8,128)(2,1)}, bf16[768,256]{1,0:T(8,128)(2,1)}, u32[]{:S(2)}, u32[]{:S(2)}) collective-permute-start(bf16[768,256]{1,0:T(8,128)(2,1)} %get-tuple-element.49), channel_id=1, source_target_pairs={{0,4},{4,8},{8,12},{12,0},{1,5},{5,9},{9,13},{13,1},{2,6},{6,10},{... | collective-permute-start | bytes 1179656 | tf_op jit(solution)/shard_map/ppermute | solution.py:240
  116.8 1.0 copy-start.5
  121.3 13.6 %collective-permute-start.9 = (bf16[768,256]{1,0:T(8,128)(2,1)}, bf16[768,256]{1,0:T(8,128)(2,1)S(1)}, u32[]{:S(2)}, u32[]{:S(2)}) collective-permute-start(bf16[768,256]{1,0:T(8,128)(2,1)} %get-tuple-element.56), channel_id=1, source_target_pairs={{0,8},{4,12},{8,0},{12,4},{1,9},{5,13},{9,1},{13,5},{2,10},{6,14},... | collective-permute-start | bytes 1179656 | tf_op jit(solution)/shard_map/ppermute | solution.py:240
  125.5 16.4 %collective-permute-start.10 = (bf16[768,256]{1,0:T(8,128)(2,1)}, bf16[768,256]{1,0:T(8,128)(2,1)S(1)}, u32[]{:S(2)}, u32[]{:S(2)}) collective-permute-start(bf16[768,256]{1,0:T(8,128)(2,1)} %get-tuple-element.57), channel_id=1, source_target_pairs={{0,12},{4,0},{8,4},{12,8},{1,13},{5,1},{9,5},{13,9},{2,14},{6,2},{... | collective-permute-start | bytes 1179656 | tf_op jit(solution)/shard_map/ppermute | solution.py:240
  134.9 0.7 copy-start.6
  141.8 0.8 copy-start.8
  142.6 1.0 copy-start.7
  143.6 1.0 copy-start.9

commit v8 on v5

--- a/solution.py
+++ b/solution.py
@@ -84,14 +84,17 @@
         send.wait()
 
 
-def shrink_kernel(core_ref, pay_ref, own_ref, other_hbm, out_ref, ids_ref, other_ref, sem):
+def shrink_kernel(core_ref, pay_ref, own_hbm, other_hbm, out_ref, ids_ref, pools, sem):
     core = core_ref[0]
-    bring = pltpu.make_async_copy(other_hbm, other_ref, sem.at[0])
-    bring.start()
+    brings = [
+        pltpu.make_async_copy(pool, pools.at[i], sem.at[i])
+        for i, pool in enumerate((own_hbm, other_hbm))
+    ]
+    for bring in brings:
+        bring.start()
     low = lax.broadcasted_iota(I32, (8, 128), 1) < PAIR
-    for pool_ref, c in ((own_ref, core), (other_ref, 1 - core)):
-        if pool_ref is other_ref:
-            bring.wait()
+    for i, c in enumerate((core, 1 - core)):
+        brings[i].wait()
         at = pl.multiple_of(128 * c, 128)
         for b in range(4):
             parts = []
@@ -106,14 +109,14 @@
                     low, pay_ref[z, 256:264, :].astype(F32), pay_ref[z + 1, 256:264, :].astype(F32)
                 )
                 mark = jnp.where(c == 0, both[0:1, :], both[4:5, :])
-                ids_ref[8 * c + 2 * b + j] = jnp.broadcast_to(mark, (8, 128))
+                ids_ref[pl.ds(8 * c + 2 * b + j, 1), :] = mark.astype(I32)
                 marks.append(mark)
             rows = jnp.concatenate(parts, axis=0)
             mark = jnp.broadcast_to(jnp.concatenate(marks, axis=1), (RANK, 256))
             total = jnp.zeros((RANK, 256), F32)
             for q in range(8):
                 prod = lax.dot_general(
-                    pool_ref[256 * q : 256 * q + 256, :], rows, NT, preferred_element_type=F32
+                    pools[i, 256 * q : 256 * q + 256, :], rows, NT, preferred_element_type=F32
                 )
                 for a in range(4):
                     total = jnp.where(mark == 4 * q + a, prod[64 * a : 64 * a + 64], total)
@@ -121,7 +124,7 @@
             out_ref[8 * c + 2 * b + 1] = total[:, 128:256].astype(BF)
 
 
-def sum_kernel(p_ref, out_ref):
+def sum_kernel(p_ref, pool_hbm, out_ref):
     total = p_ref[0].astype(F32)
     for t in range(1, TENSOR):
         total = total + p_ref[t].astype(F32)
@@ -130,47 +133,39 @@
         out_ref[t] = mine
 
 
-def marks_kernel(ids_ref, pool_hbm, out_ref):
-    high = (lax.broadcasted_iota(I32, (128, 128), 1) >= RANK).astype(F32)
-    for t in range(TENSOR):
-        column = jnp.broadcast_to(ids_ref[t][0:1], (128, 128)).T
-        out_ref[t] = (column - high).astype(BF)
-
-
 def expand_kernel(
-    core_ref, s_ref, marks_ref, own_ref, other_hbm, out_hbm, other_ref, rows_ref, sem, out_sem
+    core_ref, slot_ref, s_ref, own_ref, other_hbm, out_hbm, other_ref, rows_ref, sem, out_sem
 ):
     core = core_ref[0]
     bring = pltpu.make_async_copy(other_hbm, other_ref, sem.at[0])
     bring.start()
+    place = (lax.broadcasted_iota(I32, (128, 256), 0) & (PAIR - 1)) >> 4
+    mine = place == lax.broadcasted_iota(I32, (128, 256), 1) >> 6
     sends = []
     for i, (pool_ref, c) in enumerate(((own_ref, core), (other_ref, 1 - core))):
         if i:
             bring.wait()
-        for b in range(4):
-            at = 8 * c + 2 * b
-            s, mark = [], []
+        for b in range(8):
+            at = 8 * c + b
+            s = s_ref[at].astype(F32)
+            s = jnp.concatenate([s, s], axis=0).T
+            s = jnp.where(mine, jnp.concatenate([s, s], axis=1), 0.0).astype(BF)
             for k in range(2):
-                one = s_ref[at + k].astype(F32)
-                s.append(jnp.concatenate([one, one], axis=0).T.astype(BF))
-                mark.append(marks_ref[at + k])
-            s, mark = jnp.concatenate(s, axis=0), jnp.concatenate(mark, axis=0)
-            m = jnp.concatenate(
-                [
-                    jnp.where(mark == jnp.asarray(2 * j, BF), s, jnp.zeros_like(s))
-                    for j in range(HELD // 2)
-                ],
-                axis=1,
-            )
-            e = jnp.dot(m, pool_ref[...], preferred_element_type=F32)
-            part = pl.ds(4 * b, 4)
-            rows_ref[i, part] = e.astype(BF).reshape(4, PAIR, WIDTH)
-            sends.append(
-                pltpu.make_async_copy(
-                    rows_ref.at[i, part], out_hbm.at[part, c], out_sem.at[4 * i + b]
+                named = []
+                for q in range(SLOTS):
+                    row = pl.multiple_of(slot_ref[at, PAIR * k + RPA * q] * RANK, RANK)
+                    named.append(pool_ref[pl.ds(row, RANK), :])
+                factors = jnp.concatenate(named, axis=0)
+                e = jnp.dot(s[64 * k : 64 * k + 64], factors, preferred_element_type=F32)
+                rows_ref[i, 2 * b + k] = e.astype(BF)
+            if b % 2:
+                part = pl.ds(2 * b - 2, 4)
+                sends.append(
+                    pltpu.make_async_copy(
+                        rows_ref.at[i, part], out_hbm.at[part, c], out_sem.at[4 * i + b // 2]
+                    )
                 )
-            )
-            sends[-1].start()
+                sends[-1].start()
     for send in sends:
         send.wait()
 
@@ -290,35 +285,27 @@
         shrink_kernel,
         out_shape=(
             jax.ShapeDtypeStruct((TENSOR, RANK, 128), BF),
-            jax.ShapeDtypeStruct((TENSOR, 8, 128), F32),
+            jax.ShapeDtypeStruct((TENSOR, 128), I32),
         ),
-        in_specs=[scalar()] + vmem(2) + hbm(1),
+        in_specs=[scalar()] + vmem(1) + hbm(2),
         out_specs=tuple(vmem(2)),
-        scratch_shapes=[pltpu.VMEM((HELD * RANK, WIDTH), BF), pltpu.SemaphoreType.DMA((1,))],
+        scratch_shapes=[pltpu.VMEM((2, HELD * RANK, WIDTH), BF), pltpu.SemaphoreType.DMA((2,))],
         compiler_params=params(),
         name="shrink",
     )(core, arrived, a_own, a_other)
     summed = pl.pallas_call(
         sum_kernel,
         out_shape=jax.ShapeDtypeStruct((TENSOR, RANK, 128), BF),
-        in_specs=vmem(1),
-        out_specs=pl.BlockSpec(memory_space=pltpu.VMEM),
-        compiler_params=params(),
-        name="total",
-    )(exchange(partial, tensor))
-    shrunk = exchange(summed, tensor)
-    marks = pl.pallas_call(
-        marks_kernel,
-        out_shape=jax.ShapeDtypeStruct((TENSOR, 128, 128), BF),
         in_specs=vmem(1) + hbm(1),
         out_specs=pl.BlockSpec(memory_space=pltpu.VMEM),
         compiler_params=params(),
-        name="marks",
-    )(ids, b_own)
+        name="total",
+    )(exchange(partial, tensor), b_own)
+    shrunk = exchange(summed, tensor)
     expanded = pl.pallas_call(
         expand_kernel,
         out_shape=jax.ShapeDtypeStruct((CHIPS, 2, PAIR, WIDTH), BF),
-        in_specs=[scalar()] + vmem(3) + hbm(1),
+        in_specs=[scalar(), scalar()] + vmem(2) + hbm(1),
         out_specs=pl.BlockSpec(memory_space=pltpu.HBM),
         scratch_shapes=[
             pltpu.VMEM((HELD * RANK, WIDTH), BF),
@@ -328,7 +315,7 @@
         ],
         compiler_params=params(),
         name="expand",
-    )(core, shrunk, marks, b_own, b_other)
+    )(core, ids, shrunk, b_own, b_other)
     p0, p1, p2, p3, expanded = lax.optimization_barrier((*parts, expanded))
     back = exchange(expanded, "z").reshape(BUCKETS, WIDTH)
     sums = [turn(p, "y", s) for s, p in ((1, p1), (2, p2), (3, p3))]

time: 165 us -> 164 us (level)
  transfers between devices with their start and end apart: 14 -> 14, of which waited for: 6 -> 6; matrix products, arithmetic and copies ran while one was open for 2% -> 2% of each run, Pallas kernels for 6% -> 5%
where the time goes in v8:
time: 164 us; the launch traced here: 163 us
  starting transfers between devices  61.8 us (38%)
  waiting for transfers between devices  60.7 us (37%)
  Pallas kernels  17.3 us (11%)
  blocking collectives  15.7 us (10%)
  local copies, waits for them, and re-layouts  6.58 us (4%)
    all_to_all x3, waiting for transfers between devices, exchange(): return lax.all_to_all(x, axis, split_axis=0, concat_axis=0, tiled=True)  41.7 us
    ppermute x9, starting transfers between devices, turn(): return lax.ppermute(x, axis, [(i, (i + step) % 4) for i in range(4)])  30.5 us
    all_to_all x3, starting transfers between devices, exchange(): return lax.all_to_all(x, axis, split_axis=0, concat_axis=0, tiled=True)  27.5 us
    ppermute x9, waiting for transfers between devices, turn(): return lax.ppermute(x, axis, [(i, (i + step) % 4) for i in range(4)])  19 us
    all_to_all x1, blocking collectives, exchange(): return lax.all_to_all(x, axis, split_axis=0, concat_axis=0, tiled=True)  15.7 us
    pallas_call x1, Pallas kernels, body(): pl.pallas_call(base_kernel, out_shape=tuple((jax.ShapeDtypeStruct((ROWS,...  4.49 us
    pallas_call x1, Pallas kernels, body(): pl.pallas_call(pack_kernel, out_shape=(jax.ShapeDtypeStruct((CHIPS, PAY,...  3.92 us
    ppermute x2, starting transfers between devices, sibling(): return lax.ppermute(x, 'core', [(0, 1), (1, 0)])  3.84 us
  transfers between devices with their start and end apart: 14, of which 6 were waited for; matrix products, arithmetic and copies ran while one was open for 2% of the time, Pallas kernels for 5%

profile of v8, /device:TPU:32, one launch (start us, length us, event | category | flops | bytes accessed | tf_op | source)
XLA Modules:
  0.0 163.2 jit_solution(12278329166835054799)
XLA Ops:
  0.0 0.0 copy-start.1
  0.0 0.0 copy-start
  0.0 0.9 pad_add_fusion
  0.9 3.9 %pack.1 = (bf16[16,264,128]{2,1,0:T(8,128)(2,1)}, s32[1,768]{1,0:T(1,128)S(1)}) custom-call(s32[1,1792]{1,0:T(1,128)S(1)} %reshape.21.table_ref, bf16[768,256]{1,0:T(8,128)(2,1)} %refs_0_), custom_call_target="tpu_custom_call" | custom-call | tf_op jit(solution)/shard_map/pack/pallas_call | solution.py:239
  4.8 15.2 %all-to-all-start = ((bf16[16,264,128]{2,1,0:T(8,128)(2,1)}), bf16[16,264,128]{2,1,0:T(8,128)(2,1)S(1)}, u32[]{:S(2)}, u32[]{:S(2)}) async-start(bf16[16,264,128]{2,1,0:T(8,128)(2,1)} %get-tuple-element.31), calls=%async_computation | async-start | bytes 2162688 | tf_op jit(solution)/shard_map/all_to_all | solution.py:216
  20.0 0.0 copy-done.1
  20.0 1.9 %collective-permute-start.6 = (bf16[2048,256]{1,0:T(8,128)(2,1)S(1)}, bf16[2048,256]{1,0:T(8,128)(2,1)}, u32[]{:S(2)}, u32[]{:S(2)}) collective-permute-start(bf16[2048,256]{1,0:T(8,128)(2,1)S(1)} %bitcast.10), channel_id=1, source_target_pairs={{0,16},{16,0},{1,17},{17,1},{2,18},{18,2},{3,19},{19,3},{4,20},{20... | collective-permute-start | bytes 3145736 | tf_op jit(solution)/shard_map/ppermute | solution.py:220
  22.0 4.7 %collective-permute-start = (bf16[768,256]{1,0:T(8,128)(2,1)}, bf16[768,256]{1,0:T(8,128)(2,1)}, u32[]{:S(2)}, u32[]{:S(2)}) collective-permute-start(bf16[768,256]{1,0:T(8,128)(2,1)} %refs_0_), channel_id=1, source_target_pairs={{0,3},{1,0},{2,1},{3,2},{4,7},{5,4},{6,5},{7,6},{8,11},{9,8},{10,9... | collective-permute-start | bytes 1179656 | tf_op jit(solution)/shard_map/ppermute | solution.py:232
  26.6 2.7 %collective-permute-start.1 = (bf16[768,256]{1,0:T(8,128)(2,1)}, bf16[768,256]{1,0:T(8,128)(2,1)}, u32[]{:S(2)}, u32[]{:S(2)}) collective-permute-start(bf16[768,256]{1,0:T(8,128)(2,1)} %refs_0_), channel_id=1, source_target_pairs={{0,2},{1,3},{2,0},{3,1},{4,6},{5,7},{6,4},{7,5},{8,10},{9,11},{10,... | collective-permute-start | bytes 1179656 | tf_op jit(solution)/shard_map/ppermute | solution.py:232
  29.3 0.0 copy-done
  29.4 1.9 %collective-permute-start.7 = (bf16[2048,256]{1,0:T(8,128)(2,1)S(1)}, bf16[2048,256]{1,0:T(8,128)(2,1)}, u32[]{:S(2)}, u32[]{:S(2)}) collective-permute-start(bf16[2048,256]{1,0:T(8,128)(2,1)S(1)} %bitcast.6), channel_id=1, source_target_pairs={{0,16},{16,0},{1,17},{17,1},{2,18},{18,2},{3,19},{19,3},{4,20},{20... | collective-permute-start | bytes 3145736 | tf_op jit(solution)/shard_map/ppermute | solution.py:220
  31.4 2.9 %constant_dynamic-slice_fusion = (bf16[1024,256]{1,0:T(8,128)(2,1)}, bf16[1024,256]{1,0:T(8,128)(2,1)}, bf16[1024,256]{1,0:T(8,128)(2,1)}, bf16[1024,256]{1,0:T(8,128)(2,1)}) fusion(bf16[4096,256]{1,0:T(8,128)(2,1)} %param.7, s32[]{:T(128)S(6)} %select_n.38, s32[]{:T(128)S(6)} %select_n.36, s32[]{:T(128)S(6)} %select_n.34, s32[]{:T(128)S(6)} %select_n.32), kind=kLoop, calls=%fused_computation.1 | loop fusion | bytes 4194320 | tf_op jit(solution)/shard_map/dynamic_slice | solution.py:266
  34.3 4.9 %collective-permute-start.3 = (bf16[1024,256]{1,0:T(8,128)(2,1)}, bf16[1024,256]{1,0:T(8,128)(2,1)}, u32[]{:S(2)}, u32[]{:S(2)}) collective-permute-start(bf16[1024,256]{1,0:T(8,128)(2,1)} %get-tuple-element.43), channel_id=1, source_target_pairs={{0,12},{4,0},{8,4},{12,8},{1,13},{5,1},{9,5},{13,9},{2,14},{6,2},{... | collective-permute-start | bytes 1572872 | tf_op jit(solution)/shard_map/ppermute | solution.py:232
  39.2 5.2 %collective-permute-done.refs_1_ = bf16[768,256]{1,0:T(8,128)(2,1)} collective-permute-done((bf16[768,256]{1,0:T(8,128)(2,1)}, bf16[768,256]{1,0:T(8,128)(2,1)}, u32[]{:S(2)}, u32[]{:S(2)}) %collective-permute-start) | collective-permute-done | bytes 393248 | tf_op jit(solution)/shard_map/ppermute | solution.py:232
  44.4 5.1 %collective-permute-start.4 = (bf16[1024,256]{1,0:T(8,128)(2,1)}, bf16[1024,256]{1,0:T(8,128)(2,1)}, u32[]{:S(2)}, u32[]{:S(2)}) collective-permute-start(bf16[1024,256]{1,0:T(8,128)(2,1)} %get-tuple-element.42), channel_id=1, source_target_pairs={{0,8},{4,12},{8,0},{12,4},{1,9},{5,13},{9,1},{13,5},{2,10},{6,14},... | collective-permute-start | bytes 1572872 | tf_op jit(solution)/shard_map/ppermute | solution.py:232
  49.5 0.0 collective-permute-done.1.refs_2_
  49.5 2.6 %collective-permute-start.5 = (bf16[1024,256]{1,0:T(8,128)(2,1)}, bf16[1024,256]{1,0:T(8,128)(2,1)}, u32[]{:S(2)}, u32[]{:S(2)}) collective-permute-start(bf16[1024,256]{1,0:T(8,128)(2,1)} %get-tuple-element.41), channel_id=1, source_target_pairs={{0,4},{4,8},{8,12},{12,0},{1,5},{5,9},{9,13},{13,1},{2,6},{6,10},{... | collective-permute-start | bytes 1572872 | tf_op jit(solution)/shard_map/ppermute | solution.py:232
  52.1 0.0 collective-permute-done.6.other_hbm
  52.1 1.9 %collective-permute-start.2 = (bf16[768,256]{1,0:T(8,128)(2,1)}, bf16[768,256]{1,0:T(8,128)(2,1)}, u32[]{:S(2)}, u32[]{:S(2)}) collective-permute-start(bf16[768,256]{1,0:T(8,128)(2,1)} %refs_0_), channel_id=1, source_target_pairs={{0,1},{1,2},{2,3},{3,0},{4,5},{5,6},{6,7},{7,4},{8,9},{9,10},{10,1... | collective-permute-start | bytes 1179656 | tf_op jit(solution)/shard_map/ppermute | solution.py:232
  54.1 16.7 %all-to-all-done.pay_ref = bf16[16,264,128]{2,1,0:T(8,128)(2,1)S(1)} async-done(((bf16[16,264,128]{2,1,0:T(8,128)(2,1)}), bf16[16,264,128]{2,1,0:T(8,128)(2,1)S(1)}, u32[]{:S(2)}, u32[]{:S(2)}) %all-to-all-start) | async-done | bytes 1081376 | tf_op jit(solution)/shard_map/all_to_all | solution.py:216
  70.7 2.7 %shrink.1 = (bf16[16,64,128]{2,1,0:T(8,128)(2,1)S(1)}, s32[16,128]{1,0:T(8,128)S(1)}) custom-call(s32[1]{0:T(128)} %bitcast.2.core_ref, bf16[16,264,128]{2,1,0:T(8,128)(2,1)S(1)} %all-to-all-done.pay_ref, bf16[2048,256]{1,0:T(8,128)(2,1)S(1)} %bitcast.11, bf16[2048,256]{1,0:T(8,128)(2,1)} %collective-permute-done.6.other_hbm), custom_call_target="tpu_custom_call" | custom-call | tf_op jit(solution)/shard_map/shrink/pallas_call | solution.py:284
  73.4 0.0 copy-start.2
  73.4 15.7 %all_to_all.20.p_ref = bf16[16,64,128]{2,1,0:T(8,128)(2,1)S(1)} all-to-all(bf16[16,64,128]{2,1,0:T(8,128)(2,1)S(1)} %get-tuple-element.34), channel_id=1, replica_groups=mesh['z'=16,'core'=2,'y'=4,'x'=4] {'y','x'}, dimensions={0} | all-to-all | bytes 524288 | tf_op jit(solution)/shard_map/all_to_all | solution.py:216
  89.1 0.8 total.1
  89.9 3.5 %all-to-all-start.2 = ((bf16[16,64,128]{2,1,0:T(8,128)(2,1)}), bf16[16,64,128]{2,1,0:T(8,128)(2,1)S(1)}, u32[]{:S(2)}, u32[]{:S(2)}) async-start(bf16[16,64,128]{2,1,0:T(8,128)(2,1)} %total.1), calls=%async_computation.2 | async-start | bytes 524288 | tf_op jit(solution)/shard_map/all_to_all | solution.py:216
  93.4 0.0 collective-permute-done.2.refs_3_
  93.4 0.0 collective-permute-done.3.refs_5_
  93.4 0.0 collective-permute-done.4.refs_6_
  93.4 0.0 collective-permute-done.5.refs_7_
  93.4 0.0 copy-done.2
  93.5 4.5 %base.1 = (f32[768,256]{1,0:T(8,128)S(1)}, bf16[768,256]{1,0:T(8,128)(2,1)}, bf16[768,256]{1,0:T(8,128)(2,1)}, bf16[768,256]{1,0:T(8,128)(2,1)}) custom-call(s32[1]{0:T(128)} %bitcast.1.place_ref, bf16[768,256]{1,0:T(8,128)(2,1)} %refs_0_, bf16[768,256]{1,0:T(8,128)(2,1)} %collective-permute-done.refs_1_, bf16[768,256]{1,0:T(8,128)(2,1)} %collective-permute-done.1.refs_2_, ...), custom_call_target="tpu_custom_call" | custom-call | flops 1610612736 | bytes 6291456 | tf_op jit(solution)/shard_map/base/pallas_call | solution.py:268
  98.0 0.0 collective-permute-done.7.other_hbm
  98.0 4.1 %all-to-all-done.2.s_ref = bf16[16,64,128]{2,1,0:T(8,128)(2,1)S(1)} async-done(((bf16[16,64,128]{2,1,0:T(8,128)(2,1)}), bf16[16,64,128]{2,1,0:T(8,128)(2,1)S(1)}, u32[]{:S(2)}, u32[]{:S(2)}) %all-to-all-start.2) | async-done | bytes 262176 | tf_op jit(solution)/shard_map/all_to_all | solution.py:216
  102.1 3.6 %expand.1 = bf16[16,2,64,256]{3,2,1,0:T(8,128)(2,1)} custom-call(s32[1]{0:T(128)} %bitcast.2.core_ref, s32[16,128]{1,0:T(8,128)S(1)} %get-tuple-element.33.slot_ref, bf16[16,64,128]{2,1,0:T(8,128)(2,1)S(1)} %all-to-all-done.2.s_ref, bf16[2048,256]{1,0:T(8,128)(2,1)S(1)} %bitcast.8, bf16[2048,256]{1,0:T(8,128)(2,1)} %collective-permute-done.7.other_hbm), custom_call_target="tpu_custom_call" | custom-call | tf_op jit(solution)/shard_map/expand/pallas_call | solution.py:305
  105.6 8.7 %all-to-all-start.3 = ((bf16[16,2,64,256]{3,2,1,0:T(8,128)(2,1)}), bf16[16,2,64,256]{3,2,1,0:T(8,128)(2,1)S(1)}, u32[]{:S(2)}, u32[]{:S(2)}) async-start(bf16[16,2,64,256]{3,2,1,0:T(8,128)(2,1)} %expand.1), calls=%async_computation.3 | async-start | bytes 2097152 | tf_op jit(solution)/shard_map/all_to_all | solution.py:216
  114.4 2.7 %collective-permute-start.10 = (bf16[768,256]{1,0:T(8,128)(2,1)}, bf16[768,256]{1,0:T(8,128)(2,1)S(1)}, u32[]{:S(2)}, u32[]{:S(2)}) collective-permute-start(bf16[768,256]{1,0:T(8,128)(2,1)} %get-tuple-element.39), channel_id=1, source_target_pairs={{0,12},{4,0},{8,4},{12,8},{1,13},{5,1},{9,5},{13,9},{2,14},{6,2},{... | collective-permute-start | bytes 1179656 | tf_op jit(solution)/shard_map/ppermute | solution.py:232
  117.1 3.1 %collective-permute-start.8 = (bf16[768,256]{1,0:T(8,128)(2,1)}, bf16[768,256]{1,0:T(8,128)(2,1)S(1)}, u32[]{:S(2)}, u32[]{:S(2)}) collective-permute-start(bf16[768,256]{1,0:T(8,128)(2,1)} %get-tuple-element.37), channel_id=1, source_target_pairs={{0,4},{4,8},{8,12},{12,0},{1,5},{5,9},{9,13},{13,1},{2,6},{6,10},{... | collective-permute-start | bytes 1179656 | tf_op jit(solution)/shard_map/ppermute | solution.py:232
  120.2 2.7 %collective-permute-start.9 = (bf16[768,256]{1,0:T(8,128)(2,1)}, bf16[768,256]{1,0:T(8,128)(2,1)S(1)}, u32[]{:S(2)}, u32[]{:S(2)}) collective-permute-start(bf16[768,256]{1,0:T(8,128)(2,1)} %get-tuple-element.38), channel_id=1, source_target_pairs={{0,8},{4,12},{8,0},{12,4},{1,9},{5,13},{9,1},{13,5},{2,10},{6,14},... | collective-permute-start | bytes 1179656 | tf_op jit(solution)/shard_map/ppermute | solution.py:232
  122.9 0.2 copy.7.dest_ref
  123.1 3.6 %collective-permute-done.10.p3_ref = bf16[768,256]{1,0:T(8,128)(2,1)S(1)} collective-permute-done((bf16[768,256]{1,0:T(8,128)(2,1)}, bf16[768,256]{1,0:T(8,128)(2,1)S(1)}, u32[]{:S(2)}, u32[]{:S(2)}) %collective-permute-start.10) | collective-permute-done | bytes 393248 | tf_op jit(solution)/shard_map/ppermute | solution.py:232
  126.7 10.1 %collective-permute-done.8.p1_ref = bf16[768,256]{1,0:T(8,128)(2,1)S(1)} collective-permute-done((bf16[768,256]{1,0:T(8,128)(2,1)}, bf16[768,256]{1,0:T(8,128)(2,1)S(1)}, u32[]{:S(2)}, u32[]{:S(2)}) %collective-permute-start.8) | collective-permute-done | bytes 393248 | tf_op jit(solution)/shard_map/ppermute | solution.py:232
  136.9 0.0 copy-start.3
  136.9 0.7 copy-done.3
  137.6 0.0 collective-permute-done.9.p2_ref
  137.6 0.0 copy-start.5
  137.6 0.7 copy-done.5
  138.4 0.0 copy-start.4
  138.4 1.0 copy-done.4
  139.4 0.0 copy-start.6
  139.4 1.0 copy-done.6
  140.4 0.2 ready.1.base_ref
  140.5 20.9 %all-to-all-done.3 = bf16[16,2,64,256]{3,2,1,0:T(8,128)(2,1)S(1)} async-done(((bf16[16,2,64,256]{3,2,1,0:T(8,128)(2,1)}), bf16[16,2,64,256]{3,2,1,0:T(8,128)(2,1)S(1)}, u32[]{:S(2)}, u32[]{:S(2)}) %all-to-all-start.3) | async-done | bytes 1048608 | tf_op jit(solution)/shard_map/all_to_all | solution.py:216
  161.4 1.8 %final.1 = bf16[768,256]{1,0:T(8,128)(2,1)} custom-call(s32[768,1]{1,0:T(8,128)S(1)} %copy.7.dest_ref, f32[768,256]{1,0:T(8,128)S(1)} %ready.1.base_ref, bf16[2048,256]{1,0:T(8,128)(2,1)S(1)} %bitcast.9), custom_call_target="tpu_custom_call" | custom-call | tf_op jit(solution)/shard_map/final/pallas_call | solution.py:330
  (1 shorter events, 0.0 us)
Async XLA Ops:
  0.0 20.0 %copy-start.1 = (bf16[32,64,256]{2,1,0:T(8,128)(2,1)S(1)}, bf16[32,64,256]{2,1,0:T(8,128)(2,1)}, u32[]{:S(2)}) copy-start(bf16[32,64,256]{2,1,0:T(8,128)(2,1)} %param.8) | copy-start | bytes 3145732
  0.0 29.3 %copy-start = (bf16[32,64,256]{2,1,0:T(8,128)(2,1)S(1)}, bf16[32,64,256]{2,1,0:T(8,128)(2,1)}, u32[]{:S(2)}) copy-start(bf16[32,64,256]{2,1,0:T(8,128)(2,1)} %param.9) | copy-start | bytes 3145732
  4.8 65.9 %all-to-all-start = ((bf16[16,264,128]{2,1,0:T(8,128)(2,1)}), bf16[16,264,128]{2,1,0:T(8,128)(2,1)S(1)}, u32[]{:S(2)}, u32[]{:S(2)}) async-start(bf16[16,264,128]{2,1,0:T(8,128)(2,1)} %get-tuple-element.31), calls=%async_computation | async-start | bytes 2162688 | tf_op jit(solution)/shard_map/all_to_all | solution.py:216
  20.0 32.1 %collective-permute-start.6 = (bf16[2048,256]{1,0:T(8,128)(2,1)S(1)}, bf16[2048,256]{1,0:T(8,128)(2,1)}, u32[]{:S(2)}, u32[]{:S(2)}) collective-permute-start(bf16[2048,256]{1,0:T(8,128)(2,1)S(1)} %bitcast.10), channel_id=1, source_target_pairs={{0,16},{16,0},{1,17},{17,1},{2,18},{18,2},{3,19},{19,3},{4,20},{20... | collective-permute-start | bytes 3145736 | tf_op jit(solution)/shard_map/ppermute | solution.py:220
  22.0 22.5 %collective-permute-start = (bf16[768,256]{1,0:T(8,128)(2,1)}, bf16[768,256]{1,0:T(8,128)(2,1)}, u32[]{:S(2)}, u32[]{:S(2)}) collective-permute-start(bf16[768,256]{1,0:T(8,128)(2,1)} %refs_0_), channel_id=1, source_target_pairs={{0,3},{1,0},{2,1},{3,2},{4,7},{5,4},{6,5},{7,6},{8,11},{9,8},{10,9... | collective-permute-start | bytes 1179656 | tf_op jit(solution)/shard_map/ppermute | solution.py:232
  26.6 22.9 %collective-permute-start.1 = (bf16[768,256]{1,0:T(8,128)(2,1)}, bf16[768,256]{1,0:T(8,128)(2,1)}, u32[]{:S(2)}, u32[]{:S(2)}) collective-permute-start(bf16[768,256]{1,0:T(8,128)(2,1)} %refs_0_), channel_id=1, source_target_pairs={{0,2},{1,3},{2,0},{3,1},{4,6},{5,7},{6,4},{7,5},{8,10},{9,11},{10,... | collective-permute-start | bytes 1179656 | tf_op jit(solution)/shard_map/ppermute | solution.py:232
  29.4 68.6 %collective-permute-start.7 = (bf16[2048,256]{1,0:T(8,128)(2,1)S(1)}, bf16[2048,256]{1,0:T(8,128)(2,1)}, u32[]{:S(2)}, u32[]{:S(2)}) collective-permute-start(bf16[2048,256]{1,0:T(8,128)(2,1)S(1)} %bitcast.6), channel_id=1, source_target_pairs={{0,16},{16,0},{1,17},{17,1},{2,18},{18,2},{3,19},{19,3},{4,20},{20... | collective-permute-start | bytes 3145736 | tf_op jit(solution)/shard_map/ppermute | solution.py:220
  34.3 59.2 %collective-permute-start.3 = (bf16[1024,256]{1,0:T(8,128)(2,1)}, bf16[1024,256]{1,0:T(8,128)(2,1)}, u32[]{:S(2)}, u32[]{:S(2)}) collective-permute-start(bf16[1024,256]{1,0:T(8,128)(2,1)} %get-tuple-element.43), channel_id=1, source_target_pairs={{0,12},{4,0},{8,4},{12,8},{1,13},{5,1},{9,5},{13,9},{2,14},{6,2},{... | collective-permute-start | bytes 1572872 | tf_op jit(solution)/shard_map/ppermute | solution.py:232
  44.4 49.0 %collective-permute-start.4 = (bf16[1024,256]{1,0:T(8,128)(2,1)}, bf16[1024,256]{1,0:T(8,128)(2,1)}, u32[]{:S(2)}, u32[]{:S(2)}) collective-permute-start(bf16[1024,256]{1,0:T(8,128)(2,1)} %get-tuple-element.42), channel_id=1, source_target_pairs={{0,8},{4,12},{8,0},{12,4},{1,9},{5,13},{9,1},{13,5},{2,10},{6,14},... | collective-permute-start | bytes 1572872 | tf_op jit(solution)/shard_map/ppermute | solution.py:232
  49.5 43.9 %collective-permute-start.5 = (bf16[1024,256]{1,0:T(8,128)(2,1)}, bf16[1024,256]{1,0:T(8,128)(2,1)}, u32[]{:S(2)}, u32[]{:S(2)}) collective-permute-start(bf16[1024,256]{1,0:T(8,128)(2,1)} %get-tuple-element.41), channel_id=1, source_target_pairs={{0,4},{4,8},{8,12},{12,0},{1,5},{5,9},{9,13},{13,1},{2,6},{6,10},{... | collective-permute-start | bytes 1572872 | tf_op jit(solution)/shard_map/ppermute | solution.py:232
  52.1 41.3 %collective-permute-start.2 = (bf16[768,256]{1,0:T(8,128)(2,1)}, bf16[768,256]{1,0:T(8,128)(2,1)}, u32[]{:S(2)}, u32[]{:S(2)}) collective-permute-start(bf16[768,256]{1,0:T(8,128)(2,1)} %refs_0_), channel_id=1, source_target_pairs={{0,1},{1,2},{2,3},{3,0},{4,5},{5,6},{6,7},{7,4},{8,9},{9,10},{10,1... | collective-permute-start | bytes 1179656 | tf_op jit(solution)/shard_map/ppermute | solution.py:232
  73.4 20.0 %copy-start.2 = (bf16[1024,256]{1,0:T(8,128)(2,1)S(1)}, bf16[1024,256]{1,0:T(8,128)(2,1)}, u32[]{:S(2)}) copy-start(bf16[1024,256]{1,0:T(8,128)(2,1)} %get-tuple-element.44.refs_4_) | copy-start | bytes 1572868
  89.9 12.2 %all-to-all-start.2 = ((bf16[16,64,128]{2,1,0:T(8,128)(2,1)}), bf16[16,64,128]{2,1,0:T(8,128)(2,1)S(1)}, u32[]{:S(2)}, u32[]{:S(2)}) async-start(bf16[16,64,128]{2,1,0:T(8,128)(2,1)} %total.1), calls=%async_computation.2 | async-start | bytes 524288 | tf_op jit(solution)/shard_map/all_to_all | solution.py:216
  105.6 55.8 %all-to-all-start.3 = ((bf16[16,2,64,256]{3,2,1,0:T(8,128)(2,1)}), bf16[16,2,64,256]{3,2,1,0:T(8,128)(2,1)S(1)}, u32[]{:S(2)}, u32[]{:S(2)}) async-start(bf16[16,2,64,256]{3,2,1,0:T(8,128)(2,1)} %expand.1), calls=%async_computation.3 | async-start | bytes 2097152 | tf_op jit(solution)/shard_map/all_to_all | solution.py:216
  114.4 12.4 %collective-permute-start.10 = (bf16[768,256]{1,0:T(8,128)(2,1)}, bf16[768,256]{1,0:T(8,128)(2,1)S(1)}, u32[]{:S(2)}, u32[]{:S(2)}) collective-permute-start(bf16[768,256]{1,0:T(8,128)(2,1)} %get-tuple-element.39), channel_id=1, source_target_pairs={{0,12},{4,0},{8,4},{12,8},{1,13},{5,1},{9,5},{13,9},{2,14},{6,2},{... | collective-permute-start | bytes 1179656 | tf_op jit(solution)/shard_map/ppermute | solution.py:232
  117.1 19.8 %collective-permute-start.8 = (bf16[768,256]{1,0:T(8,128)(2,1)}, bf16[768,256]{1,0:T(8,128)(2,1)S(1)}, u32[]{:S(2)}, u32[]{:S(2)}) collective-permute-start(bf16[768,256]{1,0:T(8,128)(2,1)} %get-tuple-element.37), channel_id=1, source_target_pairs={{0,4},{4,8},{8,12},{12,0},{1,5},{5,9},{9,13},{13,1},{2,6},{6,10},{... | collective-permute-start | bytes 1179656 | tf_op jit(solution)/shard_map/ppermute | solution.py:232
  120.2 17.4 %collective-permute-start.9 = (bf16[768,256]{1,0:T(8,128)(2,1)}, bf16[768,256]{1,0:T(8,128)(2,1)S(1)}, u32[]{:S(2)}, u32[]{:S(2)}) collective-permute-start(bf16[768,256]{1,0:T(8,128)(2,1)} %get-tuple-element.38), channel_id=1, source_target_pairs={{0,8},{4,12},{8,0},{12,4},{1,9},{5,13},{9,1},{13,5},{2,10},{6,14},... | collective-permute-start | bytes 1179656 | tf_op jit(solution)/shard_map/ppermute | solution.py:232
  136.9 0.7 copy-start.3
  137.6 0.7 copy-start.5
  138.4 1.0 copy-start.4
  139.4 1.0 copy-start.6

commit v9 on v8

--- a/solution.py
+++ b/solution.py
@@ -134,22 +134,33 @@
 
 
 def expand_kernel(
-    core_ref, slot_ref, s_ref, own_ref, other_hbm, out_hbm, other_ref, rows_ref, sem, out_sem
+    core_ref, ids_ref, s_ref, own_ref, other_hbm, out_hbm, slot_ref, mine_ref, other_ref, rows_ref, sem, out_sem
 ):
     core = core_ref[0]
-    bring = pltpu.make_async_copy(other_hbm, other_ref, sem.at[0])
-    bring.start()
+    slots = pltpu.make_async_copy(ids_ref, slot_ref, sem.at[4])
+    slots.start()
+    quarters = [pl.ds(512 * k, 512) for k in range(4)]
+    brings = [
+        pltpu.make_async_copy(other_hbm.at[part], other_ref.at[part], sem.at[k])
+        for k, part in enumerate(quarters)
+    ]
+    for bring in brings:
+        bring.start()
     place = (lax.broadcasted_iota(I32, (128, 256), 0) & (PAIR - 1)) >> 4
     mine = place == lax.broadcasted_iota(I32, (128, 256), 1) >> 6
+    for t in range(TENSOR):
+        s = s_ref[t].astype(F32)
+        s = jnp.concatenate([s, s], axis=0).T
+        mine_ref[t] = jnp.where(mine, jnp.concatenate([s, s], axis=1), 0.0).astype(BF)
+    slots.wait()
     sends = []
     for i, (pool_ref, c) in enumerate(((own_ref, core), (other_ref, 1 - core))):
         if i:
-            bring.wait()
+            for bring in brings:
+                bring.wait()
         for b in range(8):
             at = 8 * c + b
-            s = s_ref[at].astype(F32)
-            s = jnp.concatenate([s, s], axis=0).T
-            s = jnp.where(mine, jnp.concatenate([s, s], axis=1), 0.0).astype(BF)
+            s = mine_ref[at]
             for k in range(2):
                 named = []
                 for q in range(SLOTS):
@@ -203,13 +214,19 @@
     base_ref[...] = base
 
 
-def final_kernel(dest_ref, base_ref, back_ref, out_ref):
+def final_kernel(dest_ref, base_ref, back_ref, out_hbm, out_ref, sem):
+    sends = []
     for b in range(3):
         lo = 256 * b
         at = lax.broadcasted_iota(I32, (256, BUCKETS), 1)
         pick = (at == dest_ref[lo : lo + 256, :]).astype(F32).astype(BF)
         rows = jnp.dot(pick, back_ref[...], preferred_element_type=F32)
         out_ref[lo : lo + 256, :] = (base_ref[lo : lo + 256, :] + SCALE * rows).astype(BF)
+        part = pl.ds(lo, 256)
+        sends.append(pltpu.make_async_copy(out_ref.at[part], out_hbm.at[part], sem.at[b]))
+        sends[-1].start()
+    for send in sends:
+        send.wait()
 
 
 def exchange(x, axis):
@@ -305,12 +322,14 @@
     expanded = pl.pallas_call(
         expand_kernel,
         out_shape=jax.ShapeDtypeStruct((CHIPS, 2, PAIR, WIDTH), BF),
-        in_specs=[scalar(), scalar()] + vmem(2) + hbm(1),
+        in_specs=[scalar()] + vmem(3) + hbm(1),
         out_specs=pl.BlockSpec(memory_space=pltpu.HBM),
         scratch_shapes=[
+            pltpu.SMEM((TENSOR, 128), I32),
+            pltpu.VMEM((TENSOR, 128, 256), BF),
             pltpu.VMEM((HELD * RANK, WIDTH), BF),
             pltpu.VMEM((2, CHIPS, PAIR, WIDTH), BF),
-            pltpu.SemaphoreType.DMA((1,)),
+            pltpu.SemaphoreType.DMA((5,)),
             pltpu.SemaphoreType.DMA((8,)),
         ],
         compiler_params=params(),
@@ -331,7 +350,8 @@
         final_kernel,
         out_shape=jax.ShapeDtypeStruct((ROWS, WIDTH), BF),
         in_specs=vmem(3),
-        out_specs=pl.BlockSpec(memory_space=pltpu.VMEM),
+        out_specs=pl.BlockSpec(memory_space=pltpu.HBM),
+        scratch_shapes=[pltpu.VMEM((ROWS, WIDTH), BF), pltpu.SemaphoreType.DMA((3,))],
         compiler_params=params(),
         name="final",
     )(dest.reshape(ROWS, 1), base, back)

time: 164 us -> 163 us (level)
  no operation moved by 1% of the time
where the time goes in v9:
time: 163 us; the launch traced here: 162 us
  starting transfers between devices  61.8 us (38%)
  waiting for transfers between devices  60.7 us (37%)
  Pallas kernels  16.2 us (10%)
  blocking collectives  15.7 us (10%)
  local copies, waits for them, and re-layouts  6.58 us (4%)
    all_to_all x3, waiting for transfers between devices, exchange(): return lax.all_to_all(x, axis, split_axis=0, concat_axis=0, tiled=True)  41.7 us
    ppermute x9, starting transfers between devices, turn(): return lax.ppermute(x, axis, [(i, (i + step) % 4) for i in range(4)])  30.5 us
    all_to_all x3, starting transfers between devices, exchange(): return lax.all_to_all(x, axis, split_axis=0, concat_axis=0, tiled=True)  27.5 us
    ppermute x9, waiting for transfers between devices, turn(): return lax.ppermute(x, axis, [(i, (i + step) % 4) for i in range(4)])  19 us
    all_to_all x1, blocking collectives, exchange(): return lax.all_to_all(x, axis, split_axis=0, concat_axis=0, tiled=True)  15.7 us
    pallas_call x1, Pallas kernels, body(): pl.pallas_call(base_kernel, out_shape=tuple((jax.ShapeDtypeStruct((ROWS,...  4.49 us
    pallas_call x1, Pallas kernels, body(): pl.pallas_call(pack_kernel, out_shape=(jax.ShapeDtypeStruct((CHIPS, PAY,...  3.92 us
    ppermute x2, starting transfers between devices, sibling(): return lax.ppermute(x, 'core', [(0, 1), (1, 0)])  3.84 us
  transfers between devices with their start and end apart: 14, of which 6 were waited for; matrix products, arithmetic and copies ran while one was open for 2% of the time, Pallas kernels for 5%

profile of v9, /device:TPU:32, one launch (start us, length us, event | category | flops | bytes accessed | tf_op | source)
XLA Modules:
  0.0 162.1 jit_solution(12971033668252916798)
XLA Ops:
  0.0 0.0 copy-start.1
  0.0 0.0 copy-start
  0.0 0.9 pad_add_fusion
  0.9 3.9 %pack.1 = (bf16[16,264,128]{2,1,0:T(8,128)(2,1)}, s32[1,768]{1,0:T(1,128)S(1)}) custom-call(s32[1,1792]{1,0:T(1,128)S(1)} %reshape.21.table_ref, bf16[768,256]{1,0:T(8,128)(2,1)} %refs_0_), custom_call_target="tpu_custom_call" | custom-call | tf_op jit(solution)/shard_map/pack/pallas_call | solution.py:256
  4.8 15.2 %all-to-all-start = ((bf16[16,264,128]{2,1,0:T(8,128)(2,1)}), bf16[16,264,128]{2,1,0:T(8,128)(2,1)S(1)}, u32[]{:S(2)}, u32[]{:S(2)}) async-start(bf16[16,264,128]{2,1,0:T(8,128)(2,1)} %get-tuple-element.31), calls=%async_computation | async-start | bytes 2162688 | tf_op jit(solution)/shard_map/all_to_all | solution.py:233
  20.0 0.0 copy-done.1
  20.0 1.9 %collective-permute-start.6 = (bf16[2048,256]{1,0:T(8,128)(2,1)S(1)}, bf16[2048,256]{1,0:T(8,128)(2,1)}, u32[]{:S(2)}, u32[]{:S(2)}) collective-permute-start(bf16[2048,256]{1,0:T(8,128)(2,1)S(1)} %bitcast.10), channel_id=1, source_target_pairs={{0,16},{16,0},{1,17},{17,1},{2,18},{18,2},{3,19},{19,3},{4,20},{20... | collective-permute-start | bytes 3145736 | tf_op jit(solution)/shard_map/ppermute | solution.py:237
  22.0 4.7 %collective-permute-start = (bf16[768,256]{1,0:T(8,128)(2,1)}, bf16[768,256]{1,0:T(8,128)(2,1)}, u32[]{:S(2)}, u32[]{:S(2)}) collective-permute-start(bf16[768,256]{1,0:T(8,128)(2,1)} %refs_0_), channel_id=1, source_target_pairs={{0,3},{1,0},{2,1},{3,2},{4,7},{5,4},{6,5},{7,6},{8,11},{9,8},{10,9... | collective-permute-start | bytes 1179656 | tf_op jit(solution)/shard_map/ppermute | solution.py:249
  26.6 2.7 %collective-permute-start.1 = (bf16[768,256]{1,0:T(8,128)(2,1)}, bf16[768,256]{1,0:T(8,128)(2,1)}, u32[]{:S(2)}, u32[]{:S(2)}) collective-permute-start(bf16[768,256]{1,0:T(8,128)(2,1)} %refs_0_), channel_id=1, source_target_pairs={{0,2},{1,3},{2,0},{3,1},{4,6},{5,7},{6,4},{7,5},{8,10},{9,11},{10,... | collective-permute-start | bytes 1179656 | tf_op jit(solution)/shard_map/ppermute | solution.py:249
  29.3 0.0 copy-done
  29.4 1.9 %collective-permute-start.7 = (bf16[2048,256]{1,0:T(8,128)(2,1)S(1)}, bf16[2048,256]{1,0:T(8,128)(2,1)}, u32[]{:S(2)}, u32[]{:S(2)}) collective-permute-start(bf16[2048,256]{1,0:T(8,128)(2,1)S(1)} %bitcast.6), channel_id=1, source_target_pairs={{0,16},{16,0},{1,17},{17,1},{2,18},{18,2},{3,19},{19,3},{4,20},{20... | collective-permute-start | bytes 3145736 | tf_op jit(solution)/shard_map/ppermute | solution.py:237
  31.4 2.9 %constant_dynamic-slice_fusion = (bf16[1024,256]{1,0:T(8,128)(2,1)}, bf16[1024,256]{1,0:T(8,128)(2,1)}, bf16[1024,256]{1,0:T(8,128)(2,1)}, bf16[1024,256]{1,0:T(8,128)(2,1)}) fusion(bf16[4096,256]{1,0:T(8,128)(2,1)} %param.7, s32[]{:T(128)S(6)} %select_n.38, s32[]{:T(128)S(6)} %select_n.36, s32[]{:T(128)S(6)} %select_n.34, s32[]{:T(128)S(6)} %select_n.32), kind=kLoop, calls=%fused_computation.1 | loop fusion | bytes 4194320 | tf_op jit(solution)/shard_map/dynamic_slice | solution.py:283
  34.3 4.9 %collective-permute-start.3 = (bf16[1024,256]{1,0:T(8,128)(2,1)}, bf16[1024,256]{1,0:T(8,128)(2,1)}, u32[]{:S(2)}, u32[]{:S(2)}) collective-permute-start(bf16[1024,256]{1,0:T(8,128)(2,1)} %get-tuple-element.43), channel_id=1, source_target_pairs={{0,12},{4,0},{8,4},{12,8},{1,13},{5,1},{9,5},{13,9},{2,14},{6,2},{... | collective-permute-start | bytes 1572872 | tf_op jit(solution)/shard_map/ppermute | solution.py:249
  39.2 5.2 %collective-permute-done.refs_1_ = bf16[768,256]{1,0:T(8,128)(2,1)} collective-permute-done((bf16[768,256]{1,0:T(8,128)(2,1)}, bf16[768,256]{1,0:T(8,128)(2,1)}, u32[]{:S(2)}, u32[]{:S(2)}) %collective-permute-start) | collective-permute-done | bytes 393248 | tf_op jit(solution)/shard_map/ppermute | solution.py:249
  44.4 5.1 %collective-permute-start.4 = (bf16[1024,256]{1,0:T(8,128)(2,1)}, bf16[1024,256]{1,0:T(8,128)(2,1)}, u32[]{:S(2)}, u32[]{:S(2)}) collective-permute-start(bf16[1024,256]{1,0:T(8,128)(2,1)} %get-tuple-element.42), channel_id=1, source_target_pairs={{0,8},{4,12},{8,0},{12,4},{1,9},{5,13},{9,1},{13,5},{2,10},{6,14},... | collective-permute-start | bytes 1572872 | tf_op jit(solution)/shard_map/ppermute | solution.py:249
  49.5 0.0 collective-permute-done.1.refs_2_
  49.5 2.6 %collective-permute-start.5 = (bf16[1024,256]{1,0:T(8,128)(2,1)}, bf16[1024,256]{1,0:T(8,128)(2,1)}, u32[]{:S(2)}, u32[]{:S(2)}) collective-permute-start(bf16[1024,256]{1,0:T(8,128)(2,1)} %get-tuple-element.41), channel_id=1, source_target_pairs={{0,4},{4,8},{8,12},{12,0},{1,5},{5,9},{9,13},{13,1},{2,6},{6,10},{... | collective-permute-start | bytes 1572872 | tf_op jit(solution)/shard_map/ppermute | solution.py:249
  52.1 0.0 collective-permute-done.6.other_hbm
  52.1 1.9 %collective-permute-start.2 = (bf16[768,256]{1,0:T(8,128)(2,1)}, bf16[768,256]{1,0:T(8,128)(2,1)}, u32[]{:S(2)}, u32[]{:S(2)}) collective-permute-start(bf16[768,256]{1,0:T(8,128)(2,1)} %refs_0_), channel_id=1, source_target_pairs={{0,1},{1,2},{2,3},{3,0},{4,5},{5,6},{6,7},{7,4},{8,9},{9,10},{10,1... | collective-permute-start | bytes 1179656 | tf_op jit(solution)/shard_map/ppermute | solution.py:249
  54.1 16.7 %all-to-all-done.pay_ref = bf16[16,264,128]{2,1,0:T(8,128)(2,1)S(1)} async-done(((bf16[16,264,128]{2,1,0:T(8,128)(2,1)}), bf16[16,264,128]{2,1,0:T(8,128)(2,1)S(1)}, u32[]{:S(2)}, u32[]{:S(2)}) %all-to-all-start) | async-done | bytes 1081376 | tf_op jit(solution)/shard_map/all_to_all | solution.py:233
  70.7 2.7 %shrink.1 = (bf16[16,64,128]{2,1,0:T(8,128)(2,1)S(1)}, s32[16,128]{1,0:T(8,128)S(1)}) custom-call(s32[1]{0:T(128)} %bitcast.2.core_ref, bf16[16,264,128]{2,1,0:T(8,128)(2,1)S(1)} %all-to-all-done.pay_ref, bf16[2048,256]{1,0:T(8,128)(2,1)S(1)} %bitcast.11, bf16[2048,256]{1,0:T(8,128)(2,1)} %collective-permute-done.6.other_hbm), custom_call_target="tpu_custom_call" | custom-call | tf_op jit(solution)/shard_map/shrink/pallas_call | solution.py:301
  73.4 0.0 copy-start.2
  73.4 15.7 %all_to_all.20.p_ref = bf16[16,64,128]{2,1,0:T(8,128)(2,1)S(1)} all-to-all(bf16[16,64,128]{2,1,0:T(8,128)(2,1)S(1)} %get-tuple-element.34), channel_id=1, replica_groups=mesh['z'=16,'core'=2,'y'=4,'x'=4] {'y','x'}, dimensions={0} | all-to-all | bytes 524288 | tf_op jit(solution)/shard_map/all_to_all | solution.py:233
  89.1 0.8 total.1
  89.9 3.5 %all-to-all-start.2 = ((bf16[16,64,128]{2,1,0:T(8,128)(2,1)}), bf16[16,64,128]{2,1,0:T(8,128)(2,1)S(1)}, u32[]{:S(2)}, u32[]{:S(2)}) async-start(bf16[16,64,128]{2,1,0:T(8,128)(2,1)} %total.1), calls=%async_computation.2 | async-start | bytes 524288 | tf_op jit(solution)/shard_map/all_to_all | solution.py:233
  93.4 0.0 collective-permute-done.2.refs_3_
  93.4 0.0 collective-permute-done.3.refs_5_
  93.4 0.0 collective-permute-done.4.refs_6_
  93.4 0.0 collective-permute-done.5.refs_7_
  93.4 0.0 copy-done.2
  93.5 4.5 %base.1 = (f32[768,256]{1,0:T(8,128)S(1)}, bf16[768,256]{1,0:T(8,128)(2,1)}, bf16[768,256]{1,0:T(8,128)(2,1)}, bf16[768,256]{1,0:T(8,128)(2,1)}) custom-call(s32[1]{0:T(128)} %bitcast.1.place_ref, bf16[768,256]{1,0:T(8,128)(2,1)} %refs_0_, bf16[768,256]{1,0:T(8,128)(2,1)} %collective-permute-done.refs_1_, bf16[768,256]{1,0:T(8,128)(2,1)} %collective-permute-done.1.refs_2_, ...), custom_call_target="tpu_custom_call" | custom-call | flops 1610612736 | bytes 6291456 | tf_op jit(solution)/shard_map/base/pallas_call | solution.py:285
  98.0 0.0 collective-permute-done.7.other_hbm
  98.0 4.1 %all-to-all-done.2.s_ref = bf16[16,64,128]{2,1,0:T(8,128)(2,1)S(1)} async-done(((bf16[16,64,128]{2,1,0:T(8,128)(2,1)}), bf16[16,64,128]{2,1,0:T(8,128)(2,1)S(1)}, u32[]{:S(2)}, u32[]{:S(2)}) %all-to-all-start.2) | async-done | bytes 262176 | tf_op jit(solution)/shard_map/all_to_all | solution.py:233
  102.1 2.4 %expand.1 = bf16[16,2,64,256]{3,2,1,0:T(8,128)(2,1)} custom-call(s32[1]{0:T(128)} %bitcast.2.core_ref, s32[16,128]{1,0:T(8,128)S(1)} %get-tuple-element.33.ids_ref, bf16[16,64,128]{2,1,0:T(8,128)(2,1)S(1)} %all-to-all-done.2.s_ref, bf16[2048,256]{1,0:T(8,128)(2,1)S(1)} %bitcast.8, bf16[2048,256]{1,0:T(8,128)(2,1)} %collective-permute-done.7.other_hbm), custom_call_target="tpu_custom_call" | custom-call | tf_op jit(solution)/shard_map/expand/pallas_call | solution.py:322
  104.5 8.7 %all-to-all-start.3 = ((bf16[16,2,64,256]{3,2,1,0:T(8,128)(2,1)}), bf16[16,2,64,256]{3,2,1,0:T(8,128)(2,1)S(1)}, u32[]{:S(2)}, u32[]{:S(2)}) async-start(bf16[16,2,64,256]{3,2,1,0:T(8,128)(2,1)} %expand.1), calls=%async_computation.3 | async-start | bytes 2097152 | tf_op jit(solution)/shard_map/all_to_all | solution.py:233
  113.2 2.7 %collective-permute-start.10 = (bf16[768,256]{1,0:T(8,128)(2,1)}, bf16[768,256]{1,0:T(8,128)(2,1)S(1)}, u32[]{:S(2)}, u32[]{:S(2)}) collective-permute-start(bf16[768,256]{1,0:T(8,128)(2,1)} %get-tuple-element.39), channel_id=1, source_target_pairs={{0,12},{4,0},{8,4},{12,8},{1,13},{5,1},{9,5},{13,9},{2,14},{6,2},{... | collective-permute-start | bytes 1179656 | tf_op jit(solution)/shard_map/ppermute | solution.py:249
  116.0 3.1 %collective-permute-start.8 = (bf16[768,256]{1,0:T(8,128)(2,1)}, bf16[768,256]{1,0:T(8,128)(2,1)S(1)}, u32[]{:S(2)}, u32[]{:S(2)}) collective-permute-start(bf16[768,256]{1,0:T(8,128)(2,1)} %get-tuple-element.37), channel_id=1, source_target_pairs={{0,4},{4,8},{8,12},{12,0},{1,5},{5,9},{9,13},{13,1},{2,6},{6,10},{... | collective-permute-start | bytes 1179656 | tf_op jit(solution)/shard_map/ppermute | solution.py:249
  119.1 2.7 %collective-permute-start.9 = (bf16[768,256]{1,0:T(8,128)(2,1)}, bf16[768,256]{1,0:T(8,128)(2,1)S(1)}, u32[]{:S(2)}, u32[]{:S(2)}) collective-permute-start(bf16[768,256]{1,0:T(8,128)(2,1)} %get-tuple-element.38), channel_id=1, source_target_pairs={{0,8},{4,12},{8,0},{12,4},{1,9},{5,13},{9,1},{13,5},{2,10},{6,14},... | collective-permute-start | bytes 1179656 | tf_op jit(solution)/shard_map/ppermute | solution.py:249
  121.8 0.2 copy.7.dest_ref
  122.0 3.6 %collective-permute-done.10.p3_ref = bf16[768,256]{1,0:T(8,128)(2,1)S(1)} collective-permute-done((bf16[768,256]{1,0:T(8,128)(2,1)}, bf16[768,256]{1,0:T(8,128)(2,1)S(1)}, u32[]{:S(2)}, u32[]{:S(2)}) %collective-permute-start.10) | collective-permute-done | bytes 393248 | tf_op jit(solution)/shard_map/ppermute | solution.py:249
  125.6 10.1 %collective-permute-done.8.p1_ref = bf16[768,256]{1,0:T(8,128)(2,1)S(1)} collective-permute-done((bf16[768,256]{1,0:T(8,128)(2,1)}, bf16[768,256]{1,0:T(8,128)(2,1)S(1)}, u32[]{:S(2)}, u32[]{:S(2)}) %collective-permute-start.8) | collective-permute-done | bytes 393248 | tf_op jit(solution)/shard_map/ppermute | solution.py:249
  135.8 0.0 copy-start.3
  135.8 0.7 copy-done.3
  136.5 0.0 collective-permute-done.9.p2_ref
  136.5 0.0 copy-start.5
  136.5 0.7 copy-done.5
  137.3 0.0 copy-start.4
  137.3 1.0 copy-done.4
  138.3 0.0 copy-start.6
  138.3 1.0 copy-done.6
  139.3 0.2 ready.1.base_ref
  139.4 20.9 %all-to-all-done.3 = bf16[16,2,64,256]{3,2,1,0:T(8,128)(2,1)S(1)} async-done(((bf16[16,2,64,256]{3,2,1,0:T(8,128)(2,1)}), bf16[16,2,64,256]{3,2,1,0:T(8,128)(2,1)S(1)}, u32[]{:S(2)}, u32[]{:S(2)}) %all-to-all-start.3) | async-done | bytes 1048608 | tf_op jit(solution)/shard_map/all_to_all | solution.py:233
  160.3 1.7 %final.1 = bf16[768,256]{1,0:T(8,128)(2,1)} custom-call(s32[768,1]{1,0:T(8,128)S(1)} %copy.7.dest_ref, f32[768,256]{1,0:T(8,128)S(1)} %ready.1.base_ref, bf16[2048,256]{1,0:T(8,128)(2,1)S(1)} %bitcast.9), custom_call_target="tpu_custom_call" | custom-call | tf_op jit(solution)/shard_map/final/pallas_call | solution.py:349
  (1 shorter events, 0.0 us)
Async XLA Ops:
  0.0 20.0 %copy-start.1 = (bf16[32,64,256]{2,1,0:T(8,128)(2,1)S(1)}, bf16[32,64,256]{2,1,0:T(8,128)(2,1)}, u32[]{:S(2)}) copy-start(bf16[32,64,256]{2,1,0:T(8,128)(2,1)} %param.8) | copy-start | bytes 3145732
  0.0 29.3 %copy-start = (bf16[32,64,256]{2,1,0:T(8,128)(2,1)S(1)}, bf16[32,64,256]{2,1,0:T(8,128)(2,1)}, u32[]{:S(2)}) copy-start(bf16[32,64,256]{2,1,0:T(8,128)(2,1)} %param.9) | copy-start | bytes 3145732
  4.8 65.9 %all-to-all-start = ((bf16[16,264,128]{2,1,0:T(8,128)(2,1)}), bf16[16,264,128]{2,1,0:T(8,128)(2,1)S(1)}, u32[]{:S(2)}, u32[]{:S(2)}) async-start(bf16[16,264,128]{2,1,0:T(8,128)(2,1)} %get-tuple-element.31), calls=%async_computation | async-start | bytes 2162688 | tf_op jit(solution)/shard_map/all_to_all | solution.py:233
  20.0 32.1 %collective-permute-start.6 = (bf16[2048,256]{1,0:T(8,128)(2,1)S(1)}, bf16[2048,256]{1,0:T(8,128)(2,1)}, u32[]{:S(2)}, u32[]{:S(2)}) collective-permute-start(bf16[2048,256]{1,0:T(8,128)(2,1)S(1)} %bitcast.10), channel_id=1, source_target_pairs={{0,16},{16,0},{1,17},{17,1},{2,18},{18,2},{3,19},{19,3},{4,20},{20... | collective-permute-start | bytes 3145736 | tf_op jit(solution)/shard_map/ppermute | solution.py:237
  22.0 22.5 %collective-permute-start = (bf16[768,256]{1,0:T(8,128)(2,1)}, bf16[768,256]{1,0:T(8,128)(2,1)}, u32[]{:S(2)}, u32[]{:S(2)}) collective-permute-start(bf16[768,256]{1,0:T(8,128)(2,1)} %refs_0_), channel_id=1, source_target_pairs={{0,3},{1,0},{2,1},{3,2},{4,7},{5,4},{6,5},{7,6},{8,11},{9,8},{10,9... | collective-permute-start | bytes 1179656 | tf_op jit(solution)/shard_map/ppermute | solution.py:249
  26.6 22.9 %collective-permute-start.1 = (bf16[768,256]{1,0:T(8,128)(2,1)}, bf16[768,256]{1,0:T(8,128)(2,1)}, u32[]{:S(2)}, u32[]{:S(2)}) collective-permute-start(bf16[768,256]{1,0:T(8,128)(2,1)} %refs_0_), channel_id=1, source_target_pairs={{0,2},{1,3},{2,0},{3,1},{4,6},{5,7},{6,4},{7,5},{8,10},{9,11},{10,... | collective-permute-start | bytes 1179656 | tf_op jit(solution)/shard_map/ppermute | solution.py:249
  29.4 68.6 %collective-permute-start.7 = (bf16[2048,256]{1,0:T(8,128)(2,1)S(1)}, bf16[2048,256]{1,0:T(8,128)(2,1)}, u32[]{:S(2)}, u32[]{:S(2)}) collective-permute-start(bf16[2048,256]{1,0:T(8,128)(2,1)S(1)} %bitcast.6), channel_id=1, source_target_pairs={{0,16},{16,0},{1,17},{17,1},{2,18},{18,2},{3,19},{19,3},{4,20},{20... | collective-permute-start | bytes 3145736 | tf_op jit(solution)/shard_map/ppermute | solution.py:237
  34.3 59.2 %collective-permute-start.3 = (bf16[1024,256]{1,0:T(8,128)(2,1)}, bf16[1024,256]{1,0:T(8,128)(2,1)}, u32[]{:S(2)}, u32[]{:S(2)}) collective-permute-start(bf16[1024,256]{1,0:T(8,128)(2,1)} %get-tuple-element.43), channel_id=1, source_target_pairs={{0,12},{4,0},{8,4},{12,8},{1,13},{5,1},{9,5},{13,9},{2,14},{6,2},{... | collective-permute-start | bytes 1572872 | tf_op jit(solution)/shard_map/ppermute | solution.py:249
  44.4 49.0 %collective-permute-start.4 = (bf16[1024,256]{1,0:T(8,128)(2,1)}, bf16[1024,256]{1,0:T(8,128)(2,1)}, u32[]{:S(2)}, u32[]{:S(2)}) collective-permute-start(bf16[1024,256]{1,0:T(8,128)(2,1)} %get-tuple-element.42), channel_id=1, source_target_pairs={{0,8},{4,12},{8,0},{12,4},{1,9},{5,13},{9,1},{13,5},{2,10},{6,14},... | collective-permute-start | bytes 1572872 | tf_op jit(solution)/shard_map/ppermute | solution.py:249
  49.5 43.9 %collective-permute-start.5 = (bf16[1024,256]{1,0:T(8,128)(2,1)}, bf16[1024,256]{1,0:T(8,128)(2,1)}, u32[]{:S(2)}, u32[]{:S(2)}) collective-permute-start(bf16[1024,256]{1,0:T(8,128)(2,1)} %get-tuple-element.41), channel_id=1, source_target_pairs={{0,4},{4,8},{8,12},{12,0},{1,5},{5,9},{9,13},{13,1},{2,6},{6,10},{... | collective-permute-start | bytes 1572872 | tf_op jit(solution)/shard_map/ppermute | solution.py:249
  52.1 41.3 %collective-permute-start.2 = (bf16[768,256]{1,0:T(8,128)(2,1)}, bf16[768,256]{1,0:T(8,128)(2,1)}, u32[]{:S(2)}, u32[]{:S(2)}) collective-permute-start(bf16[768,256]{1,0:T(8,128)(2,1)} %refs_0_), channel_id=1, source_target_pairs={{0,1},{1,2},{2,3},{3,0},{4,5},{5,6},{6,7},{7,4},{8,9},{9,10},{10,1... | collective-permute-start | bytes 1179656 | tf_op jit(solution)/shard_map/ppermute | solution.py:249
  73.4 20.0 %copy-start.2 = (bf16[1024,256]{1,0:T(8,128)(2,1)S(1)}, bf16[1024,256]{1,0:T(8,128)(2,1)}, u32[]{:S(2)}) copy-start(bf16[1024,256]{1,0:T(8,128)(2,1)} %get-tuple-element.44.refs_4_) | copy-start | bytes 1572868
  89.9 12.2 %all-to-all-start.2 = ((bf16[16,64,128]{2,1,0:T(8,128)(2,1)}), bf16[16,64,128]{2,1,0:T(8,128)(2,1)S(1)}, u32[]{:S(2)}, u32[]{:S(2)}) async-start(bf16[16,64,128]{2,1,0:T(8,128)(2,1)} %total.1), calls=%async_computation.2 | async-start | bytes 524288 | tf_op jit(solution)/shard_map/all_to_all | solution.py:233
  104.5 55.8 %all-to-all-start.3 = ((bf16[16,2,64,256]{3,2,1,0:T(8,128)(2,1)}), bf16[16,2,64,256]{3,2,1,0:T(8,128)(2,1)S(1)}, u32[]{:S(2)}, u32[]{:S(2)}) async-start(bf16[16,2,64,256]{3,2,1,0:T(8,128)(2,1)} %expand.1), calls=%async_computation.3 | async-start | bytes 2097152 | tf_op jit(solution)/shard_map/all_to_all | solution.py:233
  113.2 12.4 %collective-permute-start.10 = (bf16[768,256]{1,0:T(8,128)(2,1)}, bf16[768,256]{1,0:T(8,128)(2,1)S(1)}, u32[]{:S(2)}, u32[]{:S(2)}) collective-permute-start(bf16[768,256]{1,0:T(8,128)(2,1)} %get-tuple-element.39), channel_id=1, source_target_pairs={{0,12},{4,0},{8,4},{12,8},{1,13},{5,1},{9,5},{13,9},{2,14},{6,2},{... | collective-permute-start | bytes 1179656 | tf_op jit(solution)/shard_map/ppermute | solution.py:249
  116.0 19.8 %collective-permute-start.8 = (bf16[768,256]{1,0:T(8,128)(2,1)}, bf16[768,256]{1,0:T(8,128)(2,1)S(1)}, u32[]{:S(2)}, u32[]{:S(2)}) collective-permute-start(bf16[768,256]{1,0:T(8,128)(2,1)} %get-tuple-element.37), channel_id=1, source_target_pairs={{0,4},{4,8},{8,12},{12,0},{1,5},{5,9},{9,13},{13,1},{2,6},{6,10},{... | collective-permute-start | bytes 1179656 | tf_op jit(solution)/shard_map/ppermute | solution.py:249
  119.1 17.4 %collective-permute-start.9 = (bf16[768,256]{1,0:T(8,128)(2,1)}, bf16[768,256]{1,0:T(8,128)(2,1)S(1)}, u32[]{:S(2)}, u32[]{:S(2)}) collective-permute-start(bf16[768,256]{1,0:T(8,128)(2,1)} %get-tuple-element.38), channel_id=1, source_target_pairs={{0,8},{4,12},{8,0},{12,4},{1,9},{5,13},{9,1},{13,5},{2,10},{6,14},... | collective-permute-start | bytes 1179656 | tf_op jit(solution)/shard_map/ppermute | solution.py:249
  135.8 0.7 copy-start.3
  136.5 0.7 copy-start.5
  137.3 1.0 copy-start.4
  138.3 1.0 copy-start.6

commit v10 on v9

--- a/solution.py
+++ b/solution.py
@@ -38,8 +38,13 @@
 
 
 def pack_kernel(table_ref, tokens_hbm, pay_hbm, dest_ref, tokens_ref, pay_ref, sem, out_sem):
-    bring = pltpu.make_async_copy(tokens_hbm, tokens_ref, sem.at[0])
-    bring.start()
+    thirds = [pl.ds(256 * k, 256) for k in range(3)]
+    brings = [
+        pltpu.make_async_copy(tokens_hbm.at[part], tokens_ref.at[part], sem.at[k])
+        for k, part in enumerate(thirds)
+    ]
+    for bring in brings:
+        bring.start()
     adapters = table_ref.shape[1] - ROWS
     index = table_ref[:, 0:ROWS]
     table = table_ref[:, ROWS:]
@@ -66,7 +71,8 @@
     ids = lax.dot_general(to, value, NT, preferred_element_type=F32)
     for z in range(CHIPS):
         pay_ref[z, 256:264, :] = ids[8 * z : 8 * z + 8, :].astype(BF)
-    bring.wait()
+    for bring in brings:
+        bring.wait()
     sends = []
     for b in range(8):
         at = lax.broadcasted_iota(I32, (256, ROWS), 0) + b * 256
@@ -86,15 +92,20 @@
 
 def shrink_kernel(core_ref, pay_ref, own_hbm, other_hbm, out_ref, ids_ref, pools, sem):
     core = core_ref[0]
+    quarters = [pl.ds(512 * k, 512) for k in range(4)]
     brings = [
-        pltpu.make_async_copy(pool, pools.at[i], sem.at[i])
+        [
+            pltpu.make_async_copy(pool.at[part], pools.at[i, part], sem.at[4 * i + k])
+            for k, part in enumerate(quarters)
+        ]
         for i, pool in enumerate((own_hbm, other_hbm))
     ]
-    for bring in brings:
+    for bring in brings[0] + brings[1]:
         bring.start()
     low = lax.broadcasted_iota(I32, (8, 128), 1) < PAIR
     for i, c in enumerate((core, 1 - core)):
-        brings[i].wait()
+        for bring in brings[i]:
+            bring.wait()
         at = pl.multiple_of(128 * c, 128)
         for b in range(4):
             parts = []
@@ -264,7 +275,7 @@
         scratch_shapes=[
             pltpu.VMEM((ROWS, WIDTH), BF),
             pltpu.VMEM((CHIPS, PAY, 128), BF),
-            pltpu.SemaphoreType.DMA((1,)),
+            pltpu.SemaphoreType.DMA((3,)),
             pltpu.SemaphoreType.DMA((8,)),
         ],
         compiler_params=params(),
@@ -306,7 +317,7 @@
         ),
         in_specs=[scalar()] + vmem(1) + hbm(2),
         out_specs=tuple(vmem(2)),
-        scratch_shapes=[pltpu.VMEM((2, HELD * RANK, WIDTH), BF), pltpu.SemaphoreType.DMA((2,))],
+        scratch_shapes=[pltpu.VMEM((2, HELD * RANK, WIDTH), BF), pltpu.SemaphoreType.DMA((8,))],
         compiler_params=params(),
         name="shrink",
     )(core, arrived, a_own, a_other)

time: 163 us -> 163 us (level)
  no operation moved by 1% of the time
where the time goes in v10:
time: 163 us; the launch traced here: 162 us
  starting transfers between devices  61.8 us (38%)
  waiting for transfers between devices  60.7 us (37%)
  Pallas kernels  16.3 us (10%)
  blocking collectives  15.7 us (10%)
  local copies, waits for them, and re-layouts  6.58 us (4%)
    all_to_all x3, waiting for transfers between devices, exchange(): return lax.all_to_all(x, axis, split_axis=0, concat_axis=0, tiled=True)  41.7 us
    ppermute x9, starting transfers between devices, turn(): return lax.ppermute(x, axis, [(i, (i + step) % 4) for i in range(4)])  30.5 us
    all_to_all x3, starting transfers between devices, exchange(): return lax.all_to_all(x, axis, split_axis=0, concat_axis=0, tiled=True)  27.5 us
    ppermute x9, waiting for transfers between devices, turn(): return lax.ppermute(x, axis, [(i, (i + step) % 4) for i in range(4)])  19 us
    all_to_all x1, blocking collectives, exchange(): return lax.all_to_all(x, axis, split_axis=0, concat_axis=0, tiled=True)  15.7 us
    pallas_call x1, Pallas kernels, body(): pl.pallas_call(base_kernel, out_shape=tuple((jax.ShapeDtypeStruct((ROWS,...  4.49 us
    pallas_call x1, Pallas kernels, body(): pl.pallas_call(pack_kernel, out_shape=(jax.ShapeDtypeStruct((CHIPS, PAY,...  3.97 us
    ppermute x2, starting transfers between devices, sibling(): return lax.ppermute(x, 'core', [(0, 1), (1, 0)])  3.84 us
  transfers between devices with their start and end apart: 14, of which 6 were waited for; matrix products, arithmetic and copies ran while one was open for 2% of the time, Pallas kernels for 5%

profile of v10, /device:TPU:32, one launch (start us, length us, event | category | flops | bytes accessed | tf_op | source)
XLA Modules:
  0.0 162.2 jit_solution(12072189287479756550)
XLA Ops:
  0.0 0.0 copy-start.1
  0.0 0.0 copy-start
  0.0 0.9 pad_add_fusion
  0.9 4.0 %pack.1 = (bf16[16,264,128]{2,1,0:T(8,128)(2,1)}, s32[1,768]{1,0:T(1,128)S(1)}) custom-call(s32[1,1792]{1,0:T(1,128)S(1)} %reshape.21.table_ref, bf16[768,256]{1,0:T(8,128)(2,1)} %refs_0_), custom_call_target="tpu_custom_call" | custom-call | tf_op jit(solution)/shard_map/pack/pallas_call | solution.py:267
  4.8 15.2 %all-to-all-start = ((bf16[16,264,128]{2,1,0:T(8,128)(2,1)}), bf16[16,264,128]{2,1,0:T(8,128)(2,1)S(1)}, u32[]{:S(2)}, u32[]{:S(2)}) async-start(bf16[16,264,128]{2,1,0:T(8,128)(2,1)} %get-tuple-element.31), calls=%async_computation | async-start | bytes 2162688 | tf_op jit(solution)/shard_map/all_to_all | solution.py:244
  20.1 0.0 copy-done.1
  20.1 1.9 %collective-permute-start.6 = (bf16[2048,256]{1,0:T(8,128)(2,1)S(1)}, bf16[2048,256]{1,0:T(8,128)(2,1)}, u32[]{:S(2)}, u32[]{:S(2)}) collective-permute-start(bf16[2048,256]{1,0:T(8,128)(2,1)S(1)} %bitcast.10), channel_id=1, source_target_pairs={{0,16},{16,0},{1,17},{17,1},{2,18},{18,2},{3,19},{19,3},{4,20},{20... | collective-permute-start | bytes 3145736 | tf_op jit(solution)/shard_map/ppermute | solution.py:248
  22.0 4.7 %collective-permute-start = (bf16[768,256]{1,0:T(8,128)(2,1)}, bf16[768,256]{1,0:T(8,128)(2,1)}, u32[]{:S(2)}, u32[]{:S(2)}) collective-permute-start(bf16[768,256]{1,0:T(8,128)(2,1)} %refs_0_), channel_id=1, source_target_pairs={{0,3},{1,0},{2,1},{3,2},{4,7},{5,4},{6,5},{7,6},{8,11},{9,8},{10,9... | collective-permute-start | bytes 1179656 | tf_op jit(solution)/shard_map/ppermute | solution.py:260
  26.7 2.7 %collective-permute-start.1 = (bf16[768,256]{1,0:T(8,128)(2,1)}, bf16[768,256]{1,0:T(8,128)(2,1)}, u32[]{:S(2)}, u32[]{:S(2)}) collective-permute-start(bf16[768,256]{1,0:T(8,128)(2,1)} %refs_0_), channel_id=1, source_target_pairs={{0,2},{1,3},{2,0},{3,1},{4,6},{5,7},{6,4},{7,5},{8,10},{9,11},{10,... | collective-permute-start | bytes 1179656 | tf_op jit(solution)/shard_map/ppermute | solution.py:260
  29.4 0.0 copy-done
  29.4 1.9 %collective-permute-start.7 = (bf16[2048,256]{1,0:T(8,128)(2,1)S(1)}, bf16[2048,256]{1,0:T(8,128)(2,1)}, u32[]{:S(2)}, u32[]{:S(2)}) collective-permute-start(bf16[2048,256]{1,0:T(8,128)(2,1)S(1)} %bitcast.6), channel_id=1, source_target_pairs={{0,16},{16,0},{1,17},{17,1},{2,18},{18,2},{3,19},{19,3},{4,20},{20... | collective-permute-start | bytes 3145736 | tf_op jit(solution)/shard_map/ppermute | solution.py:248
  31.4 2.9 %constant_dynamic-slice_fusion = (bf16[1024,256]{1,0:T(8,128)(2,1)}, bf16[1024,256]{1,0:T(8,128)(2,1)}, bf16[1024,256]{1,0:T(8,128)(2,1)}, bf16[1024,256]{1,0:T(8,128)(2,1)}) fusion(bf16[4096,256]{1,0:T(8,128)(2,1)} %param.7, s32[]{:T(128)S(6)} %select_n.38, s32[]{:T(128)S(6)} %select_n.36, s32[]{:T(128)S(6)} %select_n.34, s32[]{:T(128)S(6)} %select_n.32), kind=kLoop, calls=%fused_computation.1 | loop fusion | bytes 4194320 | tf_op jit(solution)/shard_map/dynamic_slice | solution.py:294
  34.3 4.9 %collective-permute-start.3 = (bf16[1024,256]{1,0:T(8,128)(2,1)}, bf16[1024,256]{1,0:T(8,128)(2,1)}, u32[]{:S(2)}, u32[]{:S(2)}) collective-permute-start(bf16[1024,256]{1,0:T(8,128)(2,1)} %get-tuple-element.43), channel_id=1, source_target_pairs={{0,12},{4,0},{8,4},{12,8},{1,13},{5,1},{9,5},{13,9},{2,14},{6,2},{... | collective-permute-start | bytes 1572872 | tf_op jit(solution)/shard_map/ppermute | solution.py:260
  39.2 5.2 %collective-permute-done.refs_1_ = bf16[768,256]{1,0:T(8,128)(2,1)} collective-permute-done((bf16[768,256]{1,0:T(8,128)(2,1)}, bf16[768,256]{1,0:T(8,128)(2,1)}, u32[]{:S(2)}, u32[]{:S(2)}) %collective-permute-start) | collective-permute-done | bytes 393248 | tf_op jit(solution)/shard_map/ppermute | solution.py:260
  44.5 5.1 %collective-permute-start.4 = (bf16[1024,256]{1,0:T(8,128)(2,1)}, bf16[1024,256]{1,0:T(8,128)(2,1)}, u32[]{:S(2)}, u32[]{:S(2)}) collective-permute-start(bf16[1024,256]{1,0:T(8,128)(2,1)} %get-tuple-element.42), channel_id=1, source_target_pairs={{0,8},{4,12},{8,0},{12,4},{1,9},{5,13},{9,1},{13,5},{2,10},{6,14},... | collective-permute-start | bytes 1572872 | tf_op jit(solution)/shard_map/ppermute | solution.py:260
  49.6 0.0 collective-permute-done.1.refs_2_
  49.6 2.6 %collective-permute-start.5 = (bf16[1024,256]{1,0:T(8,128)(2,1)}, bf16[1024,256]{1,0:T(8,128)(2,1)}, u32[]{:S(2)}, u32[]{:S(2)}) collective-permute-start(bf16[1024,256]{1,0:T(8,128)(2,1)} %get-tuple-element.41), channel_id=1, source_target_pairs={{0,4},{4,8},{8,12},{12,0},{1,5},{5,9},{9,13},{13,1},{2,6},{6,10},{... | collective-permute-start | bytes 1572872 | tf_op jit(solution)/shard_map/ppermute | solution.py:260
  52.2 0.0 collective-permute-done.6.other_hbm
  52.2 1.9 %collective-permute-start.2 = (bf16[768,256]{1,0:T(8,128)(2,1)}, bf16[768,256]{1,0:T(8,128)(2,1)}, u32[]{:S(2)}, u32[]{:S(2)}) collective-permute-start(bf16[768,256]{1,0:T(8,128)(2,1)} %refs_0_), channel_id=1, source_target_pairs={{0,1},{1,2},{2,3},{3,0},{4,5},{5,6},{6,7},{7,4},{8,9},{9,10},{10,1... | collective-permute-start | bytes 1179656 | tf_op jit(solution)/shard_map/ppermute | solution.py:260
  54.1 16.7 %all-to-all-done.pay_ref = bf16[16,264,128]{2,1,0:T(8,128)(2,1)S(1)} async-done(((bf16[16,264,128]{2,1,0:T(8,128)(2,1)}), bf16[16,264,128]{2,1,0:T(8,128)(2,1)S(1)}, u32[]{:S(2)}, u32[]{:S(2)}) %all-to-all-start) | async-done | bytes 1081376 | tf_op jit(solution)/shard_map/all_to_all | solution.py:244
  70.8 2.7 %shrink.1 = (bf16[16,64,128]{2,1,0:T(8,128)(2,1)S(1)}, s32[16,128]{1,0:T(8,128)S(1)}) custom-call(s32[1]{0:T(128)} %bitcast.2.core_ref, bf16[16,264,128]{2,1,0:T(8,128)(2,1)S(1)} %all-to-all-done.pay_ref, bf16[2048,256]{1,0:T(8,128)(2,1)S(1)} %bitcast.11, bf16[2048,256]{1,0:T(8,128)(2,1)} %collective-permute-done.6.other_hbm), custom_call_target="tpu_custom_call" | custom-call | tf_op jit(solution)/shard_map/shrink/pallas_call | solution.py:312
  73.6 0.0 copy-start.2
  73.6 15.7 %all_to_all.20.p_ref = bf16[16,64,128]{2,1,0:T(8,128)(2,1)S(1)} all-to-all(bf16[16,64,128]{2,1,0:T(8,128)(2,1)S(1)} %get-tuple-element.34), channel_id=1, replica_groups=mesh['z'=16,'core'=2,'y'=4,'x'=4] {'y','x'}, dimensions={0} | all-to-all | bytes 524288 | tf_op jit(solution)/shard_map/all_to_all | solution.py:244
  89.2 0.8 total.1
  90.0 3.5 %all-to-all-start.2 = ((bf16[16,64,128]{2,1,0:T(8,128)(2,1)}), bf16[16,64,128]{2,1,0:T(8,128)(2,1)S(1)}, u32[]{:S(2)}, u32[]{:S(2)}) async-start(bf16[16,64,128]{2,1,0:T(8,128)(2,1)} %total.1), calls=%async_computation.2 | async-start | bytes 524288 | tf_op jit(solution)/shard_map/all_to_all | solution.py:244
  93.5 0.0 collective-permute-done.2.refs_3_
  93.5 0.0 collective-permute-done.3.refs_5_
  93.5 0.0 collective-permute-done.4.refs_6_
  93.6 0.0 collective-permute-done.5.refs_7_
  93.6 0.0 copy-done.2
  93.6 4.5 %base.1 = (f32[768,256]{1,0:T(8,128)S(1)}, bf16[768,256]{1,0:T(8,128)(2,1)}, bf16[768,256]{1,0:T(8,128)(2,1)}, bf16[768,256]{1,0:T(8,128)(2,1)}) custom-call(s32[1]{0:T(128)} %bitcast.1.place_ref, bf16[768,256]{1,0:T(8,128)(2,1)} %refs_0_, bf16[768,256]{1,0:T(8,128)(2,1)} %collective-permute-done.refs_1_, bf16[768,256]{1,0:T(8,128)(2,1)} %collective-permute-done.1.refs_2_, ...), custom_call_target="tpu_custom_call" | custom-call | flops 1610612736 | bytes 6291456 | tf_op jit(solution)/shard_map/base/pallas_call | solution.py:296
  98.1 0.0 collective-permute-done.7.other_hbm
  98.1 4.1 %all-to-all-done.2.s_ref = bf16[16,64,128]{2,1,0:T(8,128)(2,1)S(1)} async-done(((bf16[16,64,128]{2,1,0:T(8,128)(2,1)}), bf16[16,64,128]{2,1,0:T(8,128)(2,1)S(1)}, u32[]{:S(2)}, u32[]{:S(2)}) %all-to-all-start.2) | async-done | bytes 262176 | tf_op jit(solution)/shard_map/all_to_all | solution.py:244
  102.2 2.4 %expand.1 = bf16[16,2,64,256]{3,2,1,0:T(8,128)(2,1)} custom-call(s32[1]{0:T(128)} %bitcast.2.core_ref, s32[16,128]{1,0:T(8,128)S(1)} %get-tuple-element.33.ids_ref, bf16[16,64,128]{2,1,0:T(8,128)(2,1)S(1)} %all-to-all-done.2.s_ref, bf16[2048,256]{1,0:T(8,128)(2,1)S(1)} %bitcast.8, bf16[2048,256]{1,0:T(8,128)(2,1)} %collective-permute-done.7.other_hbm), custom_call_target="tpu_custom_call" | custom-call | tf_op jit(solution)/shard_map/expand/pallas_call | solution.py:333
  104.6 8.7 %all-to-all-start.3 = ((bf16[16,2,64,256]{3,2,1,0:T(8,128)(2,1)}), bf16[16,2,64,256]{3,2,1,0:T(8,128)(2,1)S(1)}, u32[]{:S(2)}, u32[]{:S(2)}) async-start(bf16[16,2,64,256]{3,2,1,0:T(8,128)(2,1)} %expand.1), calls=%async_computation.3 | async-start | bytes 2097152 | tf_op jit(solution)/shard_map/all_to_all | solution.py:244
  113.3 2.7 %collective-permute-start.10 = (bf16[768,256]{1,0:T(8,128)(2,1)}, bf16[768,256]{1,0:T(8,128)(2,1)S(1)}, u32[]{:S(2)}, u32[]{:S(2)}) collective-permute-start(bf16[768,256]{1,0:T(8,128)(2,1)} %get-tuple-element.39), channel_id=1, source_target_pairs={{0,12},{4,0},{8,4},{12,8},{1,13},{5,1},{9,5},{13,9},{2,14},{6,2},{... | collective-permute-start | bytes 1179656 | tf_op jit(solution)/shard_map/ppermute | solution.py:260
  116.1 3.1 %collective-permute-start.8 = (bf16[768,256]{1,0:T(8,128)(2,1)}, bf16[768,256]{1,0:T(8,128)(2,1)S(1)}, u32[]{:S(2)}, u32[]{:S(2)}) collective-permute-start(bf16[768,256]{1,0:T(8,128)(2,1)} %get-tuple-element.37), channel_id=1, source_target_pairs={{0,4},{4,8},{8,12},{12,0},{1,5},{5,9},{9,13},{13,1},{2,6},{6,10},{... | collective-permute-start | bytes 1179656 | tf_op jit(solution)/shard_map/ppermute | solution.py:260
  119.2 2.7 %collective-permute-start.9 = (bf16[768,256]{1,0:T(8,128)(2,1)}, bf16[768,256]{1,0:T(8,128)(2,1)S(1)}, u32[]{:S(2)}, u32[]{:S(2)}) collective-permute-start(bf16[768,256]{1,0:T(8,128)(2,1)} %get-tuple-element.38), channel_id=1, source_target_pairs={{0,8},{4,12},{8,0},{12,4},{1,9},{5,13},{9,1},{13,5},{2,10},{6,14},... | collective-permute-start | bytes 1179656 | tf_op jit(solution)/shard_map/ppermute | solution.py:260
  121.9 0.2 copy.7.dest_ref
  122.1 3.6 %collective-permute-done.10.p3_ref = bf16[768,256]{1,0:T(8,128)(2,1)S(1)} collective-permute-done((bf16[768,256]{1,0:T(8,128)(2,1)}, bf16[768,256]{1,0:T(8,128)(2,1)S(1)}, u32[]{:S(2)}, u32[]{:S(2)}) %collective-permute-start.10) | collective-permute-done | bytes 393248 | tf_op jit(solution)/shard_map/ppermute | solution.py:260
  125.7 10.1 %collective-permute-done.8.p1_ref = bf16[768,256]{1,0:T(8,128)(2,1)S(1)} collective-permute-done((bf16[768,256]{1,0:T(8,128)(2,1)}, bf16[768,256]{1,0:T(8,128)(2,1)S(1)}, u32[]{:S(2)}, u32[]{:S(2)}) %collective-permute-start.8) | collective-permute-done | bytes 393248 | tf_op jit(solution)/shard_map/ppermute | solution.py:260
  135.9 0.0 copy-start.3
  135.9 0.7 copy-done.3
  136.6 0.0 collective-permute-done.9.p2_ref
  136.6 0.0 copy-start.5
  136.6 0.7 copy-done.5
  137.4 0.0 copy-start.4
  137.4 1.0 copy-done.4
  138.4 0.0 copy-start.6
  138.4 1.0 copy-done.6
  139.4 0.2 ready.1.base_ref
  139.5 20.9 %all-to-all-done.3 = bf16[16,2,64,256]{3,2,1,0:T(8,128)(2,1)S(1)} async-done(((bf16[16,2,64,256]{3,2,1,0:T(8,128)(2,1)}), bf16[16,2,64,256]{3,2,1,0:T(8,128)(2,1)S(1)}, u32[]{:S(2)}, u32[]{:S(2)}) %all-to-all-start.3) | async-done | bytes 1048608 | tf_op jit(solution)/shard_map/all_to_all | solution.py:244
  160.4 1.7 %final.1 = bf16[768,256]{1,0:T(8,128)(2,1)} custom-call(s32[768,1]{1,0:T(8,128)S(1)} %copy.7.dest_ref, f32[768,256]{1,0:T(8,128)S(1)} %ready.1.base_ref, bf16[2048,256]{1,0:T(8,128)(2,1)S(1)} %bitcast.9), custom_call_target="tpu_custom_call" | custom-call | tf_op jit(solution)/shard_map/final/pallas_call | solution.py:360
  (1 shorter events, 0.0 us)
Async XLA Ops:
  0.0 20.1 %copy-start.1 = (bf16[32,64,256]{2,1,0:T(8,128)(2,1)S(1)}, bf16[32,64,256]{2,1,0:T(8,128)(2,1)}, u32[]{:S(2)}) copy-start(bf16[32,64,256]{2,1,0:T(8,128)(2,1)} %param.8) | copy-start | bytes 3145732
  0.0 29.4 %copy-start = (bf16[32,64,256]{2,1,0:T(8,128)(2,1)S(1)}, bf16[32,64,256]{2,1,0:T(8,128)(2,1)}, u32[]{:S(2)}) copy-start(bf16[32,64,256]{2,1,0:T(8,128)(2,1)} %param.9) | copy-start | bytes 3145732
  4.8 65.9 %all-to-all-start = ((bf16[16,264,128]{2,1,0:T(8,128)(2,1)}), bf16[16,264,128]{2,1,0:T(8,128)(2,1)S(1)}, u32[]{:S(2)}, u32[]{:S(2)}) async-start(bf16[16,264,128]{2,1,0:T(8,128)(2,1)} %get-tuple-element.31), calls=%async_computation | async-start | bytes 2162688 | tf_op jit(solution)/shard_map/all_to_all | solution.py:244
  20.1 32.1 %collective-permute-start.6 = (bf16[2048,256]{1,0:T(8,128)(2,1)S(1)}, bf16[2048,256]{1,0:T(8,128)(2,1)}, u32[]{:S(2)}, u32[]{:S(2)}) collective-permute-start(bf16[2048,256]{1,0:T(8,128)(2,1)S(1)} %bitcast.10), channel_id=1, source_target_pairs={{0,16},{16,0},{1,17},{17,1},{2,18},{18,2},{3,19},{19,3},{4,20},{20... | collective-permute-start | bytes 3145736 | tf_op jit(solution)/shard_map/ppermute | solution.py:248
  22.0 22.5 %collective-permute-start = (bf16[768,256]{1,0:T(8,128)(2,1)}, bf16[768,256]{1,0:T(8,128)(2,1)}, u32[]{:S(2)}, u32[]{:S(2)}) collective-permute-start(bf16[768,256]{1,0:T(8,128)(2,1)} %refs_0_), channel_id=1, source_target_pairs={{0,3},{1,0},{2,1},{3,2},{4,7},{5,4},{6,5},{7,6},{8,11},{9,8},{10,9... | collective-permute-start | bytes 1179656 | tf_op jit(solution)/shard_map/ppermute | solution.py:260
  26.7 22.9 %collective-permute-start.1 = (bf16[768,256]{1,0:T(8,128)(2,1)}, bf16[768,256]{1,0:T(8,128)(2,1)}, u32[]{:S(2)}, u32[]{:S(2)}) collective-permute-start(bf16[768,256]{1,0:T(8,128)(2,1)} %refs_0_), channel_id=1, source_target_pairs={{0,2},{1,3},{2,0},{3,1},{4,6},{5,7},{6,4},{7,5},{8,10},{9,11},{10,... | collective-permute-start | bytes 1179656 | tf_op jit(solution)/shard_map/ppermute | solution.py:260
  29.4 68.7 %collective-permute-start.7 = (bf16[2048,256]{1,0:T(8,128)(2,1)S(1)}, bf16[2048,256]{1,0:T(8,128)(2,1)}, u32[]{:S(2)}, u32[]{:S(2)}) collective-permute-start(bf16[2048,256]{1,0:T(8,128)(2,1)S(1)} %bitcast.6), channel_id=1, source_target_pairs={{0,16},{16,0},{1,17},{17,1},{2,18},{18,2},{3,19},{19,3},{4,20},{20... | collective-permute-start | bytes 3145736 | tf_op jit(solution)/shard_map/ppermute | solution.py:248
  34.3 59.2 %collective-permute-start.3 = (bf16[1024,256]{1,0:T(8,128)(2,1)}, bf16[1024,256]{1,0:T(8,128)(2,1)}, u32[]{:S(2)}, u32[]{:S(2)}) collective-permute-start(bf16[1024,256]{1,0:T(8,128)(2,1)} %get-tuple-element.43), channel_id=1, source_target_pairs={{0,12},{4,0},{8,4},{12,8},{1,13},{5,1},{9,5},{13,9},{2,14},{6,2},{... | collective-permute-start | bytes 1572872 | tf_op jit(solution)/shard_map/ppermute | solution.py:260
  44.5 49.1 %collective-permute-start.4 = (bf16[1024,256]{1,0:T(8,128)(2,1)}, bf16[1024,256]{1,0:T(8,128)(2,1)}, u32[]{:S(2)}, u32[]{:S(2)}) collective-permute-start(bf16[1024,256]{1,0:T(8,128)(2,1)} %get-tuple-element.42), channel_id=1, source_target_pairs={{0,8},{4,12},{8,0},{12,4},{1,9},{5,13},{9,1},{13,5},{2,10},{6,14},... | collective-permute-start | bytes 1572872 | tf_op jit(solution)/shard_map/ppermute | solution.py:260
  49.6 44.0 %collective-permute-start.5 = (bf16[1024,256]{1,0:T(8,128)(2,1)}, bf16[1024,256]{1,0:T(8,128)(2,1)}, u32[]{:S(2)}, u32[]{:S(2)}) collective-permute-start(bf16[1024,256]{1,0:T(8,128)(2,1)} %get-tuple-element.41), channel_id=1, source_target_pairs={{0,4},{4,8},{8,12},{12,0},{1,5},{5,9},{9,13},{13,1},{2,6},{6,10},{... | collective-permute-start | bytes 1572872 | tf_op jit(solution)/shard_map/ppermute | solution.py:260
  52.2 41.3 %collective-permute-start.2 = (bf16[768,256]{1,0:T(8,128)(2,1)}, bf16[768,256]{1,0:T(8,128)(2,1)}, u32[]{:S(2)}, u32[]{:S(2)}) collective-permute-start(bf16[768,256]{1,0:T(8,128)(2,1)} %refs_0_), channel_id=1, source_target_pairs={{0,1},{1,2},{2,3},{3,0},{4,5},{5,6},{6,7},{7,4},{8,9},{9,10},{10,1... | collective-permute-start | bytes 1179656 | tf_op jit(solution)/shard_map/ppermute | solution.py:260
  73.6 20.0 %copy-start.2 = (bf16[1024,256]{1,0:T(8,128)(2,1)S(1)}, bf16[1024,256]{1,0:T(8,128)(2,1)}, u32[]{:S(2)}) copy-start(bf16[1024,256]{1,0:T(8,128)(2,1)} %get-tuple-element.44.refs_4_) | copy-start | bytes 1572868
  90.0 12.2 %all-to-all-start.2 = ((bf16[16,64,128]{2,1,0:T(8,128)(2,1)}), bf16[16,64,128]{2,1,0:T(8,128)(2,1)S(1)}, u32[]{:S(2)}, u32[]{:S(2)}) async-start(bf16[16,64,128]{2,1,0:T(8,128)(2,1)} %total.1), calls=%async_computation.2 | async-start | bytes 524288 | tf_op jit(solution)/shard_map/all_to_all | solution.py:244
  104.6 55.8 %all-to-all-start.3 = ((bf16[16,2,64,256]{3,2,1,0:T(8,128)(2,1)}), bf16[16,2,64,256]{3,2,1,0:T(8,128)(2,1)S(1)}, u32[]{:S(2)}, u32[]{:S(2)}) async-start(bf16[16,2,64,256]{3,2,1,0:T(8,128)(2,1)} %expand.1), calls=%async_computation.3 | async-start | bytes 2097152 | tf_op jit(solution)/shard_map/all_to_all | solution.py:244
  113.3 12.4 %collective-permute-start.10 = (bf16[768,256]{1,0:T(8,128)(2,1)}, bf16[768,256]{1,0:T(8,128)(2,1)S(1)}, u32[]{:S(2)}, u32[]{:S(2)}) collective-permute-start(bf16[768,256]{1,0:T(8,128)(2,1)} %get-tuple-element.39), channel_id=1, source_target_pairs={{0,12},{4,0},{8,4},{12,8},{1,13},{5,1},{9,5},{13,9},{2,14},{6,2},{... | collective-permute-start | bytes 1179656 | tf_op jit(solution)/shard_map/ppermute | solution.py:260
  116.1 19.8 %collective-permute-start.8 = (bf16[768,256]{1,0:T(8,128)(2,1)}, bf16[768,256]{1,0:T(8,128)(2,1)S(1)}, u32[]{:S(2)}, u32[]{:S(2)}) collective-permute-start(bf16[768,256]{1,0:T(8,128)(2,1)} %get-tuple-element.37), channel_id=1, source_target_pairs={{0,4},{4,8},{8,12},{12,0},{1,5},{5,9},{9,13},{13,1},{2,6},{6,10},{... | collective-permute-start | bytes 1179656 | tf_op jit(solution)/shard_map/ppermute | solution.py:260
  119.2 17.4 %collective-permute-start.9 = (bf16[768,256]{1,0:T(8,128)(2,1)}, bf16[768,256]{1,0:T(8,128)(2,1)S(1)}, u32[]{:S(2)}, u32[]{:S(2)}) collective-permute-start(bf16[768,256]{1,0:T(8,128)(2,1)} %get-tuple-element.38), channel_id=1, source_target_pairs={{0,8},{4,12},{8,0},{12,4},{1,9},{5,13},{9,1},{13,5},{2,10},{6,14},... | collective-permute-start | bytes 1179656 | tf_op jit(solution)/shard_map/ppermute | solution.py:260
  135.9 0.7 copy-start.3
  136.6 0.7 copy-start.5
  137.4 1.0 copy-start.4
  138.4 1.0 copy-start.6
